TPU v7x, 512 devices: a whole 4x8x8 slice. The times are simulated.
512 devices in a mesh: own: 16 (over z, x_lo), fine: 32 (over y, x_hi, core).
Axes of the slice: x: 4 (x_hi: 2, x_lo: 2; x = x_hi * 2 + x_lo), y: 8, z: 8, core: 2. Of those that a mesh axis runs over, the one named last changes fastest.
Arguments:
- coarse_cells: bfloat16 [5, 256, 512, 128], P(None, 'own', 'fine'), may hold values from -6 to 6
- fine_cells: bfloat16 [2048, 5, 32, 1024], P(('own', 'fine')), may hold values from -6 to 6
- diffusivity: float32 [5], replicated, may hold values from 0.03 to 0.08
- patch_column: int32 [2048], P(('own', 'fine')), may hold values from 0 to 7, as said below
- patch_count: int32 [512], P(('own', 'fine')), may hold values from 0 to 4, as said below
- neighbor_slot: int32 [2048, 4], P(('own', 'fine')), may hold values from -1 to 3, as said below
Outputs:
- coarse_new: bfloat16 [5, 256, 512, 128], P(None, 'own', 'fine')
- fine_new: bfloat16 [2048, 5, 32, 1024], P(('own', 'fine'))
Inputs may be any that keep to these rules, and one draw needn't show every extreme that they name: `patch_column`: on the devices of own index i, the 4 slots of a device hold, in some order, the 4 columns c of 0 to 7 whose pair c // 2 has the parity of i; only the first patch_count slots hold patches, so a footprint is never covered in two neighbouring slabs. `patch_count`: the counts of the devices of one own index sum to 4 * 32 // 2, and in every own index some device holds 4 patches. `neighbor_slot`: for the patch in slot s with column c on the device of fine index j: the slot of the patch at column c - 1 and c + 1 (modulo 8) on the same device, and of the patch at column c on fine index j - 1 and j + 1 (modulo the axis), or -1 where that footprint holds no patch; all four are -1 for slots that hold no patch.
All inputs are finite; a program needn't handle non-finite values.
Results may differ from a plain program's by a relative error of at most 0.0043.
Values may be sent and summed in bfloat16 or wider, within the bound.
No kernel may reach another device: no remote copies, remote signals or barrier semaphores. Data moves between devices by JAX's collectives and lax.ppermute only.
A program may use at most 128 MiB of HBM per device.

v0:
```python
import jax
import jax.numpy as jnp
from jax import lax
from jax.sharding import PartitionSpec as P


def extended(cells, sides, width):
    for axis, dim in sides:
        count = lax.axis_size(axis)
        head = lax.slice_in_dim(cells, 0, width, axis=dim)
        tail = lax.slice_in_dim(cells, cells.shape[dim] - width, cells.shape[dim], axis=dim)
        cells = jnp.concatenate(
            [
                lax.ppermute(tail, axis, [(i, (i + 1) % count) for i in range(count)]),
                cells,
                lax.ppermute(head, axis, [((i + 1) % count, i) for i in range(count)]),
            ],
            axis=dim,
        )
    return cells


def spread(layer_in):
    return jnp.repeat(jnp.repeat(layer_in, 2, axis=-1), 2, axis=-2)


def pooled(layer_in):
    shape_in = layer_in.shape
    return layer_in.reshape(shape_in[:-2] + (shape_in[-2] // 2, 2, shape_in[-1] // 2, 2)).sum(
        axis=(-1, -3)
    )


def flat_faces(field_now):
    edge_len = field_now.shape[2]
    plane_len = field_now.shape[3]
    low_z = field_now[:, :, 0].reshape(field_now.shape[:2] + (edge_len, edge_len))
    high_z = field_now[:, :, -1].reshape(field_now.shape[:2] + (edge_len, edge_len))
    return (
        field_now[..., 0::edge_len],
        field_now[..., edge_len - 1 :: edge_len],
        field_now[..., :edge_len],
        field_now[..., plane_len - edge_len :],
        low_z,
        high_z,
    )


def box_faces(box_set, offset):
    high_at = box_set.shape[-1] - 1 - offset
    middle = slice(1, -1)
    return (
        box_set[:, :, middle, middle, offset],
        box_set[:, :, middle, middle, high_at],
        box_set[:, :, middle, offset, middle],
        box_set[:, :, middle, high_at, middle],
        box_set[:, :, offset, middle, middle],
        box_set[:, :, high_at, middle, middle],
    )


def neighbour_total(padded, coarse_rate):
    centre = padded[:, 1:-1, 1:-1]
    summed = padded[:, 2:, 1:-1] + padded[:, :-2, 1:-1] + padded[:, 1:-1, 2:] + padded[:, 1:-1, :-2]
    summed = summed + jnp.roll(centre, 1, axis=3) + jnp.roll(centre, -1, axis=3)
    return centre + coarse_rate * (summed - 6.0 * centre)


def side_table(edge_len):
    plane_len = edge_len * edge_len
    entry = jnp.arange(4 * edge_len, dtype=jnp.int32)
    part_id = entry // edge_len
    inner = entry % edge_len
    target = jnp.where(
        part_id == 0,
        inner * edge_len,
        jnp.where(
            part_id == 1,
            inner * edge_len + edge_len - 1,
            jnp.where(part_id == 2, inner, (edge_len - 1) * edge_len + inner),
        ),
    )
    position = jnp.arange(plane_len, dtype=jnp.int32)
    return (target[:, None] == position[None, :]).astype(jnp.float32)


def diffuse_flat(field_now, ghost_set, placing):
    slot_count, comp_count, edge_len, plane_len = field_now.shape
    position = jnp.arange(plane_len)
    column_pos = position % edge_len
    pad_column = jnp.zeros(field_now.shape[:-1] + (1,), jnp.float32)
    pad_row = jnp.zeros(field_now.shape[:-1] + (edge_len,), jnp.float32)
    plus_x = jnp.where(
        column_pos == edge_len - 1, 0.0, jnp.concatenate([field_now[..., 1:], pad_column], axis=-1)
    )
    minus_x = jnp.where(
        column_pos == 0, 0.0, jnp.concatenate([pad_column, field_now[..., :-1]], axis=-1)
    )
    plus_y = jnp.concatenate([field_now[..., edge_len:], pad_row], axis=-1)
    minus_y = jnp.concatenate([pad_row, field_now[..., :-edge_len]], axis=-1)
    plus_z = jnp.concatenate([field_now[:, :, 1:], ghost_set[5][:, :, None]], axis=2)
    minus_z = jnp.concatenate([ghost_set[4][:, :, None], field_now[:, :, :-1]], axis=2)
    sides = jnp.concatenate([ghost_set[0], ghost_set[1], ghost_set[2], ghost_set[3]], axis=-1)
    side_terms = jnp.dot(
        sides.reshape(-1, 4 * edge_len),
        placing,
        precision=lax.Precision.HIGHEST,
        preferred_element_type=jnp.float32,
    ).reshape(field_now.shape)
    return plus_x + minus_x + plus_y + minus_y + plus_z + minus_z + side_terms - 6.0 * field_now


def local(coarse_cells, fine_cells, diffusivity, patch_column, patch_count, neighbor_slot):
    slot_count = fine_cells.shape[0]
    comp_count = fine_cells.shape[1]
    edge_len = fine_cells.shape[2]
    plane_len = fine_cells.shape[3]
    half_len = edge_len // 2
    cells_x = coarse_cells.shape[3]
    coarse_rate = diffusivity[:, None, None, None]
    face_rate = diffusivity[:, None, None]
    in_use = jnp.arange(slot_count) < patch_count[0]
    linked = neighbor_slot >= 0
    partner_slot = jnp.maximum(neighbor_slot, 0)
    placing = side_table(edge_len)
    old_padded = extended(coarse_cells, (("own", 1), ("fine", 2)), 1).astype(jnp.float32)
    coarse_mid = neighbour_total(old_padded, coarse_rate)
    mid_padded = extended(coarse_mid.astype(jnp.bfloat16), (("own", 1), ("fine", 2)), 1).astype(
        coarse_mid.dtype
    )
    anchor = jnp.zeros((), jnp.int32)
    x_start = patch_column * half_len

    def cut_boxes(padded):
        wrapped = jnp.concatenate([padded[..., -1:], padded, padded[..., :1]], axis=-1)
        return jax.vmap(
            lambda col_at: lax.dynamic_slice(
                wrapped,
                (anchor, anchor, anchor, col_at),
                (comp_count, half_len + 2, half_len + 2, half_len + 2),
            )
        )(x_start)

    old_boxes = cut_boxes(old_padded)
    mid_boxes = cut_boxes(mid_padded)
    old_ghost = box_faces(old_boxes, 0)
    old_inner = box_faces(old_boxes, 1)
    mid_ghost = box_faces(mid_boxes, 0)
    half_ghost = tuple((0.5 * (first + second) for first, second in zip(old_ghost, mid_ghost)))

    def advance(field_now, level_faces):
        boundary = flat_faces(field_now)
        outgoing = (
            jnp.stack([boundary[2], boundary[3]])
            .astype(jnp.bfloat16)
            .reshape(2, slot_count, comp_count, edge_len * edge_len)
        )
        received = extended(outgoing, (("fine", 0),), 1)
        received = received.astype(jnp.float32).reshape(
            4, slot_count, comp_count, edge_len, edge_len
        )
        partner = (boundary[1], boundary[0], received[0], received[3])
        ghost_set = []
        for facet_idx in range(4):
            picked = jnp.take(partner[facet_idx], partner_slot[:, facet_idx], axis=0)
            ghost_set.append(
                jnp.where(
                    linked[:, facet_idx][:, None, None, None],
                    picked,
                    spread(level_faces[facet_idx]),
                )
            )
        for facet_idx in (4, 5):
            ghost_set.append(
                spread(level_faces[facet_idx]).reshape(slot_count, comp_count, plane_len)
            )
        return (field_now + 2.0 * face_rate * diffuse_flat(field_now, ghost_set, placing), boundary)

    start = fine_cells.astype(jnp.float32)
    halfway_raw, first_bound = advance(start, old_ghost)
    halfway = lax.optimization_barrier(halfway_raw.astype(jnp.bfloat16)).astype(jnp.float32)
    final_raw, second_bound = advance(halfway, half_ghost)
    fine_out = jnp.where(in_use[:, None, None, None], final_raw, 0.0).astype(jnp.bfloat16)
    corrections = []
    for facet_idx in range(6):
        flux_sum = (
            2.0
            * face_rate
            * (
                pooled(first_bound[facet_idx])
                - 4.0 * old_ghost[facet_idx]
                + pooled(second_bound[facet_idx])
                - 4.0 * half_ghost[facet_idx]
            )
            / 8.0
        )
        correction = flux_sum - face_rate * (old_inner[facet_idx] - old_ghost[facet_idx])
        keep_mask = in_use & ~linked[:, facet_idx] if facet_idx < 4 else in_use
        corrections.append(jnp.where(keep_mask[:, None, None, None], correction, 0.0))
    x_index = jnp.arange(cells_x)
    in_block = (x_index // half_len)[None, :] == patch_column[:, None]

    def onto_column(correction, target):
        on_column = x_index[None, :] == target[:, None]
        return jnp.sum(
            jnp.where(on_column[:, None, None, None, :], correction[..., None], 0.0), axis=0
        )

    def onto_blocks(correction):
        tiled = jnp.tile(correction, (1, 1, 1, cells_x // half_len))
        return jnp.sum(jnp.where(in_block[:, None, None, :], tiled, 0.0), axis=0)

    local_fix = onto_column(corrections[0], (x_start - 1) % cells_x)
    local_fix = local_fix + onto_column(corrections[1], (x_start + half_len) % cells_x)
    outgoing_rows = jnp.stack([onto_blocks(corrections[2]), onto_blocks(corrections[3])])
    arrived_rows = extended(outgoing_rows.astype(jnp.bfloat16), (("fine", 0),), 1).astype(
        outgoing_rows.dtype
    )
    local_fix = local_fix.at[:, :, 0].add(arrived_rows[0]).at[:, :, -1].add(arrived_rows[3])
    outgoing_planes = jnp.stack([onto_blocks(corrections[4]), onto_blocks(corrections[5])])
    arrived_planes = extended(outgoing_planes.astype(jnp.bfloat16), (("own", 0),), 1).astype(
        outgoing_planes.dtype
    )
    local_fix = local_fix.at[:, 0].add(arrived_planes[0]).at[:, -1].add(arrived_planes[3])
    position = jnp.arange(plane_len, dtype=jnp.int32)
    pool_index = position // edge_len // 2 * half_len + position % edge_len // 2
    pool_table = (
        pool_index[:, None] == jnp.arange(half_len * half_len, dtype=jnp.int32)[None, :]
    ).astype(jnp.bfloat16)
    pooled_plane = jnp.dot(
        fine_out.reshape(-1, plane_len), pool_table, preferred_element_type=jnp.float32
    ).reshape(slot_count, comp_count, edge_len, half_len * half_len)
    averaged = (pooled_plane[:, :, 0::2] + pooled_plane[:, :, 1::2]) / 8.0
    averaged = averaged.reshape(slot_count, comp_count, half_len, half_len, half_len)
    tiled_avg = jnp.tile(averaged, (1, 1, 1, 1, cells_x // half_len))
    owned = in_block & in_use[:, None]
    level_avg = jnp.sum(jnp.where(owned[:, None, None, None, :], tiled_avg, 0.0), axis=0)
    covered = jnp.any(owned, axis=0)
    coarse_new = jnp.where(
        covered[None, None, None, :],
        level_avg.astype(jnp.bfloat16),
        (coarse_mid + local_fix).astype(jnp.bfloat16),
    )
    return (coarse_new, fine_out)


def solution(mesh):
    return jax.shard_map(
        local,
        mesh=mesh,
        in_specs=(
            P(None, "own", "fine", None),
            P(("own", "fine"), None, None, None),
            P(),
            P(("own", "fine")),
            P(("own", "fine")),
            P(("own", "fine"), None),
        ),
        out_specs=(P(None, "own", "fine", None), P(("own", "fine"), None, None, None)),
        check_vma=False,
    )
```

profile of v0, /device:TPU:1, one launch (start us, length us, event | category | flops | bytes accessed | tf_op | source)
XLA Modules:
  0.0 408.1 jit_solution(12810592917866603949)
XLA Ops:
  6.0 10.4 %collective-permute-start.1 = (bf16[5,1,16,128]{3,2,1,0:T(8,128)(2,1)S(1)}, bf16[5,1,16,128]{3,2,1,0:T(8,128)(2,1)}, u32[]{:S(2)}, u32[]{:S(2)}) collective-permute-start(bf16[5,1,16,128]{3,2,1,0:T(8,128)(2,1)S(1)} %get-tuple-element.143), channel_id=1, source_target_pairs={{32,0},{64,32},{96,64},{128,96},{160,128},{192,160},{224,192},{256... | collective-permute-start | bytes 61448 | tf_op jit(solution)/shard_map/ppermute | solution.py:16
  21.6 4.2 %collective-permute-start.4 = (bf16[1,4,5,1024]{3,1,2,0:T(4,128)(2,1)}, bf16[1,4,5,1024]{3,1,2,0:T(4,128)(2,1)}, u32[]{:S(2)}, u32[]{:S(2)}) collective-permute-start(bf16[1,4,5,1024]{3,1,2,0:T(4,128)(2,1)} %copy.541), channel_id=1, source_target_pairs={{0,1},{1,2},{2,3},{3,4},{4,5},{5,6},{6,7},{7,8},{8,9},{9,10},{10,1... | collective-permute-start | bytes 122888 | tf_op jit(solution)/shard_map/ppermute | solution.py:14
  64.8 4.1 %reduce_sum.199 = f32[4,5,16,16]{1,3,2,0:T(8,128)} reduce(f32[4,5,16,2,16,2]{1,5,4,3,2,0:T(2,128)} %bitcast.318, f32[]{:T(128)} %constant.267.clone.1), dimensions={5,3}, to_apply=%region_17.19 | reduce | flops 15360 | bytes 102404 | tf_op jit(solution)/shard_map/reduce_sum | solution.py:29
  98.5 4.5 %reduce_sum.185 = f32[4,5,16,16]{1,3,2,0:T(8,128)} reduce(f32[4,5,16,2,16,2]{1,5,4,3,2,0:T(2,128)} %bitcast.317, f32[]{:T(128)} %constant.267.clone.1), dimensions={5,3}, to_apply=%region_5.7 | reduce | flops 15360 | bytes 102404 | tf_op jit(solution)/shard_map/reduce_sum | solution.py:29
  112.9 4.4 %collective-permute-start.3 = (bf16[5,18,1,128]{3,1,2,0:T(8,128)(2,1)S(1)}, bf16[5,18,1,128]{3,1,2,0:T(8,128)(2,1)S(1)}, u32[]{:S(2)}, u32[]{:S(2)}) collective-permute-start(bf16[5,18,1,128]{3,1,2,0:T(8,128)(2,1)S(1)} %copy.546), channel_id=1, source_target_pairs={{1,0},{2,1},{3,2},{4,3},{5,4},{6,5},{7,6},{8,7},{9,8},{10,9},{11,1... | collective-permute-start | bytes 69128 | tf_op jit(solution)/shard_map/ppermute | solution.py:16
  128.3 7.9 %copy.457 = f32[5,18,18,130]{2,1,0,3:T(8,128)} copy(f32[5,18,18,130]{3,2,1,0:T(8,128)} %pad_maximum_fusion) | data formatting | bytes 1684800 | tf_op jit(solution)/shard_map/concatenate | solution.py:135
  136.2 6.2 %gather_fusion = f32[4,5,18,18,18]{3,2,1,4,0:T(8,128)} fusion(f32[5,18,18,130]{2,1,0,3:T(8,128)} %copy.457, s32[4]{0:T(128)S(1)} %get-tuple-element.157), kind=kCustom, calls=%fused_computation.8 | custom fusion | bytes 933184 | tf_op jit(solution)/shard_map/vmap()/gather | solution.py:137
  142.4 4.7 %fusion.126 = (f32[4,5,1,16,16]{3,2,1,4,0:T(1,128)}, f32[4,5,1,16,16]{3,2,1,4,0:T(1,128)S(1)}, f32[4,5,1,16,16]{3,2,1,4,0:T(1,128)S(1)}, f32[4,5,1,16,16]{3,2,1,4,0:T(1,128)}) fusion(f32[4,5,18,18,18]{3,2,1,4,0:T(8,128)} %gather_fusion), kind=kLoop, calls=%fused_computation.287 | loop fusion | bytes 163840 | tf_op jit(solution)/shard_map/slice | solution.py:57
  147.1 11.9 %fusion.125 = (f32[4,5,16,1,16]{3,2,1,4,0:T(8,128)}, f32[4,5,16,1,16]{3,2,1,4,0:T(8,128)}, f32[4,5,16,1,16]{3,2,1,4,0:T(8,128)}, f32[4,5,16,1,16]{3,2,1,4,0:T(8,128)}) fusion(f32[4,5,18,18,18]{3,2,1,4,0:T(8,128)} %gather_fusion), kind=kLoop, calls=%fused_computation.286 | loop fusion | bytes 163840 | tf_op jit(solution)/shard_map/slice | solution.py:56
  185.9 6.2 %fusion.5 = bf16[4,5,32,1024]{3,2,1,0:T(8,128)(2,1)S(1)} fusion(f32[4,5,1,1024]{3,2,1,0:T(1,128)S(1)} %broadcast_in_dim_reshape_reshape.12, f32[4,5,31,1024]{3,2,1,0:T(8,128)S(1)} %copy-done.6, f32[4,5,31,1024]{3,2,1,0:T(8,128)S(1)} %copy-done.5, f32[4,5,1,1024]{3,2,1,0:T(1,128)S(1)} %copy-done.44, f32[4,5,32,992]{3,2,1,0:T(8,128)} %get-tuple-element.118, ...), kind=kOutput, calls=%fused_computation.17 | convolution fusion | flops 1017495552 | bytes 18511380 | tf_op jit(solution)/shard_map/dot_general | solution.py:104
  212.8 4.3 %copy.551 = f32[4,5,16,1,16]{4,2,1,0,3:T(8,128)} copy(f32[4,5,16,1,16]{3,2,1,4,0:T(8,128)} %get-tuple-element.85) | data formatting | bytes 40960
  217.1 4.3 %copy.550 = f32[4,5,16,1,16]{4,2,1,0,3:T(8,128)} copy(f32[4,5,16,1,16]{3,2,1,4,0:T(8,128)} %get-tuple-element.86) | data formatting | bytes 40960
  245.2 4.3 %copy.519 = f32[4,5,16,1,16]{4,2,1,0,3:T(8,128)} copy(f32[4,5,16,1,16]{3,2,1,4,0:T(8,128)} %get-tuple-element.83) | data formatting | bytes 40960 | tf_op jit(solution)/shard_map/slice | solution.py:56
  256.2 4.3 %copy.524 = f32[4,5,16,1,16]{4,2,1,0,3:T(8,128)} copy(f32[4,5,16,1,16]{3,2,1,4,0:T(8,128)} %get-tuple-element.84) | data formatting | bytes 40960 | tf_op jit(solution)/shard_map/slice | solution.py:55
  267.9 8.7 %collective-permute-start.11 = (bf16[1,4,5,1024]{3,1,2,0:T(4,128)(2,1)S(1)}, bf16[1,4,5,1024]{3,1,2,0:T(4,128)(2,1)S(1)}, u32[]{:S(2)}, u32[]{:S(2)}) collective-permute-start(bf16[1,4,5,1024]{3,1,2,0:T(4,128)(2,1)S(1)} %copy.544), channel_id=1, source_target_pairs={{1,0},{2,1},{3,2},{4,3},{5,4},{6,5},{7,6},{8,7},{9,8},{10,9},{11,1... | collective-permute-start | bytes 122888 | tf_op jit(solution)/shard_map/ppermute | solution.py:16
  304.4 8.0 %copy.481 = f32[5,18,18,130]{2,1,0,3:T(8,128)} copy(f32[5,18,18,130]{3,2,1,0:T(8,128)} %pad_maximum_fusion.1) | data formatting | bytes 1684800 | tf_op jit(solution)/shard_map/concatenate | solution.py:135
  312.4 6.1 %gather_fusion.1 = f32[4,5,18,18,18]{3,2,1,4,0:T(8,128)} fusion(f32[5,18,18,130]{2,1,0,3:T(8,128)} %copy.481, s32[4]{0:T(128)S(1)} %get-tuple-element.157), kind=kCustom, calls=%fused_computation.9 | custom fusion | bytes 933184 | tf_op jit(solution)/shard_map/vmap()/gather | solution.py:137
  321.7 6.4 %fusion.127 = (f32[4,5,16,1,16]{3,2,1,4,0:T(8,128)}, f32[4,5,16,1,16]{3,2,1,4,0:T(8,128)}) fusion(f32[4,5,18,18,18]{3,2,1,4,0:T(8,128)} %gather_fusion.1), kind=kLoop, calls=%fused_computation.288 | loop fusion | bytes 81920 | tf_op jit(solution)/shard_map/slice | solution.py:55
  339.5 4.4 %copy.556 = f32[4,5,16,1,16]{4,2,1,0,3:T(8,128)} copy(f32[4,5,16,1,16]{3,2,1,4,0:T(8,128)} %get-tuple-element.92) | data formatting | bytes 40960
  343.8 4.3 %copy.555 = f32[4,5,16,1,16]{4,2,1,0,3:T(8,128)} copy(f32[4,5,16,1,16]{3,2,1,4,0:T(8,128)} %get-tuple-element.91) | data formatting | bytes 40960
  362.6 6.1 %fusion.12 = bf16[4,5,32,1024]{3,2,1,0:T(8,128)(2,1)S(1)} fusion(f32[4,5,1,1024]{3,2,1,0:T(1,128)S(1)} %broadcast_in_dim_reshape_reshape.14, f32[4,5,31,1024]{3,2,1,0:T(8,128)S(1)} %copy-done.4, f32[4,5,31,1024]{3,2,1,0:T(8,128)S(1)} %copy-done.3, f32[4,5,1,1024]{3,2,1,0:T(1,128)S(1)} %copy-done.43, f32[4,5,32,992]{3,2,1,0:T(8,128)} %get-tuple-element.110, ...), kind=kOutput, calls=%fused_computation.25 | convolution fusion | flops 1018150912 | bytes 18511384 | tf_op jit(solution)/shard_map/dot_general | solution.py:104
  372.0 4.8 %select_reduce_fusion = bf16[5,16,16,8,16]{4,3,2,1,0:T(8,128)(2,1)} fusion(f32[4,5,16,16,16]{4,3,2,1,0:T(8,128)S(1)} %tile.12, pred[4,8,16]{2,1,0:T(8,128)(4,1)S(1)} %copy-done.46), kind=kLoop, calls=%fused_computation.10 | loop fusion | flops 1146880 | bytes 655872 | tf_op jit(solution)/shard_map/reduce_sum | solution.py:237
  381.2 8.1 %collective-permute-start.13 = (bf16[1,5,16,128]{3,2,1,0:T(8,128)(2,1)S(1)}, bf16[1,5,16,128]{3,2,1,0:T(8,128)(2,1)S(1)}, u32[]{:S(2)}, u32[]{:S(2)}) collective-permute-start(bf16[1,5,16,128]{3,2,1,0:T(8,128)(2,1)S(1)} %stack.39), channel_id=1, source_target_pairs={{1,0},{2,1},{3,2},{4,3},{5,4},{6,5},{7,6},{8,7},{9,8},{10,9},{11,1... | collective-permute-start | bytes 61448 | tf_op jit(solution)/shard_map/ppermute | solution.py:16
  391.6 4.9 %collective-permute-start.15 = (bf16[1,5,16,128]{3,2,1,0:T(8,128)(2,1)S(1)}, bf16[1,5,16,128]{3,2,1,0:T(8,128)(2,1)S(1)}, u32[]{:S(2)}, u32[]{:S(2)}) collective-permute-start(bf16[1,5,16,128]{3,2,1,0:T(8,128)(2,1)S(1)} %stack.41), channel_id=1, source_target_pairs={{32,0},{64,32},{96,64},{128,96},{160,128},{192,160},{224,192},{256... | collective-permute-start | bytes 61448 | tf_op jit(solution)/shard_map/ppermute | solution.py:16
  (404 shorter events, 260.9 us)
Async XLA Ops:
  0.6 25.2 %copy-start = (bf16[4,5,32,1024]{3,2,1,0:T(8,128)(2,1)S(1)}, bf16[4,5,32,1024]{3,2,1,0:T(8,128)(2,1)}, u32[]{:S(2)}) copy-start(bf16[4,5,32,1024]{3,2,1,0:T(8,128)(2,1)} %param.17) | copy-start | bytes 3932164
  2.1 108.2 %collective-permute-start = (bf16[5,1,16,128]{3,2,1,0:T(8,128)(2,1)}, bf16[5,1,16,128]{3,2,1,0:T(8,128)(2,1)}, u32[]{:S(2)}, u32[]{:S(2)}) collective-permute-start(bf16[5,1,16,128]{3,2,1,0:T(8,128)(2,1)} %get-tuple-element.144), channel_id=1, source_target_pairs={{0,32},{32,64},{64,96},{96,128},{128,160},{160,192},{192,224},{224... | collective-permute-start | bytes 61448 | tf_op jit(solution)/shard_map/ppermute | solution.py:14
  6.0 106.0 %collective-permute-start.1 = (bf16[5,1,16,128]{3,2,1,0:T(8,128)(2,1)S(1)}, bf16[5,1,16,128]{3,2,1,0:T(8,128)(2,1)}, u32[]{:S(2)}, u32[]{:S(2)}) collective-permute-start(bf16[5,1,16,128]{3,2,1,0:T(8,128)(2,1)S(1)} %get-tuple-element.143), channel_id=1, source_target_pairs={{32,0},{64,32},{96,64},{128,96},{160,128},{192,160},{224,192},{256... | collective-permute-start | bytes 61448 | tf_op jit(solution)/shard_map/ppermute | solution.py:16
  17.8 102.2 %collective-permute-start.5 = (bf16[1,4,5,1024]{3,1,2,0:T(4,128)(2,1)S(1)}, bf16[1,4,5,1024]{3,1,2,0:T(4,128)(2,1)}, u32[]{:S(2)}, u32[]{:S(2)}) collective-permute-start(bf16[1,4,5,1024]{3,1,2,0:T(4,128)(2,1)S(1)} %copy.542), channel_id=1, source_target_pairs={{1,0},{2,1},{3,2},{4,3},{5,4},{6,5},{7,6},{8,7},{9,8},{10,9},{11,1... | collective-permute-start | bytes 122888 | tf_op jit(solution)/shard_map/ppermute | solution.py:16
  21.6 98.5 %collective-permute-start.4 = (bf16[1,4,5,1024]{3,1,2,0:T(4,128)(2,1)}, bf16[1,4,5,1024]{3,1,2,0:T(4,128)(2,1)}, u32[]{:S(2)}, u32[]{:S(2)}) collective-permute-start(bf16[1,4,5,1024]{3,1,2,0:T(4,128)(2,1)} %copy.541), channel_id=1, source_target_pairs={{0,1},{1,2},{2,3},{3,4},{4,5},{5,6},{6,7},{7,8},{8,9},{9,10},{10,1... | collective-permute-start | bytes 122888 | tf_op jit(solution)/shard_map/ppermute | solution.py:14
  112.9 11.1 %collective-permute-start.3 = (bf16[5,18,1,128]{3,1,2,0:T(8,128)(2,1)S(1)}, bf16[5,18,1,128]{3,1,2,0:T(8,128)(2,1)S(1)}, u32[]{:S(2)}, u32[]{:S(2)}) collective-permute-start(bf16[5,18,1,128]{3,1,2,0:T(8,128)(2,1)S(1)} %copy.546), channel_id=1, source_target_pairs={{1,0},{2,1},{3,2},{4,3},{5,4},{6,5},{7,6},{8,7},{9,8},{10,9},{11,1... | collective-permute-start | bytes 69128 | tf_op jit(solution)/shard_map/ppermute | solution.py:16
  117.3 7.9 %collective-permute-start.2 = (bf16[5,18,1,128]{3,1,2,0:T(8,128)(2,1)S(1)}, bf16[5,18,1,128]{3,1,2,0:T(8,128)(2,1)S(1)}, u32[]{:S(2)}, u32[]{:S(2)}) collective-permute-start(bf16[5,18,1,128]{3,1,2,0:T(8,128)(2,1)S(1)} %copy.545), channel_id=1, source_target_pairs={{0,1},{1,2},{2,3},{3,4},{4,5},{5,6},{6,7},{7,8},{8,9},{9,10},{10,1... | collective-permute-start | bytes 69128 | tf_op jit(solution)/shard_map/ppermute | solution.py:14
  125.6 36.5 %copy-start.1 = (f32[5,18,18,128]{3,2,1,0:T(8,128)}, f32[5,18,18,128]{3,2,1,0:T(8,128)S(1)}, u32[]{:S(2)}) copy-start(f32[5,18,18,128]{3,2,1,0:T(8,128)S(1)} %maximum_convert_fusion) | copy-start | bytes 2488324
  205.1 82.7 %collective-permute-start.7 = (bf16[5,1,16,128]{3,2,1,0:T(8,128)(2,1)}, bf16[5,1,16,128]{3,2,1,0:T(8,128)(2,1)S(1)}, u32[]{:S(2)}, u32[]{:S(2)}) collective-permute-start(bf16[5,1,16,128]{3,2,1,0:T(8,128)(2,1)} %get-tuple-element.142), channel_id=1, source_target_pairs={{32,0},{64,32},{96,64},{128,96},{160,128},{192,160},{224,192},{256... | collective-permute-start | bytes 61448 | tf_op jit(solution)/shard_map/ppermute | solution.py:16
  207.8 80.0 %collective-permute-start.6 = (bf16[5,1,16,128]{3,2,1,0:T(8,128)(2,1)S(1)}, bf16[5,1,16,128]{3,2,1,0:T(8,128)(2,1)S(1)}, u32[]{:S(2)}, u32[]{:S(2)}) collective-permute-start(bf16[5,1,16,128]{3,2,1,0:T(8,128)(2,1)S(1)} %get-tuple-element.141), channel_id=1, source_target_pairs={{0,32},{32,64},{64,96},{96,128},{128,160},{160,192},{192,224},{224... | collective-permute-start | bytes 61448 | tf_op jit(solution)/shard_map/ppermute | solution.py:14
  267.9 27.7 %collective-permute-start.11 = (bf16[1,4,5,1024]{3,1,2,0:T(4,128)(2,1)S(1)}, bf16[1,4,5,1024]{3,1,2,0:T(4,128)(2,1)S(1)}, u32[]{:S(2)}, u32[]{:S(2)}) collective-permute-start(bf16[1,4,5,1024]{3,1,2,0:T(4,128)(2,1)S(1)} %copy.544), channel_id=1, source_target_pairs={{1,0},{2,1},{3,2},{4,3},{5,4},{6,5},{7,6},{8,7},{9,8},{10,9},{11,1... | collective-permute-start | bytes 122888 | tf_op jit(solution)/shard_map/ppermute | solution.py:16
  276.9 18.8 %collective-permute-start.10 = (bf16[1,4,5,1024]{3,1,2,0:T(4,128)(2,1)S(1)}, bf16[1,4,5,1024]{3,1,2,0:T(4,128)(2,1)S(1)}, u32[]{:S(2)}, u32[]{:S(2)}) collective-permute-start(bf16[1,4,5,1024]{3,1,2,0:T(4,128)(2,1)S(1)} %copy.543), channel_id=1, source_target_pairs={{0,1},{1,2},{2,3},{3,4},{4,5},{5,6},{6,7},{7,8},{8,9},{9,10},{10,1... | collective-permute-start | bytes 122888 | tf_op jit(solution)/shard_map/ppermute | solution.py:14
  287.9 9.5 %collective-permute-start.9 = (bf16[5,18,1,128]{3,1,2,0:T(8,128)(2,1)S(1)}, bf16[5,18,1,128]{3,1,2,0:T(8,128)(2,1)}, u32[]{:S(2)}, u32[]{:S(2)}) collective-permute-start(bf16[5,18,1,128]{3,1,2,0:T(8,128)(2,1)S(1)} %copy.478), channel_id=1, source_target_pairs={{1,0},{2,1},{3,2},{4,3},{5,4},{6,5},{7,6},{8,7},{9,8},{10,9},{11,1... | collective-permute-start | bytes 69128 | tf_op jit(solution)/shard_map/ppermute | solution.py:16
  292.4 8.3 %collective-permute-start.8 = (bf16[5,18,1,128]{3,1,2,0:T(8,128)(2,1)}, bf16[5,18,1,128]{3,1,2,0:T(8,128)(2,1)}, u32[]{:S(2)}, u32[]{:S(2)}) collective-permute-start(bf16[5,18,1,128]{3,1,2,0:T(8,128)(2,1)} %copy.477), channel_id=1, source_target_pairs={{0,1},{1,2},{2,3},{3,4},{4,5},{5,6},{6,7},{7,8},{8,9},{9,10},{10,1... | collective-permute-start | bytes 69128 | tf_op jit(solution)/shard_map/ppermute | solution.py:14
  376.7 21.8 %copy-start.25 = (f32[4,5,16,16]{3,2,1,0:T(8,128)S(1)}, f32[4,5,16,16]{3,2,1,0:T(8,128)}, u32[]{:S(2)}) copy-start(f32[4,5,16,16]{3,2,1,0:T(8,128)} %copy.509) | copy-start | bytes 61444
  376.7 21.8 %copy-start.26 = (f32[4,5,16,16]{3,2,1,0:T(8,128)S(1)}, f32[4,5,16,16]{3,2,1,0:T(8,128)}, u32[]{:S(2)}) copy-start(f32[4,5,16,16]{3,2,1,0:T(8,128)} %copy.502) | copy-start | bytes 61444
  376.7 21.8 %copy-start.27 = (f32[4,5,16,16]{3,2,1,0:T(8,128)S(1)}, f32[4,5,16,16]{3,2,1,0:T(8,128)}, u32[]{:S(2)}) copy-start(f32[4,5,16,16]{3,2,1,0:T(8,128)} %copy.511) | copy-start | bytes 61444
  376.8 21.8 %copy-start.28 = (f32[4,5,16,16]{3,2,1,0:T(8,128)S(1)}, f32[4,5,16,16]{3,2,1,0:T(8,128)}, u32[]{:S(2)}) copy-start(f32[4,5,16,16]{3,2,1,0:T(8,128)} %copy.505) | copy-start | bytes 61444
  376.8 21.8 %copy-start.75 = (pred[4]{0:T(512)(128)(4,1)S(1)}, pred[4]{0:T(512)(128)(4,1)}, u32[]{:S(2)}) copy-start(pred[4]{0:T(512)(128)(4,1)} %get-tuple-element.172) | copy-start | bytes 16
  376.8 21.8 %copy-start.76 = (pred[4]{0:T(512)(128)(4,1)S(1)}, pred[4]{0:T(512)(128)(4,1)}, u32[]{:S(2)}) copy-start(pred[4]{0:T(512)(128)(4,1)} %get-tuple-element.173) | copy-start | bytes 16
  381.2 21.1 %collective-permute-start.13 = (bf16[1,5,16,128]{3,2,1,0:T(8,128)(2,1)S(1)}, bf16[1,5,16,128]{3,2,1,0:T(8,128)(2,1)S(1)}, u32[]{:S(2)}, u32[]{:S(2)}) collective-permute-start(bf16[1,5,16,128]{3,2,1,0:T(8,128)(2,1)S(1)} %stack.39), channel_id=1, source_target_pairs={{1,0},{2,1},{3,2},{4,3},{5,4},{6,5},{7,6},{8,7},{9,8},{10,9},{11,1... | collective-permute-start | bytes 61448 | tf_op jit(solution)/shard_map/ppermute | solution.py:16
  389.5 12.8 %collective-permute-start.12 = (bf16[1,5,16,128]{3,2,1,0:T(8,128)(2,1)S(1)}, bf16[1,5,16,128]{3,2,1,0:T(8,128)(2,1)S(1)}, u32[]{:S(2)}, u32[]{:S(2)}) collective-permute-start(bf16[1,5,16,128]{3,2,1,0:T(8,128)(2,1)S(1)} %stack.38), channel_id=1, source_target_pairs={{0,1},{1,2},{2,3},{3,4},{4,5},{5,6},{6,7},{7,8},{8,9},{9,10},{10,1... | collective-permute-start | bytes 61448 | tf_op jit(solution)/shard_map/ppermute | solution.py:14
  391.6 15.3 %collective-permute-start.15 = (bf16[1,5,16,128]{3,2,1,0:T(8,128)(2,1)S(1)}, bf16[1,5,16,128]{3,2,1,0:T(8,128)(2,1)S(1)}, u32[]{:S(2)}, u32[]{:S(2)}) collective-permute-start(bf16[1,5,16,128]{3,2,1,0:T(8,128)(2,1)S(1)} %stack.41), channel_id=1, source_target_pairs={{32,0},{64,32},{96,64},{128,96},{160,128},{192,160},{224,192},{256... | collective-permute-start | bytes 61448 | tf_op jit(solution)/shard_map/ppermute | solution.py:16
  396.6 10.3 %collective-permute-start.14 = (bf16[1,5,16,128]{3,2,1,0:T(8,128)(2,1)S(1)}, bf16[1,5,16,128]{3,2,1,0:T(8,128)(2,1)S(1)}, u32[]{:S(2)}, u32[]{:S(2)}) collective-permute-start(bf16[1,5,16,128]{3,2,1,0:T(8,128)(2,1)S(1)} %stack.40), channel_id=1, source_target_pairs={{0,32},{32,64},{64,96},{96,128},{128,160},{160,192},{192,224},{224... | collective-permute-start | bytes 61448 | tf_op jit(solution)/shard_map/ppermute | solution.py:14
  (74 other events, 529.8 us)
where the time goes:
time: 415 us; the launch traced here: 408 us
  local copies, waits for them, and re-layouts  237 us (57%)
  other arithmetic  83.1 us (20%)
  starting transfers between devices  68.3 us (16%)
  matrix products  12.9 us (3%)
    ppermute x8, starting transfers between devices, extended(): lax.ppermute(head, axis, [((i + 1) % count, i) for i in range(count)])  45.9 us
    reduce_sum x12, other arithmetic, pooled(): layer_in.reshape(shape_in[:-2] + (shape_in[-2] // 2, 2, shape_in[-1] // 2...  44.6 us
    unnamed x177, local copies, waits for them, and re-layouts  25.9 us
    ppermute x8, starting transfers between devices, extended(): lax.ppermute(tail, axis, [(i, (i + 1) % count) for i in range(count)])  22.3 us
    reduce_sum x12, local copies, waits for them, and re-layouts, pooled(): layer_in.reshape(shape_in[:-2] + (shape_in[-2] // 2, 2, shape_in[-1] // 2...  20 us
    slice x2, local copies, waits for them, and re-layouts, box_faces(): box_set[:, :, middle, high_at, middle]  16.3 us
    concatenate x2, local copies, waits for them, and re-layouts, cut_boxes(): jnp.concatenate([padded[..., -1:], padded, padded[..., :1]], axis=-1)  15.9 us
    gather x2, local copies, waits for them, and re-layouts, cut_boxes(): lax.dynamic_slice(wrapped, (anchor, anchor, anchor, col_at), (comp_count,...  12.3 us
  transfers between devices with their start and end apart: 16, of which 2 were waited for; matrix products, arithmetic and copies ran while one was open for 42% of the time, Pallas kernels for 0%

commit v1 on v0

v1 whole, which is shorter than its diff:
```python
import jax
import jax.numpy as jnp
from jax import lax
from jax.experimental import pallas as pl
from jax.experimental.pallas import tpu as pltpu
from jax.sharding import PartitionSpec as P

F32, BF16 = jnp.float32, jnp.bfloat16
SLOTS, COMPS, EDGE, HALF, LANES = 4, 5, 32, 16, 128
ROWS = COMPS * EDGE
CROWS = COMPS * HALF
CELLS = CROWS * HALF
PLANE = EDGE * EDGE
QUAD = 256

Y_NEAR, Y_NEXT, Y_ROW, Y_HALF, Y_FLUX, Y_COVER = 0, 80, 160, 320, 480, 560
Y_ROWS = 576
Z_NEAR, Z_NEXT, Z_FLUX, Z_LOW, Z_HIGH, Z_COVER = 0, 80, 160, 240, 256, 272
Z_ROWS = 288


def iota(shape, dim):
    return lax.broadcasted_iota(jnp.int32, shape, dim)


def ones_at(mask):
    return jnp.where(mask, 1.0, 0.0).astype(BF16)


def mm(left, right):
    return lax.dot_general(left, right, (((1,), (0,)), ((), ())), preferred_element_type=F32)


def chain(index, values):
    out = jnp.full(index.shape, values[-1], values[-1].dtype)
    for k in range(len(values) - 2, -1, -1):
        out = jnp.where(index == k, values[k], out)
    return out


class Tables:
    def __init__(self, col, cnt, nbr, rate):
        self.start = [col[s] * HALF for s in range(SLOTS)]
        self.used = [jnp.where(s < cnt[0], 1, 0) for s in range(SLOTS)]
        self.near = [[nbr[s, f] for s in range(SLOTS)] for f in range(4)]
        self.rate = [rate[c] for c in range(COMPS)]

    def rates(self, rows, per):
        return chain(iota((rows, LANES), 0) // per, self.rate)

    def packed(self, dim):
        n, x = iota((LANES, LANES), dim), iota((LANES, LANES), 1 - dim)
        return n // EDGE, n % EDGE, x

    def to_coarse(self, face):
        s, e, x = self.packed(0)
        hit = (x == chain(s, self.start) + e // 2) & (chain(s, self.used) > 0)
        if face is not None:
            hit = hit & (chain(s, self.near[face]) < 0)
        return ones_at(hit)

    def from_coarse(self, face, unlinked):
        s, e, x = self.packed(1)
        hit = x == chain(s, self.start) + e // 2
        if unlinked:
            hit = hit & (chain(s, self.near[face]) < 0)
        return ones_at(hit)

    def linked_lanes(self, face):
        s, e, n = self.packed(1)
        return ones_at(n == chain(s, self.near[face]) * EDGE + jnp.where(chain(s, self.near[face]) < 0, -LANES, e))

    def row_stencil(self):
        s, e, n = self.packed(1)
        low, high, x0 = chain(s, self.near[0]), chain(s, self.near[1]), chain(s, self.start)
        inside = (n // EDGE == s) & ((n % EDGE == e - 1) | (n % EDGE == e + 1))
        at_low = (e == 0) & (low >= 0) & (n == low * EDGE + EDGE - 1)
        at_high = (e == EDGE - 1) & (high >= 0) & (n == high * EDGE)
        left = (e == 0) & (low < 0) & (n == (x0 - 1) % LANES)
        right = (e == EDGE - 1) & (high < 0) & (n == (x0 + HALF) % LANES)
        return jnp.concatenate([ones_at(inside | at_low | at_high), ones_at(left | right)], axis=0)

    def side_pick(self):
        n, x = iota((LANES, LANES), 1), iota((LANES, LANES), 0)
        s, high = n // EDGE, n % EDGE >= HALF
        x0 = chain(s, self.start)
        spot = jnp.where(high, (x0 + HALF) % LANES, (x0 - 1) % LANES)
        open_face = jnp.where(high, chain(s, self.near[1]), chain(s, self.near[0])) < 0
        return ones_at((x == spot) & open_face)

    def pool_spread(self, mode):
        m, k = iota((SLOTS * LANES, QUAD), 0), iota((SLOTS * LANES, QUAD), 1)
        s, lane, x = m // LANES, m % LANES, k % LANES
        e, x0 = lane % EDGE, chain(s, self.start)
        hit = (lane // (2 * EDGE) == k // LANES) & (chain(s, self.used) > 0)
        if mode == 0:
            return ones_at(hit & (x == x0 + e // 2))
        left = (e == 0) & (chain(s, self.near[0]) < 0) & (x == (x0 - 1) % LANES)
        right = (e == EDGE - 1) & (chain(s, self.near[1]) < 0) & (x == (x0 + HALF) % LANES)
        return ones_at(hit & (left | right))


def copies(rows, per):
    out, src = iota((rows, rows // per), 0), iota((rows, rows // per), 1)
    return ones_at(out // per == src)


def pair_rows():
    out, src = iota((CROWS, ROWS), 0), iota((CROWS, ROWS), 1)
    return ones_at(src // 2 == out)


def z_stencil():
    out, src = iota((ROWS, ROWS), 0), iota((ROWS, ROWS), 1)
    same = out // EDGE == src // EDGE
    beside = same & ((src == out + 1) | (src == out - 1))
    return jnp.where(src == out, -6.0, jnp.where(beside, 1.0, 0.0)).astype(BF16)


def plane_stencil():
    m, n = iota((3 * QUAD, QUAD), 0), iota((3 * QUAD, QUAD), 1)
    e = n % EDGE
    own = (m < QUAD) & (
        ((m == n - 1) & (e > 0)) | ((m == n + 1) & (e < EDGE - 1)) | (m == n - EDGE) | (m == n + EDGE)
    )
    before = (m >= QUAD) & (m < QUAD + LANES) & (m - QUAD - LANES == n - EDGE)
    after = (m >= QUAD + LANES) & (m < 2 * QUAD) & (m - QUAD - LANES + QUAD == n + EDGE)
    p = m - 2 * QUAD
    partner = (m >= 2 * QUAD) & (
        ((e == 0) & (p == n + EDGE - 1)) | ((e == EDGE - 1) & (p == n - EDGE + 1))
    )
    return ones_at(own | before | after | partner)


def side_place(q):
    m, n = iota((LANES, QUAD), 0), iota((LANES, QUAD), 1)
    y, e = (n // EDGE + q * (QUAD // EDGE)) // 2, n % EDGE
    return ones_at((m < EDGE) & (m % HALF == y) & (e == jnp.where(m < HALF, 0, EDGE - 1)))


def partner_columns(load, tables, rows):
    lane = iota((rows, PLANE), 1) % EDGE
    at_low = jnp.where(lane == EDGE - 1, 1.0, 0.0).astype(BF16)
    at_high = jnp.where(lane == 0, 1.0, 0.0).astype(BF16)
    out = []
    for s in range(SLOTS):
        low, high = tables.near[0][s], tables.near[1][s]
        has_low = jnp.where(low >= 0, 1.0, 0.0).astype(BF16)
        has_high = jnp.where(high >= 0, 1.0, 0.0).astype(BF16)
        out.append(
            load(jnp.maximum(low, 0)) * (at_low * has_low) + load(jnp.maximum(high, 0)) * (at_high * has_high)
        )
    return out


def plane_terms(fields, partners, sides, q, weights):
    lo, hi = QUAD * q, QUAD * (q + 1)
    parts = []
    for s in range(SLOTS):
        field = fields[s]
        rows = field.shape[0]
        none = jnp.zeros((rows, LANES), BF16)
        parts.append(
            jnp.concatenate(
                [
                    field[:, lo:hi],
                    field[:, lo - LANES : lo] if q else none,
                    field[:, hi : hi + LANES] if q < 3 else none,
                    partners[s][:, lo:hi],
                    sides[s],
                ],
                axis=1,
            )
        )
    return mm(
        jnp.concatenate(parts, axis=0), jnp.concatenate([weights, side_place(q)], axis=0)
    )


def slot_sides(sides):
    return [sides if s == 0 else pltpu.roll(sides, LANES - EDGE * s, 1) for s in range(SLOTS)]


def edge_lanes(ghost, s, top):
    shift = (LANES - EDGE * (s + 1 if top else s)) % LANES
    moved = pltpu.roll(ghost, shift, 1) if shift else ghost
    lane = iota(ghost.shape, 1)
    kept = jnp.where(lane >= LANES - EDGE if top else lane < EDGE, moved, 0.0)
    none = jnp.zeros(ghost.shape, F32)
    return jnp.concatenate([none, kept] if top else [kept, none], axis=1)


def y_message_kernel(col, cnt, nbr, rate, low_ref, high_ref, coarse_ref, near_ref, far_ref, level):
    tables = Tables(col, cnt, nbr, rate)
    level[...] = coarse_ref[...].astype(F32)
    rates = tables.rates(ROWS, EDGE)
    coarse_rates = tables.rates(CROWS, HALF)
    stencil, rows_z, double, pairs = tables.row_stencil(), z_stencil(), copies(ROWS, 2), pair_rows()
    messages = []
    for top in (True, False):
        m, n = iota((SLOTS * LANES, QUAD), 0), iota((SLOTS * LANES, QUAD), 1)
        edge, inner = (LANES - EDGE, LANES - 2 * EDGE) if top else (0, EDGE)
        pack = ones_at(
            (m // LANES == n % LANES // EDGE)
            & (m % LANES == n % EDGE + jnp.where(n < LANES, edge, inner))
        )
        tile = high_ref if top else low_ref
        both = mm(jnp.concatenate([tile[s] for s in range(SLOTS)], axis=1), pack)
        row = both[:, :LANES].astype(BF16)
        near = level[pl.ds(HALF - 1 if top else 0, CROWS, stride=HALF), :]
        following = level[pl.ds(HALF - 2 if top else 1, CROWS, stride=HALF), :]
        near_fine = mm(double, near.astype(BF16)).astype(BF16)
        around = mm(jnp.concatenate([row, near_fine], axis=1), stencil) + mm(rows_z, row) + both[:, LANES:]
        half = (both[:, :LANES] + 2.0 * rates * around).astype(BF16)
        place = tables.to_coarse(3 if top else 2)
        sums = mm(pairs, jnp.concatenate([row, half], axis=1)).astype(BF16)
        cover = jnp.minimum(mm(jnp.ones((HALF, LANES), BF16), place), 1.0)
        flux = 0.25 * coarse_rates * mm(sums, jnp.concatenate([place, place], axis=0))
        flux = flux - coarse_rates * near * cover[:1]
        messages.append(
            (
                (Y_NEAR, near.astype(BF16)),
                (Y_NEXT, following.astype(BF16)),
                (Y_ROW, row),
                (Y_HALF, half),
                (Y_FLUX, flux.astype(BF16)),
                (Y_COVER, cover.astype(BF16)),
            )
        )
    even = lax.axis_index("fine") % 2 == 0
    up_ref_is_near = even

    @pl.when(up_ref_is_near)
    def _():
        for at, value in messages[0]:
            near_ref[at : at + value.shape[0], :] = value
        for at, value in messages[1]:
            far_ref[at : at + value.shape[0], :] = value

    @pl.when(jnp.logical_not(up_ref_is_near))
    def _():
        for at, value in messages[1]:
            near_ref[at : at + value.shape[0], :] = value
        for at, value in messages[0]:
            far_ref[at : at + value.shape[0], :] = value


def sort_arrivals(axis, near_ref, far_ref, arrived):
    even = lax.axis_index(axis) % 2 == 0

    @pl.when(even)
    def _():
        arrived[0] = far_ref[...]
        arrived[1] = near_ref[...]

    @pl.when(jnp.logical_not(even))
    def _():
        arrived[0] = near_ref[...]
        arrived[1] = far_ref[...]


PLANES = 16


def plane_rows(per, scale_inner):
    rows = COMPS * per
    out, src = iota((PLANES, rows), 0), iota((PLANES, rows), 1)
    c, last = out % 8, out >= 8
    edge = src == jnp.where(last, c * per + per - 1, c * per)
    real = c < COMPS
    if not scale_inner:
        return ones_at(edge & real)
    inner = src == jnp.where(last, c * per + per - 2, c * per + 1)
    return jnp.where(edge & real, -6.0, jnp.where(inner & real, 1.0, 0.0)).astype(BF16)


def z_message_kernel(
    col, cnt, nbr, rate, fine_ref, coarse_ref, y_near, y_far, near_ref, far_ref, arrived, planes, flux
):
    tables = Tables(col, cnt, nbr, rate)
    sort_arrivals("fine", y_near, y_far, arrived)
    picks = jnp.concatenate([plane_rows(EDGE, False), plane_rows(EDGE, True)], axis=0)
    inner = []
    for s in range(SLOTS):
        got = mm(picks, fine_ref[s])
        planes[s] = got[:PLANES].astype(BF16)
        inner.append(got[PLANES:])
    level = [
        [coarse_ref[pl.ds((c * HALF + z) * HALF, HALF), :] for c in range(COMPS)] for z in (0, 1, HALF - 2, HALF - 1)
    ]
    level = [jnp.concatenate(part, axis=0) for part in level]
    outer = jnp.concatenate([level[0], level[3]], axis=0)
    m, n = iota((2 * CROWS, LANES), 0), iota((2 * CROWS, LANES), 1)
    picked = jnp.where(m % HALF == n % HALF, mm(outer, tables.side_pick()), 0.0).astype(BF16)
    out, src = iota((PLANES, 2 * CROWS), 0), iota((PLANES, 2 * CROWS), 1)
    gather = ones_at((out // 8 == src // CROWS) & (out % 8 == src % CROWS // HALF))
    sides = slot_sides(mm(gather, picked))
    sides = [part.astype(BF16) for part in sides]
    fields = [planes[s] for s in range(SLOTS)]
    partners = partner_columns(lambda t: planes[t], tables, PLANES)
    fine_pick, coarse_pick = plane_rows(EDGE, False), plane_rows(HALF, False)
    ghosts, corners = [], []
    for k, face in ((0, 2), (1, 3)):
        row = mm(fine_pick, arrived[k, Y_ROW : Y_ROW + ROWS, :]).astype(BF16)
        corner = mm(coarse_pick, arrived[k, Y_NEAR : Y_NEAR + CROWS, :]).astype(BF16)
        corners.append(corner)
        ghosts.append(
            mm(
                jnp.concatenate([row, corner], axis=1),
                jnp.concatenate([tables.linked_lanes(face), tables.from_coarse(face, True)], axis=0),
            )
        )
    weights = plane_stencil()
    rates = chain(iota((PLANES, QUAD), 0) % 8, tables.rate + [jnp.zeros((), F32)] * 3)
    place = tables.pool_spread(0)
    for q in range(4):
        terms = plane_terms(fields, partners, sides, q, weights)
        summed = []
        for s in range(SLOTS):
            around = terms[PLANES * s : PLANES * (s + 1)] + inner[s][:, QUAD * q : QUAD * (q + 1)]
            if q == 0:
                around = around + edge_lanes(ghosts[0], s, False)
            if q == 3:
                around = around + edge_lanes(ghosts[1], s, True)
            field = fields[s][:, QUAD * q : QUAD * (q + 1)].astype(F32)
            summed.append((2.0 * field + 2.0 * rates * around).astype(BF16))
        for half in range(2):
            cells = mm(
                jnp.concatenate([part[:, LANES * half : LANES * (half + 1)] for part in summed], axis=1), place
            )
            y = 4 * q + 2 * half
            flux[pl.ds(y, PLANES, stride=HALF), :] = cells[:, :LANES]
            flux[pl.ds(y + 1, PLANES, stride=HALF), :] = cells[:, LANES:]
    cover = jnp.minimum(mm(jnp.ones((HALF, LANES), BF16), tables.to_coarse(None)), 1.0)
    coarse_rates = tables.rates(CROWS, HALF)
    messages = []
    for top in (True, False):
        near, following = (level[3], level[2]) if top else (level[0], level[1])
        at = 8 * HALF if top else 0
        total = 0.25 * coarse_rates * flux[at : at + CROWS, :] - coarse_rates * near.astype(F32) * cover[:1]
        messages.append(
            (
                (Z_NEAR, near),
                (Z_NEXT, following),
                (Z_FLUX, total.astype(BF16)),
                (Z_LOW, corners[0]),
                (Z_HIGH, corners[1]),
                (Z_COVER, cover.astype(BF16)),
            )
        )
    even = lax.axis_index("own") % 2 == 0

    @pl.when(even)
    def _():
        for at, value in messages[0]:
            near_ref[at : at + value.shape[0], :] = value
        for at, value in messages[1]:
            far_ref[at : at + value.shape[0], :] = value

    @pl.when(jnp.logical_not(even))
    def _():
        for at, value in messages[1]:
            near_ref[at : at + value.shape[0], :] = value
        for at, value in messages[0]:
            far_ref[at : at + value.shape[0], :] = value


SPAN = 32
DEEP = HALF + 2


def at_cell(c, z, y):
    return (c * DEEP + z + 1) * SPAN + 8 + y


def advance_kernel(
    col, cnt, nbr, rate, fine_ref, coarse_ref, y_near, y_far, z_near, z_far, coarse_out, fine_out,
    y_arr, z_arr, old, mean, half, split, average, outside,
):
    tables = Tables(col, cnt, nbr, rate)
    sort_arrivals("fine", y_near, y_far, y_arr)
    sort_arrivals("own", z_near, z_far, z_arr)
    for c in range(COMPS):
        for z in range(HALF):
            old[pl.ds(at_cell(c, z, 0), HALF), :] = coarse_ref[pl.ds((c * HALF + z) * HALF, HALF), :].astype(F32)
        for k, y in ((0, -1), (1, HALF)):
            at = Y_NEAR + c * HALF
            old[pl.ds(at_cell(c, 0, y), HALF, stride=SPAN), :] = y_arr[k, at : at + HALF, :].astype(F32)
        for k, z in ((0, -1), (1, HALF)):
            at = Z_NEAR + c * HALF
            old[pl.ds(at_cell(c, z, 0), HALF), :] = z_arr[k, at : at + HALF, :].astype(F32)
            row = c + (8 if k == 0 else 0)
            low = z_arr[k, Z_LOW : Z_LOW + HALF, :].astype(F32)
            high = z_arr[k, Z_HIGH : Z_HIGH + HALF, :].astype(F32)
            old[pl.ds(at_cell(c, z, -1), 1), :] = low[row : row + 1]
            old[pl.ds(at_cell(c, z, HALF), 1), :] = high[row : row + 1]

    def mixed(centre, total, r):
        total = total + pltpu.roll(centre, 1, 1) + pltpu.roll(centre, LANES - 1, 1)
        return centre + (0.5 * r) * (total - 6.0 * centre)

    for c in range(COMPS):
        r = tables.rate[c]
        for z in range(HALF):
            centre = old[pl.ds(at_cell(c, z, 0), HALF), :]
            total = (
                old[pl.ds(at_cell(c, z, -1), HALF), :]
                + old[pl.ds(at_cell(c, z, 1), HALF), :]
                + old[pl.ds(at_cell(c, z - 1, 0), HALF), :]
                + old[pl.ds(at_cell(c, z + 1, 0), HALF), :]
            )
            mean[pl.ds(at_cell(c, z, 0), HALF), :] = mixed(centre, total, r)
        for k, y, inside in ((0, -1, 0), (1, HALF, HALF - 1)):
            centre = old[pl.ds(at_cell(c, 0, y), HALF, stride=SPAN), :]
            at = Y_NEXT + c * HALF
            total = (
                y_arr[k, at : at + HALF, :].astype(F32)
                + old[pl.ds(at_cell(c, 0, inside), HALF, stride=SPAN), :]
                + old[pl.ds(at_cell(c, -1, y), HALF, stride=SPAN), :]
                + old[pl.ds(at_cell(c, 1, y), HALF, stride=SPAN), :]
            )
            mean[pl.ds(at_cell(c, 0, y), HALF, stride=SPAN), :] = mixed(centre, total, r)
        for k, z, inside in ((0, -1, 0), (1, HALF, HALF - 1)):
            centre = old[pl.ds(at_cell(c, z, 0), HALF), :]
            at = Z_NEXT + c * HALF
            total = (
                z_arr[k, at : at + HALF, :].astype(F32)
                + old[pl.ds(at_cell(c, inside, 0), HALF), :]
                + old[pl.ds(at_cell(c, z, -1), HALF), :]
                + old[pl.ds(at_cell(c, z, 1), HALF), :]
            )
            mean[pl.ds(at_cell(c, z, 0), HALF), :] = mixed(centre, total, r)

    rates = tables.rates(ROWS, EDGE)
    rates2 = 2.0 * jnp.concatenate([rates, rates], axis=1)
    weights, double = plane_stencil(), copies(ROWS, 2)
    out, src = iota((ROWS, 2 * CROWS), 0), iota((ROWS, 2 * CROWS), 1)
    end = jnp.where(src < CROWS, 0, EDGE - 1)
    rows_z = jnp.concatenate(
        [z_stencil(), ones_at((out % EDGE == end) & (out // EDGE == src % CROWS // HALF))], axis=1
    )
    pick = tables.side_pick()
    m, n = iota((CELLS, LANES), 0), iota((CELLS, LANES), 1)
    own_y = m % HALF == n % HALF
    picked = []
    for level in (old, mean):
        cells = jnp.concatenate(
            [level[pl.ds(at_cell(c, z, 0), HALF), :] for c in range(COMPS) for z in range(HALF)], axis=0
        ).astype(BF16)
        picked.append(jnp.where(own_y, mm(cells, pick), 0.0).astype(BF16))
    sides_both = mm(side_rows(), jnp.concatenate(picked, axis=1))

    linked = [tables.linked_lanes(2), tables.linked_lanes(3)]
    opened = [tables.from_coarse(2, True), tables.from_coarse(3, True)]
    window = tables.from_coarse(None, False)

    def level_row(level, y):
        rows = [level[pl.ds(at_cell(c, 0, y), HALF, stride=SPAN), :] for c in range(COMPS)]
        return mm(double, jnp.concatenate(rows, axis=0).astype(BF16)).astype(BF16)

    def ghost_planes(level):
        planes = []
        for z in (-1, HALF):
            planes += [level[pl.ds(at_cell(c, z, 0), HALF), :] for c in range(COMPS)]
        return mm(jnp.concatenate(planes, axis=0).astype(BF16), window)

    def substep(load, sides, ghosts, planes, finish):
        fields = [load(s) for s in range(SLOTS)]
        partners = partner_columns(load, tables, ROWS)
        sides = [part.astype(BF16) for part in slot_sides(sides)]
        spread = []
        for s in range(SLOTS):
            part = jnp.where(iota(planes.shape, 1) // EDGE == s, planes, 0.0)
            part = part + pltpu.roll(part, EDGE, 1)
            spread.append(part + pltpu.roll(part, 2 * EDGE, 1))
        m, n = iota((2 * CROWS, LANES), 0), iota((2 * CROWS, LANES), 1)
        for q in range(4):
            terms = plane_terms(fields, partners, sides, q, weights)
            for s in range(SLOTS):
                outer = []
                for k in (2 * q, 2 * q + 1):
                    outer.append(jnp.where(m % HALF == 2 * k + n // (2 * EDGE), spread[s], 0.0).astype(BF16))
                field = fields[s][:, QUAD * q : QUAD * (q + 1)]
                around = terms[ROWS * s : ROWS * (s + 1)] + mm(
                    rows_z, jnp.concatenate([field, jnp.concatenate(outer, axis=1)], axis=0)
                )
                if q == 0:
                    around = around + edge_lanes(ghosts[0], s, False)
                if q == 3:
                    around = around + edge_lanes(ghosts[1], s, True)
                finish(s, q, field.astype(F32) + rates2 * around)

    first = []
    for k, y in ((0, -1), (1, HALF)):
        row = y_arr[k, Y_ROW : Y_ROW + ROWS, :]
        first.append(
            mm(
                jnp.concatenate([row, level_row(old, y)], axis=1),
                jnp.concatenate([linked[k], opened[k]], axis=0),
            )
        )

    def keep_half(s, q, value):
        half[s, :, QUAD * q : QUAD * (q + 1)] = value.astype(BF16)

    substep(lambda s: fine_ref[s], sides_both[:, :LANES], first, ghost_planes(old), keep_half)

    out, src = iota((ROWS, 2 * PLANES), 0), iota((ROWS, 2 * PLANES), 1)
    low_end = (out % EDGE == 0) & (src == 8 + out // EDGE)
    high_end = (out % EDGE == EDGE - 1) & (src == PLANES + out // EDGE)
    ends = ones_at(low_end | high_end)
    second = []
    for k, y in ((0, -1), (1, HALF)):
        m, n = iota((SLOTS * LANES, LANES), 0), iota((SLOTS * LANES, LANES), 1)
        edge = LANES - EDGE if k else 0
        pack = ones_at((m // LANES == n // EDGE) & (m % LANES == n % EDGE + edge))
        tile = PLANE - LANES if k else 0
        mine = mm(jnp.concatenate([fine_ref[s, :, tile : tile + LANES] for s in range(SLOTS)], axis=1), pack)
        at = Z_HIGH if k else Z_LOW
        corner = jnp.concatenate([z_arr[0, at : at + PLANES, :], z_arr[1, at : at + PLANES, :]], axis=0)
        corner = mm(mm(ends, corner).astype(BF16), window)
        theirs = mm(y_arr[k, Y_HALF : Y_HALF + ROWS, :], linked[k]) + 2.0 * rates * (mine + corner)
        theirs = theirs.astype(BF16).astype(F32)
        is_linked = chain(iota((ROWS, LANES), 1) // EDGE, tables.near[2 + k]) >= 0
        second.append(jnp.where(is_linked, theirs, mm(level_row(mean, y), opened[k])))

    def keep_new(s, q, value):
        value = jnp.where(tables.used[s] > 0, value, 0.0)
        fine_out[s, :, QUAD * q : QUAD * (q + 1)] = value.astype(BF16)

    substep(lambda s: half[s], sides_both[:, LANES:], second, ghost_planes(mean), keep_new)

    into_cells, into_faces = tables.pool_spread(0), tables.pool_spread(1)
    faces_twice = jnp.concatenate([into_faces, into_faces], axis=0)
    for k in range(8):
        lanes = slice(LANES * k, LANES * (k + 1))
        new = jnp.concatenate([fine_out[s, :, lanes] for s in range(SLOTS)], axis=1)
        states = jnp.concatenate(
            [fine_ref[s, :, lanes] for s in range(SLOTS)] + [half[s, :, lanes] for s in range(SLOTS)], axis=1
        )
        cells, faces = mm(new, into_cells), mm(states, faces_twice)
        for i, value in enumerate((cells[:, :LANES], cells[:, LANES:], faces[:, :LANES], faces[:, LANES:])):
            split[i] = value
            pair = split[i, pl.ds(0, CROWS, stride=2), :] + split[i, pl.ds(1, CROWS, stride=2), :]
            target = average if i < 2 else outside
            target[pl.ds(2 * k + i % 2, CROWS, stride=HALF), :] = pair

    x = iota((HALF, LANES), 1)
    covered, left, right = x < 0, x < 0, x < 0
    for s in range(SLOTS):
        x0, used = tables.start[s], tables.used[s] > 0
        covered = covered | ((x >= x0) & (x < x0 + HALF) & used)
        left = left | ((x == (x0 - 1) % LANES) & used & (tables.near[0][s] < 0))
        right = right | ((x == (x0 + HALF) % LANES) & used & (tables.near[1][s] < 0))
    left, right = jnp.where(left, 1.0, 0.0), jnp.where(right, 1.0, 0.0)
    row = iota((HALF, LANES), 0)
    below = [jnp.where(row == (HALF - 1 if k else 0), y_arr[k, Y_COVER : Y_COVER + HALF, :].astype(F32), 0.0) for k in (0, 1)]
    ahead = [z_arr[k, Z_COVER : Z_COVER + HALF, :].astype(F32) for k in (0, 1)]
    for c in range(COMPS):
        r = tables.rate[c]
        for z in range(HALF):
            level0 = old[pl.ds(at_cell(c, z, 0), HALF), :]
            level1 = mean[pl.ds(at_cell(c, z, 0), HALF), :]
            line = pl.ds((c * HALF + z) * HALF, HALF)
            base = -r * level1
            change = 0.25 * r * outside[line, :] + (left + right) * base
            change = change - r * (left * pltpu.roll(level0, LANES - 1, 1) + right * pltpu.roll(level0, 1, 1))
            for k in (0, 1):
                whole = y_arr[k, Y_FLUX + c * HALF : Y_FLUX + (c + 1) * HALF, :].astype(F32)
                gain = base + (2.0 * r * r) * level0
                if z in (0, HALF - 1):
                    corner = old[pl.ds(at_cell(c, -1 if z == 0 else HALF, HALF if k else -1), 1), :]
                    gain = gain + (r * r) * corner
                one = row == (HALF - 1 if k else 0)
                change = change + jnp.where(one, whole[z : z + 1], 0.0) + below[k] * gain
            for k, edge in ((0, 0), (1, HALF - 1)):
                if z == edge:
                    flux = z_arr[k, Z_FLUX + c * HALF : Z_FLUX + (c + 1) * HALF, :].astype(F32)
                    change = change + flux + ahead[k] * (base + (2.0 * r * r) * level0)
            value = jnp.where(covered, 0.125 * average[line, :], 2.0 * level1 - level0 + change)
            coarse_out[line, :] = value.astype(BF16)


def side_rows():
    out, src = iota((ROWS, CELLS), 0), iota((ROWS, CELLS), 1)
    return ones_at(out // 2 == src // HALF)


SCALARS = [pl.BlockSpec(memory_space=pltpu.SMEM)] * 4
PARAMS = pltpu.CompilerParams(vmem_limit_bytes=48 * 1024 * 1024)


def whole():
    return pl.BlockSpec(memory_space=pltpu.VMEM)


def tile(lane):
    return pl.BlockSpec((SLOTS, ROWS, LANES), lambda i: (0, 0, lane))


def local(coarse_cells, fine_cells, diffusivity, patch_column, patch_count, neighbor_slot):
    fine = fine_cells.reshape(SLOTS, ROWS, PLANE)
    coarse = coarse_cells.reshape(CELLS, LANES)
    tables = (patch_column, patch_count, neighbor_slot, diffusivity)
    n_own, n_fine = lax.axis_size("own"), lax.axis_size("fine")

    def swap(value, axis, count, far):
        shift = 1 if far else 0
        pairs = []
        for i in range(count):
            partner = ((i - shift) ^ 1) + shift
            pairs.append((i, partner % count))
        return lax.ppermute(value, axis, pairs)

    y_shape = jax.ShapeDtypeStruct((Y_ROWS, LANES), BF16)
    y_near, y_far = pl.pallas_call(
        y_message_kernel,
        grid=(1,),
        in_specs=SCALARS + [tile(0), tile(7), pl.BlockSpec((CELLS, LANES), lambda i: (0, 0))],
        out_specs=[pl.BlockSpec((Y_ROWS, LANES), lambda i: (0, 0))] * 2,
        out_shape=[y_shape] * 2,
        scratch_shapes=[pltpu.VMEM((CELLS, LANES), F32)],
        compiler_params=PARAMS,
        name="y_messages",
    )(*tables, fine, fine, coarse)
    y_near, y_far = swap(y_near, "fine", n_fine, False), swap(y_far, "fine", n_fine, True)

    z_shape = jax.ShapeDtypeStruct((Z_ROWS, LANES), BF16)
    z_near, z_far = pl.pallas_call(
        z_message_kernel,
        in_specs=SCALARS + [whole()] * 4,
        out_specs=[whole()] * 2,
        out_shape=[z_shape] * 2,
        scratch_shapes=[
            pltpu.VMEM((2, Y_ROWS, LANES), BF16),
            pltpu.VMEM((SLOTS, PLANES, PLANE), BF16),
            pltpu.VMEM((PLANES * HALF, LANES), F32),
        ],
        compiler_params=PARAMS,
        name="z_messages",
    )(*tables, fine, coarse, y_near, y_far)
    z_near, z_far = swap(z_near, "own", n_own, False), swap(z_far, "own", n_own, True)

    coarse_new, fine_new = pl.pallas_call(
        advance_kernel,
        in_specs=SCALARS + [whole()] * 6,
        out_specs=[whole()] * 2,
        out_shape=[
            jax.ShapeDtypeStruct((CELLS, LANES), BF16),
            jax.ShapeDtypeStruct((SLOTS, ROWS, PLANE), BF16),
        ],
        scratch_shapes=[
            pltpu.VMEM((2, Y_ROWS, LANES), BF16),
            pltpu.VMEM((2, Z_ROWS, LANES), BF16),
            pltpu.VMEM((COMPS * DEEP * SPAN, LANES), F32),
            pltpu.VMEM((COMPS * DEEP * SPAN, LANES), F32),
            pltpu.VMEM((SLOTS, ROWS, PLANE), BF16),
            pltpu.VMEM((4, ROWS, LANES), F32),
            pltpu.VMEM((CELLS, LANES), F32),
            pltpu.VMEM((CELLS, LANES), F32),
        ],
        compiler_params=PARAMS,
        name="advance",
    )(*tables, fine, coarse, y_near, y_far, z_near, z_far)
    return coarse_new.reshape(coarse_cells.shape), fine_new.reshape(fine_cells.shape)


def solution(mesh):
    return jax.shard_map(
        local,
        mesh=mesh,
        in_specs=(
            P(None, "own", "fine", None),
            P(("own", "fine"), None, None, None),
            P(),
            P(("own", "fine")),
            P(("own", "fine")),
            P(("own", "fine"), None),
        ),
        out_specs=(P(None, "own", "fine", None), P(("own", "fine"), None, None, None)),
        check_vma=False,
    )
```

time: 415 us -> 48.7 us (0.12); the launches traced: 408 us -> 48 us
  local copies, waits for them, and re-layouts: 237 us -> 4.27 us
  other arithmetic: 83.1 us -> 0 us
  starting transfers between devices: 68.3 us -> 18.8 us
  Pallas kernels: 0 us -> 14.1 us
  matrix products: 12.9 us -> 0 us
  waiting for transfers between devices: 3.73 us -> 9.48 us
    slice x52 -> x0, local copies, waits for them, and re-layouts: 104 us -> none  [the longest x2 16.3 us: box_faces(): box_set[:, :, middle, high_at, middle]]
    reduce_sum x16 -> x0, other arithmetic: 51.8 us -> none  [the longest x12 44.6 us: pooled(): layer_in.reshape(shape_in[:-2] + (shape_in[-2] // 2, 2, shape_in[-1] // 2...]
    ppermute x16 -> x4, starting transfers between devices: 68.3 us -> 18.8 us  [swap(): return lax.ppermute(value, axis, pairs)]
    gather x10 -> x0, local copies, waits for them, and re-layouts: 22.7 us -> none  [the longest x2 12.3 us: cut_boxes(): lax.dynamic_slice(wrapped, (anchor, anchor, anchor, col_at), (comp_count,...]
    unnamed x177 -> x10, local copies, waits for them, and re-layouts: 25.9 us -> 4.27 us
    reduce_sum x12 -> x0, local copies, waits for them, and re-layouts: 20 us -> none  [pooled(): layer_in.reshape(shape_in[:-2] + (shape_in[-2] // 2, 2, shape_in[-1] // 2...]
    concatenate x3 -> x0, local copies, waits for them, and re-layouts: 16.6 us -> none  [the longest x2 15.9 us: cut_boxes(): jnp.concatenate([padded[..., -1:], padded, padded[..., :1]], axis=-1)]
    pallas_call x0 -> x3, Pallas kernels: none -> 14.1 us  [the longest x1 9.36 us: local(): pl.pallas_call(advance_kernel, in_specs=SCALARS + [whole()] * 6, out_spec...]
  transfers between devices with their start and end apart: 16 -> 4, of which waited for: 2 -> 2; matrix products, arithmetic and copies ran while one was open for 42% -> 0% of each run, Pallas kernels for 0% -> 0%
where the time goes in v1:
time: 48.7 us; the launch traced here: 48 us
  starting transfers between devices  18.8 us (39%)
  Pallas kernels  14.1 us (29%)
  waiting for transfers between devices  9.48 us (19%)
  local copies, waits for them, and re-layouts  4.27 us (9%)
  between operations  1.35 us (3%)
    ppermute x4, starting transfers between devices, swap(): return lax.ppermute(value, axis, pairs)  18.8 us
    ppermute x4, waiting for transfers between devices, swap(): return lax.ppermute(value, axis, pairs)  9.48 us
    pallas_call x1, Pallas kernels, local(): pl.pallas_call(advance_kernel, in_specs=SCALARS + [whole()] * 6, out_spec...  9.36 us
    unnamed x10, local copies, waits for them, and re-layouts  4.27 us
    pallas_call x1, Pallas kernels, local(): pl.pallas_call(z_message_kernel, in_specs=SCALARS + [whole()] * 4, out_sp...  2.89 us
    pallas_call x1, Pallas kernels, local(): pl.pallas_call(y_message_kernel, grid=(1,), in_specs=SCALARS + [tile(0),...  1.84 us
  transfers between devices with their start and end apart: 4, of which 2 were waited for; matrix products, arithmetic and copies ran while one was open for 0% of the time, Pallas kernels for 0%

profile of v1, /device:TPU:1, one launch (start us, length us, event | category | flops | bytes accessed | tf_op | source)
XLA Modules:
  0.0 48.0 jit_solution(14086002133057030782)
XLA Ops:
  1.3 0.0 copy-start
  1.3 1.3 %copy-done = bf16[4,5,32,1024]{3,2,1,0:T(8,128)(2,1)S(1)} copy-done((bf16[4,5,32,1024]{3,2,1,0:T(8,128)(2,1)S(1)}, bf16[4,5,32,1024]{3,2,1,0:T(8,128)(2,1)}, u32[]{:S(2)}) %copy-start) | copy-done | bytes 1310744
  2.6 0.0 copy-start.1
  2.6 1.0 %copy-done.1 = bf16[5,16,16,128]{3,2,1,0:T(8,128)(2,1)S(1)} copy-done((bf16[5,16,16,128]{3,2,1,0:T(8,128)(2,1)S(1)}, bf16[5,16,16,128]{3,2,1,0:T(8,128)(2,1)}, u32[]{:S(2)}) %copy-start.1) | copy-done | bytes 327704
  3.6 0.0 copy-start.2
  3.6 0.7 %copy-done.2 = s32[4,4]{1,0:T(4,128)S(1)} copy-done((s32[4,4]{1,0:T(4,128)S(1)}, s32[4,4]{1,0:T(4,128)}, u32[]{:S(2)}) %copy-start.2) | copy-done | bytes 88
  4.3 0.0 copy-start.3
  4.3 0.7 %copy-done.3 = s32[4]{0:T(128)S(1)} copy-done((s32[4]{0:T(128)S(1)}, s32[4]{0:T(128)}, u32[]{:S(2)}) %copy-start.3) | copy-done | bytes 40
  4.9 0.0 copy-start.4
  4.9 0.7 %copy-done.4 = f32[5]{0:T(128)S(1)} copy-done((f32[5]{0:T(128)S(1)}, f32[5]{0:T(128)}, u32[]{:S(2)}) %copy-start.4) | copy-done | bytes 44
  5.6 1.8 %y_messages.1 = (bf16[576,128]{1,0:T(8,128)(2,1)S(1)}, bf16[576,128]{1,0:T(8,128)(2,1)S(1)}) custom-call(s32[4]{0:T(128)S(1)} %copy-done.3, s32[1]{0:T(128)S(6)} %copy.8.cnt, s32[4,4]{1,0:T(4,128)S(1)} %copy-done.2, f32[5]{0:T(128)S(1)} %copy-done.4, bf16[4,160,1024]{2,1,0:T(8,128)(2,1)S(1)} %bitcast.4, bf16[4,160,1024]{2,1,0:T(8,128)(2,1)S(1)} %bitcast.5, ...), custom_call_target="tpu_custom_call" | custom-call | tf_op jit(solution)/shard_map/y_messages/pallas_call | solution.py:616
  7.4 8.8 %collective-permute-start = (bf16[576,128]{1,0:T(8,128)(2,1)S(1)}, bf16[576,128]{1,0:T(8,128)(2,1)S(1)}, u32[]{:S(2)}, u32[]{:S(2)}) collective-permute-start(bf16[576,128]{1,0:T(8,128)(2,1)S(1)} %get-tuple-element.8), channel_id=1, source_target_pairs={{0,1},{1,0},{2,3},{3,2},{4,5},{5,4},{6,7},{7,6},{8,9},{9,8},{10,11... | collective-permute-start | bytes 442376 | tf_op jit(solution)/shard_map/ppermute | solution.py:613
  16.2 1.9 %collective-permute-start.1 = (bf16[576,128]{1,0:T(8,128)(2,1)S(1)}, bf16[576,128]{1,0:T(8,128)(2,1)S(1)}, u32[]{:S(2)}, u32[]{:S(2)}) collective-permute-start(bf16[576,128]{1,0:T(8,128)(2,1)S(1)} %get-tuple-element.9), channel_id=1, source_target_pairs={{0,31},{1,2},{2,1},{3,4},{4,3},{5,6},{6,5},{7,8},{8,7},{9,10},{10,... | collective-permute-start | bytes 442376 | tf_op jit(solution)/shard_map/ppermute | solution.py:613
  18.1 0.0 collective-permute-done.y_near
  18.1 7.8 %collective-permute-done.1.y_far = bf16[576,128]{1,0:T(8,128)(2,1)S(1)} collective-permute-done((bf16[576,128]{1,0:T(8,128)(2,1)S(1)}, bf16[576,128]{1,0:T(8,128)(2,1)S(1)}, u32[]{:S(2)}, u32[]{:S(2)}) %collective-permute-start.1) | collective-permute-done | bytes 147488 | tf_op jit(solution)/shard_map/ppermute | solution.py:613
  25.9 2.9 %z_messages.1 = (bf16[288,128]{1,0:T(8,128)(2,1)S(1)}, bf16[288,128]{1,0:T(8,128)(2,1)S(1)}) custom-call(s32[4]{0:T(128)S(1)} %copy-done.3, s32[1]{0:T(128)S(6)} %copy.8.cnt, s32[4,4]{1,0:T(4,128)S(1)} %copy-done.2, f32[5]{0:T(128)S(1)} %copy-done.4, bf16[4,160,1024]{2,1,0:T(8,128)(2,1)S(1)} %bitcast.6, bf16[1280,128]{1,0:T(8,128)(2,1)S(1)} %bitcast.9, ...), custom_call_target="tpu_custom_call" | custom-call | tf_op jit(solution)/shard_map/z_messages/pallas_call | solution.py:629
  28.8 1.9 %collective-permute-start.2 = (bf16[288,128]{1,0:T(8,128)(2,1)S(1)}, bf16[288,128]{1,0:T(8,128)(2,1)S(1)}, u32[]{:S(2)}, u32[]{:S(2)}) collective-permute-start(bf16[288,128]{1,0:T(8,128)(2,1)S(1)} %get-tuple-element.10), channel_id=1, source_target_pairs={{0,32},{32,0},{64,96},{96,64},{128,160},{160,128},{192,224},{224,1... | collective-permute-start | bytes 221192 | tf_op jit(solution)/shard_map/ppermute | solution.py:613
  30.7 6.2 %collective-permute-start.3 = (bf16[288,128]{1,0:T(8,128)(2,1)S(1)}, bf16[288,128]{1,0:T(8,128)(2,1)S(1)}, u32[]{:S(2)}, u32[]{:S(2)}) collective-permute-start(bf16[288,128]{1,0:T(8,128)(2,1)S(1)} %get-tuple-element.11), channel_id=1, source_target_pairs={{0,480},{32,64},{64,32},{96,128},{128,96},{160,192},{192,160},{224... | collective-permute-start | bytes 221192 | tf_op jit(solution)/shard_map/ppermute | solution.py:613
  36.9 0.0 collective-permute-done.2.z_near
  36.9 1.7 %collective-permute-done.3.z_far = bf16[288,128]{1,0:T(8,128)(2,1)S(1)} collective-permute-done((bf16[288,128]{1,0:T(8,128)(2,1)S(1)}, bf16[288,128]{1,0:T(8,128)(2,1)S(1)}, u32[]{:S(2)}, u32[]{:S(2)}) %collective-permute-start.3) | collective-permute-done | bytes 73760 | tf_op jit(solution)/shard_map/ppermute | solution.py:613
  38.7 9.4 %advance.1 = (bf16[1280,128]{1,0:T(8,128)(2,1)}, bf16[4,160,1024]{2,1,0:T(8,128)(2,1)}) custom-call(s32[4]{0:T(128)S(1)} %copy-done.3, s32[1]{0:T(128)S(6)} %copy.8.cnt, s32[4,4]{1,0:T(4,128)S(1)} %copy-done.2, f32[5]{0:T(128)S(1)} %copy-done.4, bf16[4,160,1024]{2,1,0:T(8,128)(2,1)S(1)} %bitcast.7, bf16[1280,128]{1,0:T(8,128)(2,1)S(1)} %bitcast.10, ...), custom_call_target="tpu_custom_call" | custom-call | tf_op jit(solution)/shard_map/advance/pallas_call | solution.py:644
Async XLA Ops:
  1.3 1.3 %copy-start = (bf16[4,5,32,1024]{3,2,1,0:T(8,128)(2,1)S(1)}, bf16[4,5,32,1024]{3,2,1,0:T(8,128)(2,1)}, u32[]{:S(2)}) copy-start(bf16[4,5,32,1024]{3,2,1,0:T(8,128)(2,1)} %param.7) | copy-start | bytes 3932164
  2.6 1.0 %copy-start.1 = (bf16[5,16,16,128]{3,2,1,0:T(8,128)(2,1)S(1)}, bf16[5,16,16,128]{3,2,1,0:T(8,128)(2,1)}, u32[]{:S(2)}) copy-start(bf16[5,16,16,128]{3,2,1,0:T(8,128)(2,1)} %param.6) | copy-start | bytes 983044
  3.6 0.7 %copy-start.2 = (s32[4,4]{1,0:T(4,128)S(1)}, s32[4,4]{1,0:T(4,128)}, u32[]{:S(2)}) copy-start(s32[4,4]{1,0:T(4,128)} %nbr.5) | copy-start | bytes 196
  4.3 0.7 %copy-start.3 = (s32[4]{0:T(128)S(1)}, s32[4]{0:T(128)}, u32[]{:S(2)}) copy-start(s32[4]{0:T(128)} %col.5) | copy-start | bytes 52
  4.9 0.7 %copy-start.4 = (f32[5]{0:T(128)S(1)}, f32[5]{0:T(128)}, u32[]{:S(2)}) copy-start(f32[5]{0:T(128)} %rate.5) | copy-start | bytes 64
  7.4 10.7 %collective-permute-start = (bf16[576,128]{1,0:T(8,128)(2,1)S(1)}, bf16[576,128]{1,0:T(8,128)(2,1)S(1)}, u32[]{:S(2)}, u32[]{:S(2)}) collective-permute-start(bf16[576,128]{1,0:T(8,128)(2,1)S(1)} %get-tuple-element.8), channel_id=1, source_target_pairs={{0,1},{1,0},{2,3},{3,2},{4,5},{5,4},{6,7},{7,6},{8,9},{9,8},{10,11... | collective-permute-start | bytes 442376 | tf_op jit(solution)/shard_map/ppermute | solution.py:613
  16.2 9.7 %collective-permute-start.1 = (bf16[576,128]{1,0:T(8,128)(2,1)S(1)}, bf16[576,128]{1,0:T(8,128)(2,1)S(1)}, u32[]{:S(2)}, u32[]{:S(2)}) collective-permute-start(bf16[576,128]{1,0:T(8,128)(2,1)S(1)} %get-tuple-element.9), channel_id=1, source_target_pairs={{0,31},{1,2},{2,1},{3,4},{4,3},{5,6},{6,5},{7,8},{8,7},{9,10},{10,... | collective-permute-start | bytes 442376 | tf_op jit(solution)/shard_map/ppermute | solution.py:613
  28.8 8.2 %collective-permute-start.2 = (bf16[288,128]{1,0:T(8,128)(2,1)S(1)}, bf16[288,128]{1,0:T(8,128)(2,1)S(1)}, u32[]{:S(2)}, u32[]{:S(2)}) collective-permute-start(bf16[288,128]{1,0:T(8,128)(2,1)S(1)} %get-tuple-element.10), channel_id=1, source_target_pairs={{0,32},{32,0},{64,96},{96,64},{128,160},{160,128},{192,224},{224,1... | collective-permute-start | bytes 221192 | tf_op jit(solution)/shard_map/ppermute | solution.py:613
  30.7 8.0 %collective-permute-start.3 = (bf16[288,128]{1,0:T(8,128)(2,1)S(1)}, bf16[288,128]{1,0:T(8,128)(2,1)S(1)}, u32[]{:S(2)}, u32[]{:S(2)}) collective-permute-start(bf16[288,128]{1,0:T(8,128)(2,1)S(1)} %get-tuple-element.11), channel_id=1, source_target_pairs={{0,480},{32,64},{64,32},{96,128},{128,96},{160,192},{192,160},{224... | collective-permute-start | bytes 221192 | tf_op jit(solution)/shard_map/ppermute | solution.py:613

commit v2 on v1

v2 whole, which is shorter than its diff:
```python
import functools

import jax
import jax.numpy as jnp
import numpy as np
from jax import lax
from jax.experimental import pallas as pl
from jax.experimental.pallas import tpu as pltpu
from jax.sharding import PartitionSpec as P

F32, BF16 = jnp.float32, jnp.bfloat16
SLOTS, COMPS, EDGE, HALF, LANES = 4, 5, 32, 16, 128
ROWS = COMPS * EDGE
CROWS = COMPS * HALF
CELLS = CROWS * HALF
PLANE = EDGE * EDGE
QUAD = 256

Y_NEAR, Y_NEXT, Y_ROW, Y_HALF, Y_FLUX, Y_COVER = 0, 80, 160, 320, 480, 560
Y_ROWS = 576
Z_NEAR, Z_NEXT, Z_FLUX, Z_LOW, Z_HIGH, Z_COVER = 0, 80, 160, 240, 256, 272
Z_ROWS = 288


def iota(shape, dim):
    return lax.broadcasted_iota(jnp.int32, shape, dim)


def ones_at(mask):
    return jnp.where(mask, 1.0, 0.0).astype(BF16)


def mm(left, right):
    return lax.dot_general(left, right, (((1,), (0,)), ((), ())), preferred_element_type=F32)


def chain(index, values):
    out = jnp.full(index.shape, values[-1], values[-1].dtype)
    for k in range(len(values) - 2, -1, -1):
        out = jnp.where(index == k, values[k], out)
    return out


class Tables:
    def __init__(self, col, cnt, nbr, rate):
        self.start = [col[s] * HALF for s in range(SLOTS)]
        self.used = [jnp.where(s < cnt[0], 1, 0) for s in range(SLOTS)]
        self.near = [[nbr[s, f] for s in range(SLOTS)] for f in range(4)]
        self.rate = [rate[c] for c in range(COMPS)]

    def rates(self, rows, per):
        return chain(iota((rows, LANES), 0) // per, self.rate)

    def packed(self, dim):
        n, x = iota((LANES, LANES), dim), iota((LANES, LANES), 1 - dim)
        return n // EDGE, n % EDGE, x

    def to_coarse(self, face):
        s, e, x = self.packed(0)
        hit = (x == chain(s, self.start) + e // 2) & (chain(s, self.used) > 0)
        if face is not None:
            hit = hit & (chain(s, self.near[face]) < 0)
        return ones_at(hit)

    def from_coarse(self, face, unlinked):
        s, e, x = self.packed(1)
        hit = x == chain(s, self.start) + e // 2
        if unlinked:
            hit = hit & (chain(s, self.near[face]) < 0)
        return ones_at(hit)

    def linked_lanes(self, face):
        s, e, n = self.packed(1)
        return ones_at(n == chain(s, self.near[face]) * EDGE + jnp.where(chain(s, self.near[face]) < 0, -LANES, e))

    def row_stencil(self):
        s, e, n = self.packed(1)
        low, high, x0 = chain(s, self.near[0]), chain(s, self.near[1]), chain(s, self.start)
        inside = (n // EDGE == s) & ((n % EDGE == e - 1) | (n % EDGE == e + 1))
        at_low = (e == 0) & (low >= 0) & (n == low * EDGE + EDGE - 1)
        at_high = (e == EDGE - 1) & (high >= 0) & (n == high * EDGE)
        left = (e == 0) & (low < 0) & (n == (x0 - 1) % LANES)
        right = (e == EDGE - 1) & (high < 0) & (n == (x0 + HALF) % LANES)
        return jnp.concatenate([ones_at(inside | at_low | at_high), ones_at(left | right)], axis=0)

    def side_pick(self):
        n, x = iota((LANES, LANES), 1), iota((LANES, LANES), 0)
        s, high = n // EDGE, n % EDGE >= HALF
        x0 = chain(s, self.start)
        spot = jnp.where(high, (x0 + HALF) % LANES, (x0 - 1) % LANES)
        open_face = jnp.where(high, chain(s, self.near[1]), chain(s, self.near[0])) < 0
        return ones_at((x == spot) & open_face)

    def pool_spread(self, mode):
        m, x = iota((SLOTS * LANES, LANES), 0), iota((SLOTS * LANES, LANES), 1)
        s, lane = m // LANES, m % LANES
        e, x0 = lane % EDGE, chain(s, self.start)
        if mode == 0:
            target = jnp.where(chain(s, self.used) > 0, x0 + e // 2, -1)
        else:
            low = [jnp.where((self.used[k] > 0) & (self.near[0][k] < 0), (self.start[k] - 1) % LANES, -1) for k in range(SLOTS)]
            high = [jnp.where((self.used[k] > 0) & (self.near[1][k] < 0), (self.start[k] + HALF) % LANES, -1) for k in range(SLOTS)]
            target = jnp.where(e == 0, chain(s, low), jnp.where(e == EDGE - 1, chain(s, high), -1))
        first = lane < 2 * EDGE
        hit = x == target
        return jnp.concatenate([ones_at(hit & first), ones_at(hit & jnp.logical_not(first))], axis=1)


def copies(rows, per):
    out, src = iota((rows, rows // per), 0), iota((rows, rows // per), 1)
    return ones_at(out // per == src)


def pair_rows():
    out, src = iota((CROWS, ROWS), 0), iota((CROWS, ROWS), 1)
    return ones_at(src // 2 == out)


def z_stencil():
    out, src = iota((ROWS, ROWS), 0), iota((ROWS, ROWS), 1)
    same = out // EDGE == src // EDGE
    beside = same & ((src == out + 1) | (src == out - 1))
    return jnp.where(src == out, -6.0, jnp.where(beside, 1.0, 0.0)).astype(BF16)


def grid_of(rows, columns):
    return np.indices((rows, columns))


def plane_stencil():
    m, n = grid_of(3 * QUAD, QUAD)
    e = n % EDGE
    own = (m < QUAD) & (
        ((m == n - 1) & (e > 0)) | ((m == n + 1) & (e < EDGE - 1)) | (m == n - EDGE) | (m == n + EDGE)
    )
    before = (m >= QUAD) & (m < QUAD + LANES) & (m - QUAD - LANES == n - EDGE)
    after = (m >= QUAD + LANES) & (m < 2 * QUAD) & (m - QUAD - LANES + QUAD == n + EDGE)
    p = m - 2 * QUAD
    partner = (m >= 2 * QUAD) & (
        ((e == 0) & (p == n + EDGE - 1)) | ((e == EDGE - 1) & (p == n - EDGE + 1))
    )
    return own | before | after | partner


def side_place(q):
    m, n = grid_of(LANES, QUAD)
    y, e = (n // EDGE + q * (QUAD // EDGE)) // 2, n % EDGE
    return (m < EDGE) & (m % HALF == y) & (e == np.where(m < HALF, 0, EDGE - 1))


def plane_weights():
    return np.concatenate([plane_stencil()] + [side_place(q) for q in range(4)]).astype(BF16)


def side_rows():
    out, src = grid_of(ROWS, CELLS)
    return (out // 2 == src // HALF).astype(BF16)


def partner_columns(load, tables, rows):
    lane = iota((rows, PLANE), 1) % EDGE
    at_low = jnp.where(lane == EDGE - 1, 1.0, 0.0).astype(BF16)
    at_high = jnp.where(lane == 0, 1.0, 0.0).astype(BF16)
    out = []
    for s in range(SLOTS):
        low, high = tables.near[0][s], tables.near[1][s]
        has_low = jnp.where(low >= 0, 1.0, 0.0).astype(BF16)
        has_high = jnp.where(high >= 0, 1.0, 0.0).astype(BF16)
        out.append(
            load(jnp.maximum(low, 0)) * (at_low * has_low) + load(jnp.maximum(high, 0)) * (at_high * has_high)
        )
    return out


def plane_terms(fields, partners, sides, q, weights):
    lo, hi = QUAD * q, QUAD * (q + 1)
    parts = []
    for s in range(SLOTS):
        field = fields[s]
        rows = field.shape[0]
        none = jnp.zeros((rows, LANES), BF16)
        parts.append(
            jnp.concatenate(
                [
                    field[:, lo:hi],
                    field[:, lo - LANES : lo] if q else none,
                    field[:, hi : hi + LANES] if q < 3 else none,
                    partners[s][:, lo:hi],
                    sides[s],
                ],
                axis=1,
            )
        )
    place = 3 * QUAD + LANES * q
    table = jnp.concatenate([weights[: 3 * QUAD, :], weights[place : place + LANES, :]], axis=0)
    return mm(jnp.concatenate(parts, axis=0), table)


def slot_sides(sides):
    return [sides if s == 0 else pltpu.roll(sides, LANES - EDGE * s, 1) for s in range(SLOTS)]


def edge_lanes(ghost, s, top):
    shift = (LANES - EDGE * (s + 1 if top else s)) % LANES
    moved = pltpu.roll(ghost, shift, 1) if shift else ghost
    lane = iota(ghost.shape, 1)
    kept = jnp.where(lane >= LANES - EDGE if top else lane < EDGE, moved, 0.0)
    none = jnp.zeros(ghost.shape, F32)
    return jnp.concatenate([none, kept] if top else [kept, none], axis=1)


def y_message_kernel(
    col_hbm, cnt_hbm, nbr_hbm, rate_hbm, fine_hbm, coarse_hbm, near_ref, far_ref,
    col, cnt, nbr, rate, low_ref, high_ref, coarse_ref, level, packs, rows_z, sems,
):
    fetches = [
        pltpu.make_async_copy(source, target, sems.at[i])
        for i, (source, target) in enumerate(
            (
                (col_hbm, col),
                (cnt_hbm, cnt),
                (nbr_hbm, nbr),
                (rate_hbm, rate),
                (coarse_hbm, coarse_ref),
                (fine_hbm.at[:, :, 0:LANES], low_ref),
                (fine_hbm.at[:, :, PLANE - LANES : PLANE], high_ref),
            )
        )
    ]
    for fetch in fetches:
        fetch.start()
    m, n = iota((SLOTS * LANES, QUAD), 0), iota((SLOTS * LANES, QUAD), 1)
    for i, (edge, inner) in enumerate(((0, EDGE), (LANES - EDGE, LANES - 2 * EDGE))):
        packs[i] = ones_at(
            (m // LANES == n % LANES // EDGE) & (m % LANES == n % EDGE + jnp.where(n < LANES, edge, inner))
        )
    rows_z[...] = z_stencil()
    for fetch in fetches:
        fetch.wait()
    tables = Tables(col, cnt, nbr, rate)
    level[...] = coarse_ref[...].astype(F32)
    rates = tables.rates(ROWS, EDGE)
    coarse_rates = tables.rates(CROWS, HALF)
    stencil, double, pairs = tables.row_stencil(), copies(ROWS, 2), pair_rows()
    messages = []
    for top in (True, False):
        tile = high_ref if top else low_ref
        both = mm(jnp.concatenate([tile[s] for s in range(SLOTS)], axis=1), packs[int(top)])
        row = both[:, :LANES].astype(BF16)
        near = level[pl.ds(HALF - 1 if top else 0, CROWS, stride=HALF), :]
        following = level[pl.ds(HALF - 2 if top else 1, CROWS, stride=HALF), :]
        near_fine = mm(double, near.astype(BF16)).astype(BF16)
        around = mm(jnp.concatenate([row, near_fine], axis=1), stencil) + mm(rows_z[...], row) + both[:, LANES:]
        half = (both[:, :LANES] + 2.0 * rates * around).astype(BF16)
        place = tables.to_coarse(3 if top else 2)
        sums = mm(pairs, jnp.concatenate([row, half], axis=1)).astype(BF16)
        cover = jnp.minimum(mm(jnp.ones((HALF, LANES), BF16), place), 1.0)
        flux = 0.25 * coarse_rates * mm(sums, jnp.concatenate([place, place], axis=0))
        flux = flux - coarse_rates * near * cover[:1]
        messages.append(
            (
                (Y_NEAR, near.astype(BF16)),
                (Y_NEXT, following.astype(BF16)),
                (Y_ROW, row),
                (Y_HALF, half),
                (Y_FLUX, flux.astype(BF16)),
                (Y_COVER, cover.astype(BF16)),
            )
        )
    store_by_parity("fine", near_ref, far_ref, *messages)


def sort_arrivals(axis, near_ref, far_ref, arrived):
    even = lax.axis_index(axis) % 2 == 0

    @pl.when(even)
    def _():
        arrived[0] = far_ref[...]
        arrived[1] = near_ref[...]

    @pl.when(jnp.logical_not(even))
    def _():
        arrived[0] = near_ref[...]
        arrived[1] = far_ref[...]


PLANES = 16


def plane_rows(per, scale_inner):
    rows = COMPS * per
    out, src = iota((PLANES, rows), 0), iota((PLANES, rows), 1)
    c, last = out % 8, out >= 8
    edge = src == jnp.where(last, c * per + per - 1, c * per)
    real = c < COMPS
    if not scale_inner:
        return ones_at(edge & real)
    inner = src == jnp.where(last, c * per + per - 2, c * per + 1)
    return jnp.where(edge & real, -6.0, jnp.where(inner & real, 1.0, 0.0)).astype(BF16)


def store_by_parity(axis, near_ref, far_ref, up, down):
    even = lax.axis_index(axis) % 2 == 0

    @pl.when(even)
    def _():
        for at, value in up:
            near_ref[at : at + value.shape[0], :] = value
        for at, value in down:
            far_ref[at : at + value.shape[0], :] = value

    @pl.when(jnp.logical_not(even))
    def _():
        for at, value in down:
            near_ref[at : at + value.shape[0], :] = value
        for at, value in up:
            far_ref[at : at + value.shape[0], :] = value


def coarse_planes(coarse_ref, zs):
    return jnp.concatenate(
        [coarse_ref[pl.ds((c * HALF + z) * HALF, HALF), :] for z in zs for c in range(COMPS)], axis=0
    )


def interior_kernel(
    col, cnt, nbr, rate, fine_ref, coarse_ref, weights, side_sum, half_ref, edges_ref, planes_ref, flux_ref, place_ref,
    flux, summed, split,
):
    tables = Tables(col, cnt, nbr, rate)
    m, n = iota((CELLS, LANES), 0), iota((CELLS, LANES), 1)
    picked = jnp.where(m % HALF == n % HALF, mm(coarse_ref[...], tables.side_pick()), 0.0).astype(BF16)
    sides = [part.astype(BF16) for part in slot_sides(mm(side_sum[...], picked))]
    fields = [fine_ref[s] for s in range(SLOTS)]
    partners = partner_columns(lambda t: fine_ref[t], tables, ROWS)
    rows_z = z_stencil()
    rates = tables.rates(ROWS, EDGE)
    rates2 = 2.0 * jnp.concatenate([rates, rates], axis=1)
    place_ref[...] = tables.pool_spread(0)
    summed[...] = jnp.zeros(summed.shape, F32)
    planes_ref[...] = jnp.zeros(planes_ref.shape, F32)
    for q in range(4):
        lanes = slice(QUAD * q, QUAD * (q + 1))
        terms = plane_terms(fields, partners, sides, q, weights)
        for s in range(SLOTS):
            field = fields[s][:, lanes]
            start = field.astype(F32)
            value = start + rates2 * (terms[ROWS * s : ROWS * (s + 1)] + mm(rows_z, field))
            half_ref[s, :, lanes] = value.astype(BF16)
            if q == 0:
                edges_ref[s, :, :LANES] = value[:, :LANES]
            if q == 3:
                edges_ref[s, :, LANES:] = value[:, LANES:]
            both = value + start
            for h in range(2):
                part = slice(LANES * h, LANES * (h + 1))
                at = slice(QUAD * q + LANES * h, QUAD * q + LANES * (h + 1))
                split[2 * h] = value[:, part]
                split[2 * h + 1] = both[:, part]
                for p in range(2):
                    first = (EDGE - 1) * p
                    planes_ref[s, 8 * p : 8 * p + COMPS, at] = split[2 * h, pl.ds(first, COMPS, stride=EDGE), :]
                    row = PLANES * (2 * q + h) + 8 * p
                    summed[row : row + COMPS, LANES * s : LANES * (s + 1)] = (
                        split[2 * h + 1, pl.ds(first, COMPS, stride=EDGE), :]
                    )
    cells = mm(summed[...].astype(BF16), place_ref[...])
    for k in range(8):
        part = cells[PLANES * k : PLANES * (k + 1)]
        flux[pl.ds(2 * k, PLANES, stride=HALF), :] = part[:, :LANES]
        flux[pl.ds(2 * k + 1, PLANES, stride=HALF), :] = part[:, LANES:]
    cover = jnp.minimum(mm(jnp.ones((HALF, LANES), BF16), tables.to_coarse(None)), 1.0)
    coarse_rates = tables.rates(CROWS, HALF)
    for p in range(2):
        near = coarse_planes(coarse_ref, ((HALF - 1) * p,)).astype(F32)
        total = 0.25 * coarse_rates * flux[8 * HALF * p : 8 * HALF * p + CROWS, :]
        flux_ref[CROWS * p : CROWS * (p + 1), :] = total - coarse_rates * near * cover[:1]


def z_message_kernel(col, cnt, nbr, rate, coarse_ref, flux_in, y_near, y_far, near_ref, far_ref, arrived, flux):
    tables = Tables(col, cnt, nbr, rate)
    sort_arrivals("fine", y_near, y_far, arrived)
    flux[...] = flux_in[...]
    fine_pick, coarse_pick = plane_rows(EDGE, False), plane_rows(HALF, False)
    place = tables.to_coarse(None)
    rates = chain(iota((PLANES, LANES), 0) % 8, tables.rate + [jnp.zeros((), F32)] * 3)
    corners = []
    for k, face in ((0, 2), (1, 3)):
        row = mm(fine_pick, arrived[k, Y_ROW : Y_ROW + ROWS, :]).astype(BF16)
        corner = mm(coarse_pick, arrived[k, Y_NEAR : Y_NEAR + CROWS, :]).astype(BF16)
        corners.append(corner)
        ghost = mm(
            jnp.concatenate([row, corner], axis=1),
            jnp.concatenate([tables.linked_lanes(face), tables.from_coarse(face, True)], axis=0),
        )
        gain = (0.5 * rates * rates) * mm(ghost.astype(BF16), place)
        for p in range(2):
            at = pl.ds(CROWS * p + (HALF - 1) * k, COMPS, stride=HALF)
            flux[at, :] = flux[at, :] + gain[8 * p : 8 * p + COMPS]
    cover = jnp.minimum(mm(jnp.ones((HALF, LANES), BF16), place), 1.0).astype(BF16)
    messages = []
    for top in (True, False):
        near, following = (HALF - 1, HALF - 2) if top else (0, 1)
        messages.append(
            (
                (Z_NEAR, coarse_planes(coarse_ref, (near,))),
                (Z_NEXT, coarse_planes(coarse_ref, (following,))),
                (Z_FLUX, flux[CROWS * top : CROWS * (top + 1), :].astype(BF16)),
                (Z_LOW, corners[0]),
                (Z_HIGH, corners[1]),
                (Z_COVER, cover),
            )
        )
    store_by_parity("own", near_ref, far_ref, *messages)


SPAN = 32
DEEP = HALF + 2


def at_cell(c, z, y):
    return (c * DEEP + z + 1) * SPAN + 8 + y


def mixed(centre, total, r):
    total = total + pltpu.roll(centre, 1, 1) + pltpu.roll(centre, LANES - 1, 1)
    return centre + (0.5 * r) * (total - 6.0 * centre)


def own_mean(old, mean, tables, zs):
    for c in range(COMPS):
        for z in zs:
            total = (
                old[pl.ds(at_cell(c, z, -1), HALF), :]
                + old[pl.ds(at_cell(c, z, 1), HALF), :]
                + old[pl.ds(at_cell(c, z - 1, 0), HALF), :]
                + old[pl.ds(at_cell(c, z + 1, 0), HALF), :]
            )
            mean[pl.ds(at_cell(c, z, 0), HALF), :] = mixed(
                old[pl.ds(at_cell(c, z, 0), HALF), :], total, tables.rate[c]
            )


def strip_mean(old, mean, y_arr, tables):
    for c in range(COMPS):
        for k, y, inside in ((0, -1, 0), (1, HALF, HALF - 1)):
            at = Y_NEXT + c * HALF
            total = (
                y_arr[k, at : at + HALF, :].astype(F32)
                + old[pl.ds(at_cell(c, 0, inside), HALF, stride=SPAN), :]
                + old[pl.ds(at_cell(c, -1, y), HALF, stride=SPAN), :]
                + old[pl.ds(at_cell(c, 1, y), HALF, stride=SPAN), :]
            )
            mean[pl.ds(at_cell(c, 0, y), HALF, stride=SPAN), :] = mixed(
                old[pl.ds(at_cell(c, 0, y), HALF, stride=SPAN), :], total, tables.rate[c]
            )


def fill_old(old, coarse_ref, y_arr, zs):
    for c in range(COMPS):
        for z in zs:
            old[pl.ds(at_cell(c, z, 0), HALF), :] = coarse_ref[pl.ds((c * HALF + z) * HALF, HALF), :].astype(F32)
        for k, y in ((0, -1), (1, HALF)):
            at = Y_NEAR + c * HALF
            old[pl.ds(at_cell(c, 0, y), HALF, stride=SPAN), :] = y_arr[k, at : at + HALF, :].astype(F32)


def neighbour_rows(fine_ref, k):
    m, n = iota((SLOTS * LANES, LANES), 0), iota((SLOTS * LANES, LANES), 1)
    edge = LANES - EDGE if k else 0
    pack = ones_at((m // LANES == n // EDGE) & (m % LANES == n % EDGE + edge))
    tile = PLANE - LANES if k else 0
    return mm(jnp.concatenate([fine_ref[s, :, tile : tile + LANES] for s in range(SLOTS)], axis=1), pack)


class CoarseLanes:
    def __init__(self, tables, y_arr):
        x = iota((HALF, LANES), 1)
        covered, left, right = x < 0, x < 0, x < 0
        for s in range(SLOTS):
            x0, used = tables.start[s], tables.used[s] > 0
            covered = covered | ((x >= x0) & (x < x0 + HALF) & used)
            left = left | ((x == (x0 - 1) % LANES) & used & (tables.near[0][s] < 0))
            right = right | ((x == (x0 + HALF) % LANES) & used & (tables.near[1][s] < 0))
        self.covered = covered
        self.left, self.right = jnp.where(left, 1.0, 0.0), jnp.where(right, 1.0, 0.0)
        self.sides = self.left + self.right
        self.beside = [y_arr[k, Y_COVER : Y_COVER + HALF, :].astype(F32)[:1] for k in (0, 1)]

    def update(self, r, level0, level1, average, change):
        low, high = pltpu.roll(level0, LANES - 1, 1), pltpu.roll(level0, 1, 1)
        change = change - r * (self.sides * level1 + self.left * low + self.right * high)
        return jnp.where(self.covered, 0.125 * average, 2.0 * level1 - level0 + change).astype(BF16)

    def beyond_y(self, k, r, level0, level1, flux, corner):
        gain = (2.0 * r * r) * level0 - r * level1
        if corner is not None:
            gain = gain + (r * r) * corner
        return flux + self.beside[k] * gain


def middle_kernel(early, *refs):
    is_early = lax.axis_index("own") == 0

    @pl.when(is_early if early else jnp.logical_not(is_early))
    def _():
        middle_body(*(refs if early else refs[:14] + refs[20:]))

    if not early:

        @pl.when(is_early)
        def _():
            for done, out in zip(refs[14:20], refs[20:26]):
                out[...] = done[...]


def middle_body(
    col, cnt, nbr, rate, fine_ref, coarse_ref, y_near, y_far, half_in, edges_ref, planes_in, weights, side_sum, place_ref,
    coarse_out, fine_out, rows_ref, planes_ref, theirs_ref, faces_ref,
    half, y_arr, old, mean, split, average, outside, pairs,
):
    tables = Tables(col, cnt, nbr, rate)
    sort_arrivals("fine", y_near, y_far, y_arr)
    fill_old(old, coarse_ref, y_arr, range(HALF))
    for c in range(COMPS):
        for z in (-1, HALF):
            old[pl.ds(at_cell(c, z, 0) - 8, SPAN), :] = jnp.zeros((SPAN, LANES), F32)
    own_mean(old, mean, tables, range(HALF))
    strip_mean(old, mean, y_arr, tables)
    rates = tables.rates(ROWS, EDGE)
    rates2 = 2.0 * jnp.concatenate([rates, rates], axis=1)
    double, rows_z = copies(ROWS, 2), z_stencil()
    cells = jnp.concatenate(
        [mean[pl.ds(at_cell(c, z, 0), HALF), :] for c in range(COMPS) for z in range(HALF)], axis=0
    ).astype(BF16)
    m, n = iota((CELLS, LANES), 0), iota((CELLS, LANES), 1)
    picked = jnp.where(m % HALF == n % HALF, mm(cells, tables.side_pick()), 0.0).astype(BF16)
    sides = [part.astype(BF16) for part in slot_sides(mm(side_sum[...], picked))]

    def level_row(level, y):
        rows = [level[pl.ds(at_cell(c, 0, y), HALF, stride=SPAN), :] for c in range(COMPS)]
        return mm(double, jnp.concatenate(rows, axis=0).astype(BF16)).astype(BF16)

    half[...] = half_in[...]
    planes_ref[...] = planes_in[...]
    second = []
    plane_rates = chain(iota((PLANES, LANES), 0) % 8, tables.rate + [jnp.zeros((), F32)] * 3)
    for k, y in ((0, -1), (1, HALF)):
        linked, opened = tables.linked_lanes(2 + k), tables.from_coarse(2 + k, True)
        row = y_arr[k, Y_ROW : Y_ROW + ROWS, :]
        ghost = mm(jnp.concatenate([row, level_row(old, y)], axis=1), jnp.concatenate([linked, opened], axis=0))
        plane_ghost = mm(plane_rows(EDGE, False), ghost.astype(BF16))
        tile = slice(PLANE - LANES, PLANE) if k else slice(0, LANES)
        part = slice(LANES * k, LANES * (k + 1))
        for s in range(SLOTS):
            add = edge_lanes(ghost, s, bool(k))[:, part]
            half[s, :, tile] = (edges_ref[s, :, part] + 2.0 * rates * add).astype(BF16)
            add = edge_lanes(plane_ghost, s, bool(k))[:, part]
            planes_ref[s, :, tile] = planes_ref[s, :, tile] + 2.0 * plane_rates * add
        theirs = mm(y_arr[k, Y_HALF : Y_HALF + ROWS, :], linked) + 2.0 * rates * neighbour_rows(fine_ref, k)
        theirs_ref[k] = theirs
        theirs = theirs.astype(BF16).astype(F32)
        is_linked = chain(iota((ROWS, LANES), 1) // EDGE, tables.near[2 + k]) >= 0
        second.append(jnp.where(is_linked, theirs, mm(level_row(mean, y), opened)))

    rows_ref[...] = jnp.zeros(rows_ref.shape, F32)
    fields = [half[s] for s in range(SLOTS)]
    partners = partner_columns(lambda t: half[t], tables, ROWS)
    for q in range(4):
        lanes = slice(QUAD * q, QUAD * (q + 1))
        terms = plane_terms(fields, partners, sides, q, weights)
        for s in range(SLOTS):
            field = fields[s][:, lanes]
            around = terms[ROWS * s : ROWS * (s + 1)] + mm(rows_z, field)
            if q == 0:
                around = around + edge_lanes(second[0], s, False)
            if q == 3:
                around = around + edge_lanes(second[1], s, True)
            start = field.astype(F32)
            for h in range(2):
                split[h, :ROWS, :] = start[:, LANES * h : LANES * (h + 1)]
                split[h, ROWS : 2 * ROWS, :] = (
                    split[h, :ROWS, :] + fine_ref[s, :, QUAD * q + LANES * h : QUAD * q + LANES * (h + 1)].astype(F32)
                )
                pairs[2 * q + h, :, LANES * s : LANES * (s + 1)] = (
                    split[h, pl.ds(ROWS, CROWS, stride=2), :] + split[h, pl.ds(ROWS + 1, CROWS, stride=2), :]
                ).astype(BF16)
                at = slice(QUAD * q + LANES * h, QUAD * q + LANES * (h + 1))
                for w, first in enumerate((1, 2, EDGE - 3, EDGE - 2)):
                    rows_ref[s, 8 * w : 8 * w + COMPS, at] = split[h, pl.ds(first, COMPS, stride=EDGE), :]
            value = jnp.where(tables.used[s] > 0, start + rates2 * around, 0.0)
            fine_out[s, :, lanes] = value.astype(BF16)

    faces = mm(pairs[...].reshape(8 * CROWS, SLOTS * LANES), tables.pool_spread(1))
    tall = jnp.concatenate(
        [
            jnp.concatenate([fine_out[s, :, LANES * k : LANES * (k + 1)] for s in range(SLOTS)], axis=1)
            for k in range(8)
        ],
        axis=0,
    )
    cells = mm(tall, place_ref[...])
    coarse_rates = tables.rates(CROWS, HALF)
    scale = 0.25 * coarse_rates
    for j in range(2):
        lanes = slice(LANES * j, LANES * (j + 1))
        split[j] = cells[:, lanes]
        for k in range(8):
            at = pl.ds(2 * k + j, CROWS, stride=HALF)
            outside[at, :] = scale * faces[CROWS * k : CROWS * (k + 1), lanes]
            average[at, :] = (
                split[j, pl.ds(ROWS * k, CROWS, stride=2), :] + split[j, pl.ds(ROWS * k + 1, CROWS, stride=2), :]
            )
    for c in range(COMPS):
        for p in range(2):
            at = CROWS * p + HALF * c
            faces_ref[at : at + HALF, :] = outside[pl.ds((c * HALF + (HALF - 1) * p) * HALF, HALF), :]

    masks = CoarseLanes(tables, y_arr)

    def strip(level, y):
        return jnp.concatenate([level[pl.ds(at_cell(c, 0, y), HALF, stride=SPAN), :] for c in range(COMPS)], axis=0)

    for k, y in ((0, 0), (1, HALF - 1)):
        at = pl.ds(y, CROWS, stride=HALF)
        flux = y_arr[k, Y_FLUX : Y_FLUX + CROWS, :].astype(F32)
        outside[at, :] = outside[at, :] + masks.beyond_y(k, coarse_rates, strip(old, y), strip(mean, y), flux, None)
    for c in range(COMPS):
        for z in range(HALF):
            line = pl.ds((c * HALF + z) * HALF, HALF)
            if z in (0, HALF - 1):
                coarse_out[line, :] = jnp.zeros((HALF, LANES), BF16)
                continue
            coarse_out[line, :] = masks.update(
                tables.rate[c], old[pl.ds(at_cell(c, z, 0), HALF), :], mean[pl.ds(at_cell(c, z, 0), HALF), :],
                average[line, :], outside[line, :],
            )


NEAR = 32


def last_kernel(
    col, cnt, nbr, rate, coarse_ref, y_near, y_far, z_near, z_far, weights, place_ref,
    coarse_in, fine_in, rows_ref, planes_ref, theirs_ref, faces_ref,
    coarse_out, fine_hbm, y_arr, z_arr, old, mean, near, split, following, spread, ghost, level_rows, put, fine_out, sems,
):
    tables = Tables(col, cnt, nbr, rate)
    sort_arrivals("fine", y_near, y_far, y_arr)
    sort_arrivals("own", z_near, z_far, z_arr)
    fill_old(old, coarse_ref, y_arr, (0, 1, HALF - 2, HALF - 1))
    for k in (0, 1):
        following[k] = y_arr[k, Y_NEXT : Y_NEXT + CROWS, :].astype(F32)
    for c in range(COMPS):
        for k, z in ((0, -1), (1, HALF)):
            at = Z_NEAR + c * HALF
            old[pl.ds(at_cell(c, z, 0), HALF), :] = z_arr[k, at : at + HALF, :].astype(F32)
    by_comp = DEEP * SPAN
    for k, z in ((0, -1), (1, HALF)):
        first = 0 if k else 8
        low = z_arr[k, Z_LOW : Z_LOW + HALF, :].astype(F32)
        high = z_arr[k, Z_HIGH : Z_HIGH + HALF, :].astype(F32)
        old[pl.ds(at_cell(0, z, -1), COMPS, stride=by_comp), :] = low[first : first + COMPS]
        old[pl.ds(at_cell(0, z, HALF), COMPS, stride=by_comp), :] = high[first : first + COMPS]
    own_mean(old, mean, tables, (0, HALF - 1))
    comp_rates = chain(iota((COMPS, LANES), 0), tables.rate)
    level_rows[...] = jnp.zeros(level_rows.shape, F32)
    for k, y, inside in ((0, -1, 0), (1, HALF, HALF - 1)):
        for p, z in ((0, 0), (1, HALF - 1)):
            total = (
                following[k, pl.ds(z, COMPS, stride=HALF), :]
                + old[pl.ds(at_cell(0, z, inside), COMPS, stride=by_comp), :]
                + old[pl.ds(at_cell(0, z - 1, y), COMPS, stride=by_comp), :]
                + old[pl.ds(at_cell(0, z + 1, y), COMPS, stride=by_comp), :]
            )
            value = mixed(old[pl.ds(at_cell(0, z, y), COMPS, stride=by_comp), :], total, comp_rates)
            for w in (2 * p, 2 * p + 1):
                level_rows[k, 8 * w : 8 * w + COMPS, :] = value
    for c in range(COMPS):
        for k, z, inside in ((0, -1, 0), (1, HALF, HALF - 1)):
            at = Z_NEXT + c * HALF
            total = (
                z_arr[k, at : at + HALF, :].astype(F32)
                + old[pl.ds(at_cell(c, inside, 0), HALF), :]
                + old[pl.ds(at_cell(c, z, -1), HALF), :]
                + old[pl.ds(at_cell(c, z, 1), HALF), :]
            )
            mean[pl.ds(at_cell(c, z, 0), HALF), :] = mixed(
                old[pl.ds(at_cell(c, z, 0), HALF), :], total, tables.rate[c]
            )

    window = tables.from_coarse(None, False)
    n = iota((2 * CROWS, LANES), 1)

    def planes_of(level, zs):
        return jnp.concatenate([level[pl.ds(at_cell(c, z, 0), HALF), :] for z in zs for c in range(COMPS)], axis=0)

    first_y = iota((COMPS, LANES), 1) < 2 * EDGE

    def ghost_rows(level, i):
        planes = mm(planes_of(level, (-1, HALF)).astype(BF16), window)
        for s in range(SLOTS):
            part = jnp.where(n // EDGE == s, planes, 0.0)
            part = part + pltpu.roll(part, EDGE, 1)
            spread[s] = part + pltpu.roll(part, 2 * EDGE, 1)
            for k in range(8):
                for p in range(2):
                    even = spread[s, pl.ds(CROWS * p + 2 * k, COMPS, stride=HALF), :]
                    odd = spread[s, pl.ds(CROWS * p + 2 * k + 1, COMPS, stride=HALF), :]
                    ghost[i, s, 8 * p : 8 * p + COMPS, LANES * k : LANES * (k + 1)] = jnp.where(first_y, even, odd)

    ghost[...] = jnp.zeros(ghost.shape, F32)
    ghost_rows(old, 0)
    ghost_rows(mean, 1)
    rates = chain(iota((NEAR, LANES), 0) % 8, tables.rate + [jnp.zeros((), F32)] * 3)
    rates2 = 2.0 * jnp.concatenate([rates, rates], axis=1)
    wide = 2.0 * chain(iota((2 * 8, PLANE), 0) % 8, tables.rate + [jnp.zeros((), F32)] * 3)

    along = []
    for s in range(SLOTS):
        ends = (planes_ref[s] + wide * ghost[0, s]).astype(BF16).astype(F32)
        one, two, next_last, last = (rows_ref[s, 8 * w : 8 * (w + 1), :] for w in range(4))
        near[s] = jnp.concatenate([ends[:8], one, last, ends[8:]], axis=0).astype(BF16)
        along.append(
            jnp.concatenate(
                [
                    one - 6.0 * ends[:8] + ghost[1, s, :8],
                    ends[:8] + two - 6.0 * one,
                    ends[8:] + next_last - 6.0 * last,
                    last - 6.0 * ends[8:] + ghost[1, s, 8:],
                ],
                axis=0,
            )
        )

    m = iota((2 * CROWS, LANES), 0)
    picked = jnp.where(
        m % HALF == n % HALF, mm(planes_of(mean, (0, HALF - 1)).astype(BF16), tables.side_pick()), 0.0
    ).astype(BF16)
    out, src = iota((NEAR, 2 * CROWS), 0), iota((NEAR, 2 * CROWS), 1)
    side_sum = ones_at((out % 8 == src % CROWS // HALF) & (out % 8 < COMPS) & (out // 16 == src // CROWS))
    sides = [part.astype(BF16) for part in slot_sides(mm(side_sum, picked))]
    ghosts = []
    zero = jnp.zeros((8, LANES), F32)
    for k in (0, 1):
        at = Z_HIGH if k else Z_LOW
        corner = jnp.concatenate([z_arr[0, at : at + PLANES, :], z_arr[1, at : at + PLANES, :]], axis=0)
        corner = mm(corner, window)
        for w, first in enumerate((0, 1, EDGE - 2, EDGE - 1)):
            level_rows[2, 8 * w : 8 * w + COMPS, :] = theirs_ref[k, pl.ds(first, COMPS, stride=EDGE), :]
        theirs = level_rows[2] + 2.0 * rates * jnp.concatenate([corner[8:16], zero, zero, corner[16:24]], axis=0)
        theirs = theirs.astype(BF16).astype(F32)
        is_linked = chain(iota((NEAR, LANES), 1) // EDGE, tables.near[2 + k]) >= 0
        level = mm(level_rows[k].astype(BF16), tables.from_coarse(2 + k, True))
        ghosts.append(jnp.where(is_linked, theirs, level))
    fields = [near[s] for s in range(SLOTS)]
    partners = partner_columns(lambda t: near[t], tables, NEAR)
    fresh = []
    for q in range(4):
        lanes = slice(QUAD * q, QUAD * (q + 1))
        terms = plane_terms(fields, partners, sides, q, weights)
        for s in range(SLOTS):
            field = fields[s][:, lanes]
            around = terms[NEAR * s : NEAR * (s + 1)] + along[s][:, lanes]
            if q == 0:
                around = around + edge_lanes(ghosts[0], s, False)
            if q == 3:
                around = around + edge_lanes(ghosts[1], s, True)
            value = jnp.where(tables.used[s] > 0, field.astype(F32) + rates2 * around, 0.0).astype(BF16)
            fresh.append(value)
            value = value.astype(F32)
            for h in range(2):
                for w, first in enumerate((0, 1, EDGE - 2, EDGE - 1)):
                    put[s, 2 * q + h, pl.ds(first, COMPS, stride=EDGE), :] = (
                        value[8 * w : 8 * w + COMPS, LANES * h : LANES * (h + 1)]
                    )
    a = iota((ROWS, LANES), 0) % EDGE
    replaced = (a < 2) | (a >= EDGE - 2)
    sends = []
    for s in range(SLOTS):
        for k in range(8):
            lanes = slice(LANES * k, LANES * (k + 1))
            fine_out[s, :, lanes] = jnp.where(replaced, put[s, k], fine_in[s, :, lanes].astype(F32)).astype(BF16)
        sends.append(pltpu.make_async_copy(fine_out.at[s], fine_hbm.at[s], sems.at[s]))
        sends[s].start()

    tall = jnp.concatenate(
        [
            jnp.concatenate([fresh[SLOTS * q + s][:, LANES * h : LANES * (h + 1)] for s in range(SLOTS)], axis=1)
            for q in range(4)
            for h in range(2)
        ],
        axis=0,
    )
    cells = mm(tall, place_ref[...])
    for k in range(8):
        part = cells[NEAR * k : NEAR * (k + 1)]
        for j in range(2):
            lane = slice(LANES * j, LANES * (j + 1))
            for p in range(2):
                pair = part[16 * p : 16 * p + 8, lane] + part[16 * p + 8 : 16 * p + 16, lane]
                split[pl.ds(8 * HALF * p + 2 * k + j, 8, stride=HALF), :] = pair

    coarse_out[...] = coarse_in[...]
    masks = CoarseLanes(tables, y_arr)
    row = iota((HALF, LANES), 0)
    for c in range(COMPS):
        r = tables.rate[c]
        y_flux = [y_arr[k, Y_FLUX + c * HALF : Y_FLUX + (c + 1) * HALF, :].astype(F32) for k in (0, 1)]
        for p, z in ((0, 0), (1, HALF - 1)):
            beyond = -1 if z == 0 else HALF
            level0, level1 = old[pl.ds(at_cell(c, z, 0), HALF), :], mean[pl.ds(at_cell(c, z, 0), HALF), :]
            halo = old[pl.ds(at_cell(c, beyond, 0), HALF), :]
            halo = masks.left * pltpu.roll(halo, LANES - 1, 1) + masks.right * pltpu.roll(halo, 1, 1)
            at = CROWS * p + HALF * c
            change = faces_ref[at : at + HALF, :] + (r * r) * halo
            for k, y in ((0, 0), (1, HALF - 1)):
                corner = old[pl.ds(at_cell(c, beyond, HALF if k else -1), 1), :]
                extra = masks.beyond_y(k, r, level0[y : y + 1], level1[y : y + 1], y_flux[k][z : z + 1], corner)
                change = change + jnp.where(row == y, extra, 0.0)
            flux = z_arr[p, Z_FLUX + c * HALF : Z_FLUX + (c + 1) * HALF, :].astype(F32)
            ahead = z_arr[p, Z_COVER : Z_COVER + HALF, :].astype(F32)
            change = change + flux + ahead * ((2.0 * r * r) * level0 - r * level1)
            coarse_out[pl.ds((c * HALF + z) * HALF, HALF), :] = masks.update(
                r, level0, level1, split[pl.ds(8 * HALF * p + c * HALF, HALF), :], change
            )
    for send in sends:
        send.wait()


SCALARS = [pl.BlockSpec(memory_space=pltpu.SMEM)] * 4
PARAMS = pltpu.CompilerParams(vmem_limit_bytes=32 * 1024 * 1024)
FETCH_PARAMS = pltpu.CompilerParams(vmem_limit_bytes=60 * 1024 * 1024)


def whole():
    return pl.BlockSpec(memory_space=pltpu.VMEM)


def local(coarse_cells, fine_cells, diffusivity, patch_column, patch_count, neighbor_slot):
    fine = fine_cells.reshape(SLOTS, ROWS, PLANE)
    coarse = coarse_cells.reshape(CELLS, LANES)
    tables = (patch_column, patch_count, neighbor_slot, diffusivity)
    n_own, n_fine = lax.axis_size("own"), lax.axis_size("fine")

    def swap(value, axis, count, far):
        shift = 1 if far else 0
        pairs = []
        for i in range(count):
            partner = ((i - shift) ^ 1) + shift
            pairs.append((i, partner % count))
        return lax.ppermute(value, axis, pairs)

    y_shape = jax.ShapeDtypeStruct((Y_ROWS, LANES), BF16)
    field_shape = jax.ShapeDtypeStruct((SLOTS, ROWS, PLANE), BF16)
    cells_shape = jax.ShapeDtypeStruct((CELLS, LANES), BF16)
    y_near, y_far = pl.pallas_call(
        y_message_kernel,
        in_specs=[pl.BlockSpec(memory_space=pl.ANY)] * 6,
        out_specs=[whole()] * 2,
        out_shape=[y_shape] * 2,
        scratch_shapes=[
            pltpu.SMEM((SLOTS,), jnp.int32),
            pltpu.SMEM((1,), jnp.int32),
            pltpu.SMEM((SLOTS, 4), jnp.int32),
            pltpu.SMEM((COMPS,), F32),
            pltpu.VMEM((SLOTS, ROWS, LANES), BF16),
            pltpu.VMEM((SLOTS, ROWS, LANES), BF16),
            pltpu.VMEM((CELLS, LANES), BF16),
            pltpu.VMEM((CELLS, LANES), F32),
            pltpu.VMEM((2, SLOTS * LANES, QUAD), BF16),
            pltpu.VMEM((ROWS, ROWS), BF16),
            pltpu.SemaphoreType.DMA((7,)),
        ],
        compiler_params=FETCH_PARAMS,
        name="y_messages",
    )(*tables, fine, coarse)
    y_near, y_far = swap(y_near, "fine", n_fine, False), swap(y_far, "fine", n_fine, True)

    planes_shape = jax.ShapeDtypeStruct((SLOTS, PLANES, PLANE), F32)
    level = pltpu.VMEM((COMPS * DEEP * SPAN, LANES), F32)
    weights, side_sum = jnp.asarray(plane_weights()), jnp.asarray(side_rows())
    half, edges, planes, flux, place = pl.pallas_call(
        interior_kernel,
        in_specs=SCALARS + [whole()] * 4,
        out_specs=[whole()] * 5,
        out_shape=[
            field_shape,
            jax.ShapeDtypeStruct((SLOTS, ROWS, QUAD), F32),
            planes_shape,
            jax.ShapeDtypeStruct((2 * CROWS, LANES), F32),
            jax.ShapeDtypeStruct((SLOTS * LANES, QUAD), BF16),
        ],
        scratch_shapes=[
            pltpu.VMEM((PLANES * HALF, LANES), F32),
            pltpu.VMEM((8 * PLANES, SLOTS * LANES), F32),
            pltpu.VMEM((4, ROWS, LANES), F32),
        ],
        compiler_params=PARAMS,
        cost_estimate=pl.CostEstimate(flops=2_000_000_000, bytes_accessed=5_000_000, transcendentals=0),
        name="interior",
    )(*tables, fine, coarse, weights, side_sum)

    z_shape = jax.ShapeDtypeStruct((Z_ROWS, LANES), BF16)
    z_near, z_far = pl.pallas_call(
        z_message_kernel,
        in_specs=SCALARS + [whole()] * 4,
        out_specs=[whole()] * 2,
        out_shape=[z_shape] * 2,
        scratch_shapes=[pltpu.VMEM((2, Y_ROWS, LANES), BF16), pltpu.VMEM((2 * CROWS, LANES), F32)],
        compiler_params=PARAMS,
        name="z_messages",
    )(*tables, coarse, flux, y_near, y_far)
    parts_shape = [
        cells_shape,
        field_shape,
        jax.ShapeDtypeStruct((SLOTS, 32, PLANE), F32),
        planes_shape,
        jax.ShapeDtypeStruct((2, ROWS, LANES), F32),
        jax.ShapeDtypeStruct((2 * CROWS, LANES), F32),
    ]
    middle_args = (*tables, fine, coarse, y_near, y_far, half, edges, planes, weights, side_sum, place)

    def middle(early, *parts):
        return pl.pallas_call(
            functools.partial(middle_kernel, early),
            in_specs=SCALARS + [whole()] * (10 + len(parts)),
            out_specs=[whole()] * 6,
            out_shape=parts_shape,
            scratch_shapes=[
                pltpu.VMEM((SLOTS, ROWS, PLANE), BF16),
                pltpu.VMEM((2, Y_ROWS, LANES), BF16),
                level,
                level,
                pltpu.VMEM((2, CELLS, LANES), F32),
                pltpu.VMEM((CELLS, LANES), F32),
                pltpu.VMEM((CELLS, LANES), F32),
                pltpu.VMEM((8, CROWS, SLOTS * LANES), BF16),
            ],
            compiler_params=PARAMS,
            cost_estimate=pl.CostEstimate(flops=3_000_000_000, bytes_accessed=8_000_000, transcendentals=0),
            name="middle_early" if early else "middle_late",
        )(*middle_args, *parts)

    z_near = swap(z_near, "own", n_own, False)
    parts = middle(True)
    z_far, parts = lax.optimization_barrier((z_far, parts))
    z_far = swap(z_far, "own", n_own, True)
    parts = middle(False, *parts)

    coarse_new, fine_new = pl.pallas_call(
        last_kernel,
        in_specs=SCALARS + [whole()] * 13,
        out_specs=[whole(), pl.BlockSpec(memory_space=pl.ANY)],
        out_shape=[cells_shape, field_shape],
        scratch_shapes=[
            pltpu.VMEM((2, Y_ROWS, LANES), BF16),
            pltpu.VMEM((2, Z_ROWS, LANES), BF16),
            level,
            level,
            pltpu.VMEM((SLOTS, 32, PLANE), BF16),
            pltpu.VMEM((PLANES * HALF, LANES), F32),
            pltpu.VMEM((2, CROWS, LANES), F32),
            pltpu.VMEM((SLOTS, 2 * CROWS, LANES), F32),
            pltpu.VMEM((2, SLOTS, PLANES, PLANE), F32),
            pltpu.VMEM((3, 32, LANES), F32),
            pltpu.VMEM((SLOTS, 8, ROWS, LANES), F32),
            pltpu.VMEM((SLOTS, ROWS, PLANE), BF16),
            pltpu.SemaphoreType.DMA((SLOTS,)),
        ],
        compiler_params=PARAMS,
        name="last",
    )(*tables, coarse, y_near, y_far, z_near, z_far, weights, place, *parts)
    return coarse_new.reshape(coarse_cells.shape), fine_new.reshape(fine_cells.shape)


def solution(mesh):
    return jax.shard_map(
        local,
        mesh=mesh,
        in_specs=(
            P(None, "own", "fine", None),
            P(("own", "fine"), None, None, None),
            P(),
            P(("own", "fine")),
            P(("own", "fine")),
            P(("own", "fine"), None),
        ),
        out_specs=(P(None, "own", "fine", None), P(("own", "fine"), None, None, None)),
        check_vma=False,
    )
```

time: 48.7 us -> 44 us (0.903)
  Pallas kernels: 14.1 us -> 18.5 us
  starting transfers between devices: 18.8 us -> 14.5 us
  waiting for transfers between devices: 9.48 us -> 6.7 us
  local copies, waits for them, and re-layouts: 4.27 us -> 2.11 us
    pallas_call x2 -> x5, Pallas kernels: 11.2 us -> 17.4 us  [the longest x2 7.01 us: middle(): pl.pallas_call(functools.partial(middle_kernel, early), in_specs=SCALARS...]
    ppermute x4, starting transfers between devices: 18.8 us -> 14.5 us  [swap(): return lax.ppermute(value, axis, pairs)]
    ppermute x4, waiting for transfers between devices: 9.48 us -> 6.7 us  [swap(): return lax.ppermute(value, axis, pairs)]
    unnamed x10 -> x16, local copies, waits for them, and re-layouts: 4.27 us -> 2.11 us
    pallas_call x1, Pallas kernels: 2.89 us -> 1.14 us  [local(): pl.pallas_call(z_message_kernel, in_specs=SCALARS + [whole()] * 4, out_sp...]
  transfers between devices with their start and end apart: 4 -> 4, of which waited for: 2 -> 2; matrix products, arithmetic and copies ran while one was open for 0% -> 0% of each run, Pallas kernels for 0% -> 24%
where the time goes in v2:
time: 44 us; the launch traced here: 43.6 us
  Pallas kernels  18.5 us (42%)
  starting transfers between devices  14.5 us (33%)
  waiting for transfers between devices  6.7 us (15%)
  local copies, waits for them, and re-layouts  2.11 us (5%)
  between operations  1.76 us (4%)
    ppermute x4, starting transfers between devices, swap(): return lax.ppermute(value, axis, pairs)  14.5 us
    pallas_call x2, Pallas kernels, middle(): pl.pallas_call(functools.partial(middle_kernel, early), in_specs=SCALARS...  7.01 us
    ppermute x4, waiting for transfers between devices, swap(): return lax.ppermute(value, axis, pairs)  6.7 us
    pallas_call x1, Pallas kernels, local(): pl.pallas_call(last_kernel, in_specs=SCALARS + [whole()] * 13, out_specs=...  3.91 us
    pallas_call x1, Pallas kernels, local(): pl.pallas_call(interior_kernel, in_specs=SCALARS + [whole()] * 4, out_spe...  3.36 us
    pallas_call x1, Pallas kernels, local(): pl.pallas_call(y_message_kernel, in_specs=[pl.BlockSpec(memory_space=pl.A...  3.1 us
    unnamed x16, local copies, waits for them, and re-layouts  2.11 us
    pallas_call x1, Pallas kernels, local(): pl.pallas_call(z_message_kernel, in_specs=SCALARS + [whole()] * 4, out_sp...  1.14 us
  transfers between devices with their start and end apart: 4, of which 2 were waited for; matrix products, arithmetic and copies ran while one was open for 0% of the time, Pallas kernels for 24%

profile of v2, /device:TPU:1, one launch (start us, length us, event | category | flops | bytes accessed | tf_op | source)
XLA Modules:
  0.0 43.6 jit_solution(4466437635388595436)
XLA Ops:
  0.6 0.0 copy-start.4
  0.6 0.0 copy-start.5
  1.4 3.1 %y_messages.1 = (bf16[576,128]{1,0:T(8,128)(2,1)}, bf16[576,128]{1,0:T(8,128)(2,1)}) custom-call(s32[4]{0:T(128)} %col.5, s32[1]{0:T(128)S(6)} %copy.10.cnt_hbm.cnt.refs_1_, s32[4,4]{1,0:T(4,128)} %nbr.5, f32[5]{0:T(128)} %rate.5, bf16[4,160,1024]{2,1,0:T(8,128)(2,1)} %bitcast.10, bf16[1280,128]{1,0:T(8,128)(2,1)} %bitcast.4), custom_call_target="tpu_custom_call" | custom-call | tf_op jit(solution)/shard_map/y_messages/pallas_call | solution.py:857
  4.6 8.8 %collective-permute-start = (bf16[576,128]{1,0:T(8,128)(2,1)}, bf16[576,128]{1,0:T(8,128)(2,1)S(1)}, u32[]{:S(2)}, u32[]{:S(2)}) collective-permute-start(bf16[576,128]{1,0:T(8,128)(2,1)} %get-tuple-element.32), channel_id=1, source_target_pairs={{0,1},{1,0},{2,3},{3,2},{4,5},{5,4},{6,7},{7,6},{8,9},{9,8},{10,11... | collective-permute-start | bytes 442376 | tf_op jit(solution)/shard_map/ppermute | solution.py:852
  13.3 1.9 %collective-permute-start.1 = (bf16[576,128]{1,0:T(8,128)(2,1)}, bf16[576,128]{1,0:T(8,128)(2,1)S(1)}, u32[]{:S(2)}, u32[]{:S(2)}) collective-permute-start(bf16[576,128]{1,0:T(8,128)(2,1)} %get-tuple-element.33), channel_id=1, source_target_pairs={{0,31},{1,2},{2,1},{3,4},{4,3},{5,6},{6,5},{7,8},{8,7},{9,10},{10,... | collective-permute-start | bytes 442376 | tf_op jit(solution)/shard_map/ppermute | solution.py:852
  15.3 0.0 copy-done.4
  15.3 0.0 copy-done.5
  15.3 0.0 copy-done.6
  15.3 0.0 copy-done.1
  15.3 0.0 copy-done
  15.3 0.0 copy-start.2
  15.3 1.1 %copy-done.2 = bf16[1280,256]{1,0:T(8,128)(2,1)S(1)} copy-done((bf16[1280,256]{1,0:T(8,128)(2,1)S(1)}, bf16[1280,256]{1,0:T(8,128)(2,1)}, u32[]{:S(2)}) %copy-start.2) | copy-done | bytes 655384
  16.4 1.0 %copy-done.7 = bf16[160,1280]{1,0:T(8,128)(2,1)S(1)} copy-done((bf16[160,1280]{1,0:T(8,128)(2,1)S(1)}, bf16[160,1280]{1,0:T(8,128)(2,1)}, u32[]{:S(2)}) %copy-start.7) | copy-done | bytes 409624
  17.4 3.4 %interior.1 = (bf16[4,160,1024]{2,1,0:T(8,128)(2,1)S(1)}, f32[4,160,256]{2,1,0:T(8,128)S(1)}, f32[4,16,1024]{2,1,0:T(8,128)S(1)}, f32[160,128]{1,0:T(8,128)S(1)}, bf16[512,256]{1,0:T(8,128)(2,1)S(1)}) custom-call(s32[4]{0:T(128)S(1)} %copy-done.5, s32[1]{0:T(128)S(6)} %copy.10.cnt_hbm.cnt.refs_1_, s32[4,4]{1,0:T(4,128)S(1)} %copy-done.4, f32[5]{0:T(128)S(1)} %copy-done.6, ...), custom_call_target="tpu_custom_call" | custom-call | flops 2000000000 | bytes 5000000 | tf_op jit(solution)/shard_map/interior/pallas_call | solution.py:883
  20.8 0.0 collective-permute-done.y_near.refs_6_
  20.8 2.5 %collective-permute-done.1.y_far.refs_7_ = bf16[576,128]{1,0:T(8,128)(2,1)S(1)} collective-permute-done((bf16[576,128]{1,0:T(8,128)(2,1)}, bf16[576,128]{1,0:T(8,128)(2,1)S(1)}, u32[]{:S(2)}, u32[]{:S(2)}) %collective-permute-start.1) | collective-permute-done | bytes 147488 | tf_op jit(solution)/shard_map/ppermute | solution.py:852
  23.2 1.1 %z_messages.1 = (bf16[288,128]{1,0:T(8,128)(2,1)S(1)}, bf16[288,128]{1,0:T(8,128)(2,1)S(1)}) custom-call(s32[4]{0:T(128)S(1)} %copy-done.5, s32[1]{0:T(128)S(6)} %copy.10.cnt_hbm.cnt.refs_1_, s32[4,4]{1,0:T(4,128)S(1)} %copy-done.4, f32[5]{0:T(128)S(1)} %copy-done.6, bf16[1280,128]{1,0:T(8,128)(2,1)S(1)} %bitcast.6, ...), custom_call_target="tpu_custom_call" | custom-call | tf_op jit(solution)/shard_map/z_messages/pallas_call | solution.py:905
  24.4 1.9 %collective-permute-start.2 = (bf16[288,128]{1,0:T(8,128)(2,1)S(1)}, bf16[288,128]{1,0:T(8,128)(2,1)S(1)}, u32[]{:S(2)}, u32[]{:S(2)}) collective-permute-start(bf16[288,128]{1,0:T(8,128)(2,1)S(1)} %get-tuple-element.35), channel_id=1, source_target_pairs={{0,32},{32,0},{64,96},{96,64},{128,160},{160,128},{192,224},{224,1... | collective-permute-start | bytes 221192 | tf_op jit(solution)/shard_map/ppermute | solution.py:852
  26.3 6.0 %middle_early.1 = (bf16[1280,128]{1,0:T(8,128)(2,1)S(1)}, bf16[4,160,1024]{2,1,0:T(8,128)(2,1)S(1)}, f32[4,32,1024]{2,1,0:T(8,128)S(1)}, f32[4,16,1024]{2,1,0:T(...) custom-call(s32[4]{0:T(128)S(1)} %copy-done.5, s32[1]{0:T(128)S(6)} %copy.10.cnt_hbm.cnt.refs_1_, ...), custom_call_target="tpu_custom_call" | custom-call | flops 3000000000 | bytes 8000000 | tf_op jit(solution)/shard_map/middle_early/pallas_call | solution.py:925
  32.3 1.9 %collective-permute-start.3 = (bf16[288,128]{1,0:T(8,128)(2,1)S(1)}, bf16[288,128]{1,0:T(8,128)(2,1)S(1)}, u32[]{:S(2)}, u32[]{:S(2)}) collective-permute-start(bf16[288,128]{1,0:T(8,128)(2,1)S(1)} %get-tuple-element.47), channel_id=1, source_target_pairs={{0,480},{32,64},{64,32},{96,128},{128,96},{160,192},{192,160},{224... | collective-permute-start | bytes 221192 | tf_op jit(solution)/shard_map/ppermute | solution.py:852
  34.3 1.0 %middle_late.1 = (bf16[1280,128]{1,0:T(8,128)(2,1)S(1)}, bf16[4,160,1024]{2,1,0:T(8,128)(2,1)S(1)}, f32[4,32,1024]{2,1,0:T(8,128)S(1)}, f32[4,16,1024]{2,1,0:T(8...) custom-call(s32[4]{0:T(128)S(1)} %copy-done.5, s32[1]{0:T(128)S(6)} %copy.10.cnt_hbm.cnt.refs_1_, ...), custom_call_target="tpu_custom_call" | custom-call | flops 3000000000 | bytes 8000000 | tf_op jit(solution)/shard_map/middle_late/pallas_call | solution.py:925
  35.3 0.0 collective-permute-done.2.z_near
  35.3 4.2 %collective-permute-done.3.z_far = bf16[288,128]{1,0:T(8,128)(2,1)S(1)} collective-permute-done((bf16[288,128]{1,0:T(8,128)(2,1)S(1)}, bf16[288,128]{1,0:T(8,128)(2,1)S(1)}, u32[]{:S(2)}, u32[]{:S(2)}) %collective-permute-start.3) | collective-permute-done | bytes 73760 | tf_op jit(solution)/shard_map/ppermute | solution.py:852
  39.5 3.9 %last.1 = (bf16[1280,128]{1,0:T(8,128)(2,1)}, bf16[4,160,1024]{2,1,0:T(8,128)(2,1)}) custom-call(s32[4]{0:T(128)S(1)} %copy-done.5, s32[1]{0:T(128)S(6)} %copy.10.cnt_hbm.cnt.refs_1_, s32[4,4]{1,0:T(4,128)S(1)} %copy-done.4, f32[5]{0:T(128)S(1)} %copy-done.6, bf16[1280,128]{1,0:T(8,128)(2,1)S(1)} %bitcast.9, ...), custom_call_target="tpu_custom_call" | custom-call | tf_op jit(solution)/shard_map/last/pallas_call | solution.py:951
  (6 shorter events, 0.0 us)
Async XLA Ops:
  0.6 14.6 %copy-start.4 = (s32[4,4]{1,0:T(4,128)S(1)}, s32[4,4]{1,0:T(4,128)}, u32[]{:S(2)}) copy-start(s32[4,4]{1,0:T(4,128)} %nbr.5) | copy-start | bytes 196
  0.6 14.6 %copy-start.5 = (s32[4]{0:T(128)S(1)}, s32[4]{0:T(128)}, u32[]{:S(2)}) copy-start(s32[4]{0:T(128)} %col.5) | copy-start | bytes 52
  0.7 14.6 %copy-start.6 = (f32[5]{0:T(128)S(1)}, f32[5]{0:T(128)}, u32[]{:S(2)}) copy-start(f32[5]{0:T(128)} %rate.5) | copy-start | bytes 64
  0.7 14.6 %copy-start.1 = (bf16[4,5,32,1024]{3,2,1,0:T(8,128)(2,1)S(1)}, bf16[4,5,32,1024]{3,2,1,0:T(8,128)(2,1)}, u32[]{:S(2)}) copy-start(bf16[4,5,32,1024]{3,2,1,0:T(8,128)(2,1)} %param.9) | copy-start | bytes 3932164
  0.7 14.6 %copy-start = (bf16[5,16,16,128]{3,2,1,0:T(8,128)(2,1)S(1)}, bf16[5,16,16,128]{3,2,1,0:T(8,128)(2,1)}, u32[]{:S(2)}) copy-start(bf16[5,16,16,128]{3,2,1,0:T(8,128)(2,1)} %param.8) | copy-start | bytes 983044
  4.6 16.2 %collective-permute-start = (bf16[576,128]{1,0:T(8,128)(2,1)}, bf16[576,128]{1,0:T(8,128)(2,1)S(1)}, u32[]{:S(2)}, u32[]{:S(2)}) collective-permute-start(bf16[576,128]{1,0:T(8,128)(2,1)} %get-tuple-element.32), channel_id=1, source_target_pairs={{0,1},{1,0},{2,3},{3,2},{4,5},{5,4},{6,7},{7,6},{8,9},{9,8},{10,11... | collective-permute-start | bytes 442376 | tf_op jit(solution)/shard_map/ppermute | solution.py:852
  13.3 9.9 %collective-permute-start.1 = (bf16[576,128]{1,0:T(8,128)(2,1)}, bf16[576,128]{1,0:T(8,128)(2,1)S(1)}, u32[]{:S(2)}, u32[]{:S(2)}) collective-permute-start(bf16[576,128]{1,0:T(8,128)(2,1)} %get-tuple-element.33), channel_id=1, source_target_pairs={{0,31},{1,2},{2,1},{3,4},{4,3},{5,6},{6,5},{7,8},{8,7},{9,10},{10,... | collective-permute-start | bytes 442376 | tf_op jit(solution)/shard_map/ppermute | solution.py:852
  15.3 1.1 %copy-start.2 = (bf16[1280,256]{1,0:T(8,128)(2,1)S(1)}, bf16[1280,256]{1,0:T(8,128)(2,1)}, u32[]{:S(2)}) copy-start(bf16[1280,256]{1,0:T(8,128)(2,1)} %constant.4.clone.weights.refs_11_) | copy-start | bytes 1966084
  16.4 1.0 %copy-start.7 = (bf16[160,1280]{1,0:T(8,128)(2,1)S(1)}, bf16[160,1280]{1,0:T(8,128)(2,1)}, u32[]{:S(2)}) copy-start(bf16[160,1280]{1,0:T(8,128)(2,1)} %constant.5.clone.side_sum.refs_12_) | copy-start | bytes 1228804
  17.4 8.9 %copy-start.3 = (bf16[1280,256]{1,0:T(8,128)(2,1)S(1)}, bf16[1280,256]{1,0:T(8,128)(2,1)}, u32[]{:S(2)}) copy-start(bf16[1280,256]{1,0:T(8,128)(2,1)} %constant.4.clone.weights.refs_11_) | copy-start | bytes 1966084
  24.4 10.9 %collective-permute-start.2 = (bf16[288,128]{1,0:T(8,128)(2,1)S(1)}, bf16[288,128]{1,0:T(8,128)(2,1)S(1)}, u32[]{:S(2)}, u32[]{:S(2)}) collective-permute-start(bf16[288,128]{1,0:T(8,128)(2,1)S(1)} %get-tuple-element.35), channel_id=1, source_target_pairs={{0,32},{32,0},{64,96},{96,64},{128,160},{160,128},{192,224},{224,1... | collective-permute-start | bytes 221192 | tf_op jit(solution)/shard_map/ppermute | solution.py:852
  32.3 7.2 %collective-permute-start.3 = (bf16[288,128]{1,0:T(8,128)(2,1)S(1)}, bf16[288,128]{1,0:T(8,128)(2,1)S(1)}, u32[]{:S(2)}, u32[]{:S(2)}) collective-permute-start(bf16[288,128]{1,0:T(8,128)(2,1)S(1)} %get-tuple-element.47), channel_id=1, source_target_pairs={{0,480},{32,64},{64,32},{96,128},{128,96},{160,192},{192,160},{224... | collective-permute-start | bytes 221192 | tf_op jit(solution)/shard_map/ppermute | solution.py:852

commit v3 on v2

--- a/solution.py
+++ b/solution.py
@@ -499,27 +499,33 @@
         return flux + self.beside[k] * gain
 
 
-def middle_kernel(early, *refs):
+def early_kernel(*refs):
+    ins, outs, scratch = refs[:14], refs[14:19], refs[19:]
+
+    @pl.when(lax.axis_index("own") == 0)
+    def _():
+        middle_fine(*ins, *outs, *scratch)
+
+
+def late_kernel(*refs):
+    ins, done, coarse_out, faces_ref, outs, scratch = refs[:14], refs[14:19], refs[19], refs[20], refs[21:25], refs[25:]
+    pairs, strips, y_arr, old, mean, split, average, outside = scratch
     is_early = lax.axis_index("own") == 0
 
-    @pl.when(is_early if early else jnp.logical_not(is_early))
+    @pl.when(jnp.logical_not(is_early))
     def _():
-        middle_body(*(refs if early else refs[:14] + refs[20:]))
-
-    if not early:
-
-        @pl.when(is_early)
-        def _():
-            for done, out in zip(refs[14:20], refs[20:26]):
-                out[...] = done[...]
-
-
-def middle_body(
-    col, cnt, nbr, rate, fine_ref, coarse_ref, y_near, y_far, half_in, edges_ref, planes_in, weights, side_sum, place_ref,
-    coarse_out, fine_out, rows_ref, planes_ref, theirs_ref, faces_ref,
-    half, y_arr, old, mean, split, average, outside, pairs,
-):
-    tables = Tables(col, cnt, nbr, rate)
+        middle_fine(*ins, *outs, pairs, strips, y_arr, old, mean, split)
+
+    @pl.when(is_early)
+    def _():
+        for source, target in zip(done, (*outs, pairs)):
+            target[...] = source[...]
+        levels(Tables(*ins[:4]), ins[5], ins[6], ins[7], y_arr, old, mean)
+
+    middle_coarse(Tables(*ins[:4]), ins[13], pairs, y_arr, old, mean, average, outside, coarse_out, faces_ref)
+
+
+def levels(tables, coarse_ref, y_near, y_far, y_arr, old, mean):
     sort_arrivals("fine", y_near, y_far, y_arr)
     fill_old(old, coarse_ref, y_arr, range(HALF))
     for c in range(COMPS):
@@ -527,6 +533,14 @@
             old[pl.ds(at_cell(c, z, 0) - 8, SPAN), :] = jnp.zeros((SPAN, LANES), F32)
     own_mean(old, mean, tables, range(HALF))
     strip_mean(old, mean, y_arr, tables)
+
+
+def middle_fine(
+    col, cnt, nbr, rate, fine_ref, coarse_ref, y_near, y_far, half_in, edges_ref, planes_in, weights, side_sum, place_ref,
+    fine_out, rows_ref, planes_ref, theirs_ref, pairs, strips, y_arr, old, mean, split,
+):
+    tables = Tables(col, cnt, nbr, rate)
+    levels(tables, coarse_ref, y_near, y_far, y_arr, old, mean)
     rates = tables.rates(ROWS, EDGE)
     rates2 = 2.0 * jnp.concatenate([rates, rates], axis=1)
     double, rows_z = copies(ROWS, 2), z_stencil()
@@ -541,8 +555,11 @@
         rows = [level[pl.ds(at_cell(c, 0, y), HALF, stride=SPAN), :] for c in range(COMPS)]
         return mm(double, jnp.concatenate(rows, axis=0).astype(BF16)).astype(BF16)
 
-    half[...] = half_in[...]
     planes_ref[...] = planes_in[...]
+
+    def half(t):
+        return jnp.concatenate([strips[t, :, :LANES], half_in[t, :, LANES : PLANE - LANES], strips[t, :, LANES:]], axis=1)
+
     second = []
     plane_rates = chain(iota((PLANES, LANES), 0) % 8, tables.rate + [jnp.zeros((), F32)] * 3)
     for k, y in ((0, -1), (1, HALF)):
@@ -554,7 +571,7 @@
         part = slice(LANES * k, LANES * (k + 1))
         for s in range(SLOTS):
             add = edge_lanes(ghost, s, bool(k))[:, part]
-            half[s, :, tile] = (edges_ref[s, :, part] + 2.0 * rates * add).astype(BF16)
+            strips[s, :, part] = (edges_ref[s, :, part] + 2.0 * rates * add).astype(BF16)
             add = edge_lanes(plane_ghost, s, bool(k))[:, part]
             planes_ref[s, :, tile] = planes_ref[s, :, tile] + 2.0 * plane_rates * add
         theirs = mm(y_arr[k, Y_HALF : Y_HALF + ROWS, :], linked) + 2.0 * rates * neighbour_rows(fine_ref, k)
@@ -564,8 +581,8 @@
         second.append(jnp.where(is_linked, theirs, mm(level_row(mean, y), opened)))
 
     rows_ref[...] = jnp.zeros(rows_ref.shape, F32)
-    fields = [half[s] for s in range(SLOTS)]
-    partners = partner_columns(lambda t: half[t], tables, ROWS)
+    fields = [half(s) for s in range(SLOTS)]
+    partners = partner_columns(half, tables, ROWS)
     for q in range(4):
         lanes = slice(QUAD * q, QUAD * (q + 1))
         terms = plane_terms(fields, partners, sides, q, weights)
@@ -582,35 +599,33 @@
                 split[h, ROWS : 2 * ROWS, :] = (
                     split[h, :ROWS, :] + fine_ref[s, :, QUAD * q + LANES * h : QUAD * q + LANES * (h + 1)].astype(F32)
                 )
-                pairs[2 * q + h, :, LANES * s : LANES * (s + 1)] = (
+                pairs[0, 2 * q + h, :, LANES * s : LANES * (s + 1)] = (
                     split[h, pl.ds(ROWS, CROWS, stride=2), :] + split[h, pl.ds(ROWS + 1, CROWS, stride=2), :]
                 ).astype(BF16)
                 at = slice(QUAD * q + LANES * h, QUAD * q + LANES * (h + 1))
                 for w, first in enumerate((1, 2, EDGE - 3, EDGE - 2)):
                     rows_ref[s, 8 * w : 8 * w + COMPS, at] = split[h, pl.ds(first, COMPS, stride=EDGE), :]
-            value = jnp.where(tables.used[s] > 0, start + rates2 * around, 0.0)
-            fine_out[s, :, lanes] = value.astype(BF16)
-
-    faces = mm(pairs[...].reshape(8 * CROWS, SLOTS * LANES), tables.pool_spread(1))
-    tall = jnp.concatenate(
-        [
-            jnp.concatenate([fine_out[s, :, LANES * k : LANES * (k + 1)] for s in range(SLOTS)], axis=1)
-            for k in range(8)
-        ],
-        axis=0,
-    )
-    cells = mm(tall, place_ref[...])
+            value = jnp.where(tables.used[s] > 0, start + rates2 * around, 0.0).astype(BF16)
+            fine_out[s, :, lanes] = value
+            value = value.astype(F32)
+            for h in range(2):
+                split[h, 2 * ROWS : 3 * ROWS, :] = value[:, LANES * h : LANES * (h + 1)]
+                pairs[1, 2 * q + h, :, LANES * s : LANES * (s + 1)] = (
+                    split[h, pl.ds(2 * ROWS, CROWS, stride=2), :] + split[h, pl.ds(2 * ROWS + 1, CROWS, stride=2), :]
+                ).astype(BF16)
+
+
+def middle_coarse(tables, place_ref, pairs, y_arr, old, mean, average, outside, coarse_out, faces_ref):
+    faces = mm(pairs[0].reshape(8 * CROWS, SLOTS * LANES), tables.pool_spread(1))
+    cells = mm(pairs[1].reshape(8 * CROWS, SLOTS * LANES), place_ref[...])
     coarse_rates = tables.rates(CROWS, HALF)
     scale = 0.25 * coarse_rates
     for j in range(2):
         lanes = slice(LANES * j, LANES * (j + 1))
-        split[j] = cells[:, lanes]
         for k in range(8):
             at = pl.ds(2 * k + j, CROWS, stride=HALF)
             outside[at, :] = scale * faces[CROWS * k : CROWS * (k + 1), lanes]
-            average[at, :] = (
-                split[j, pl.ds(ROWS * k, CROWS, stride=2), :] + split[j, pl.ds(ROWS * k + 1, CROWS, stride=2), :]
-            )
+            average[at, :] = cells[CROWS * k : CROWS * (k + 1), lanes]
     for c in range(COMPS):
         for p in range(2):
             at = CROWS * p + HALF * c
@@ -911,42 +926,50 @@
         compiler_params=PARAMS,
         name="z_messages",
     )(*tables, coarse, flux, y_near, y_far)
-    parts_shape = [
-        cells_shape,
+    fine_shapes = [
         field_shape,
         jax.ShapeDtypeStruct((SLOTS, 32, PLANE), F32),
         planes_shape,
         jax.ShapeDtypeStruct((2, ROWS, LANES), F32),
-        jax.ShapeDtypeStruct((2 * CROWS, LANES), F32),
     ]
+    pairs_shape = (2, 8, CROWS, SLOTS * LANES)
     middle_args = (*tables, fine, coarse, y_near, y_far, half, edges, planes, weights, side_sum, place)
-
-    def middle(early, *parts):
-        return pl.pallas_call(
-            functools.partial(middle_kernel, early),
-            in_specs=SCALARS + [whole()] * (10 + len(parts)),
-            out_specs=[whole()] * 6,
-            out_shape=parts_shape,
-            scratch_shapes=[
-                pltpu.VMEM((SLOTS, ROWS, PLANE), BF16),
-                pltpu.VMEM((2, Y_ROWS, LANES), BF16),
-                level,
-                level,
-                pltpu.VMEM((2, CELLS, LANES), F32),
-                pltpu.VMEM((CELLS, LANES), F32),
-                pltpu.VMEM((CELLS, LANES), F32),
-                pltpu.VMEM((8, CROWS, SLOTS * LANES), BF16),
-            ],
-            compiler_params=PARAMS,
-            cost_estimate=pl.CostEstimate(flops=3_000_000_000, bytes_accessed=8_000_000, transcendentals=0),
-            name="middle_early" if early else "middle_late",
-        )(*middle_args, *parts)
-
+    scratch = [
+        pltpu.VMEM((SLOTS, ROWS, QUAD), BF16),
+        pltpu.VMEM((2, Y_ROWS, LANES), BF16),
+        level,
+        level,
+        pltpu.VMEM((2, 3 * ROWS, LANES), F32),
+    ]
     z_near = swap(z_near, "own", n_own, False)
-    parts = middle(True)
-    z_far, parts = lax.optimization_barrier((z_far, parts))
+    done = pl.pallas_call(
+        early_kernel,
+        in_specs=SCALARS + [whole()] * 10,
+        out_specs=[whole()] * 5,
+        out_shape=fine_shapes + [jax.ShapeDtypeStruct(pairs_shape, BF16)],
+        scratch_shapes=scratch,
+        compiler_params=PARAMS,
+        cost_estimate=pl.CostEstimate(flops=3_000_000_000, bytes_accessed=8_000_000, transcendentals=0),
+        name="early",
+    )(*middle_args)
+    z_far, done = lax.optimization_barrier((z_far, done))
     z_far = swap(z_far, "own", n_own, True)
-    parts = middle(False, *parts)
+    coarse_part, faces, *parts = pl.pallas_call(
+        late_kernel,
+        in_specs=SCALARS + [whole()] * 15,
+        out_specs=[whole()] * 6,
+        out_shape=[cells_shape, jax.ShapeDtypeStruct((2 * CROWS, LANES), F32)] + fine_shapes,
+        scratch_shapes=[
+            pltpu.VMEM(pairs_shape, BF16),
+            *scratch,
+            pltpu.VMEM((CELLS, LANES), F32),
+            pltpu.VMEM((CELLS, LANES), F32),
+        ],
+        compiler_params=PARAMS,
+        cost_estimate=pl.CostEstimate(flops=3_000_000_000, bytes_accessed=8_000_000, transcendentals=0),
+        name="late",
+    )(*middle_args, *done)
+    parts = (coarse_part, *parts, faces)
 
     coarse_new, fine_new = pl.pallas_call(
         last_kernel,

time: 44 us -> 43.1 us (0.980)
  waiting for transfers between devices: 6.7 us -> 4.73 us
  Pallas kernels: 18.5 us -> 19.3 us
    ppermute x4, waiting for transfers between devices: 6.7 us -> 4.73 us  [swap(): return lax.ppermute(value, axis, pairs)]
    pallas_call x2, Pallas kernels: 7.01 us -> 7.83 us  [the longest x1 5.1 us: local(): pl.pallas_call(early_kernel, in_specs=SCALARS + [whole()] * 10, out_specs...]
    unnamed x16 -> x18, local copies, waits for them, and re-layouts: 2.11 us -> 2.12 us
  transfers between devices with their start and end apart: 4 -> 4, of which waited for: 2 -> 2; matrix products, arithmetic and copies ran while one was open for 0% -> 0% of each run, Pallas kernels for 24% -> 26%
where the time goes in v3:
time: 43.1 us; the launch traced here: 42.7 us
  Pallas kernels  19.3 us (45%)
  starting transfers between devices  14.8 us (34%)
  waiting for transfers between devices  4.73 us (11%)
  local copies, waits for them, and re-layouts  2.12 us (5%)
  between operations  1.76 us (4%)
    ppermute x4, starting transfers between devices, swap(): return lax.ppermute(value, axis, pairs)  14.8 us
    pallas_call x1, Pallas kernels, local(): pl.pallas_call(early_kernel, in_specs=SCALARS + [whole()] * 10, out_specs...  5.1 us
    ppermute x4, waiting for transfers between devices, swap(): return lax.ppermute(value, axis, pairs)  4.73 us
    pallas_call x1, Pallas kernels, local(): pl.pallas_call(last_kernel, in_specs=SCALARS + [whole()] * 13, out_specs=...  3.91 us
    pallas_call x1, Pallas kernels, local(): pl.pallas_call(interior_kernel, in_specs=SCALARS + [whole()] * 4, out_spe...  3.36 us
    pallas_call x1, Pallas kernels, local(): pl.pallas_call(y_message_kernel, in_specs=[pl.BlockSpec(memory_space=pl.A...  3.1 us
    pallas_call x1, Pallas kernels, local(): pl.pallas_call(late_kernel, in_specs=SCALARS + [whole()] * 15, out_specs=...  2.73 us
    unnamed x18, local copies, waits for them, and re-layouts  2.12 us
  transfers between devices with their start and end apart: 4, of which 2 were waited for; matrix products, arithmetic and copies ran while one was open for 0% of the time, Pallas kernels for 26%

profile of v3, /device:TPU:1, one launch (start us, length us, event | category | flops | bytes accessed | tf_op | source)
XLA Modules:
  0.0 42.7 jit_solution(7579796274698414322)
XLA Ops:
  0.6 0.0 copy-start.4
  0.6 0.0 copy-start.5
  0.7 0.0 copy-start.6
  0.7 0.0 copy-start.1
  1.4 3.1 %y_messages.1 = (bf16[576,128]{1,0:T(8,128)(2,1)}, bf16[576,128]{1,0:T(8,128)(2,1)}) custom-call(s32[4]{0:T(128)} %col.5, s32[1]{0:T(128)S(6)} %copy.10.cnt_hbm.cnt.refs_1_, s32[4,4]{1,0:T(4,128)} %nbr.5, f32[5]{0:T(128)} %rate.5, bf16[4,160,1024]{2,1,0:T(8,128)(2,1)} %bitcast.10, bf16[1280,128]{1,0:T(8,128)(2,1)} %bitcast.4), custom_call_target="tpu_custom_call" | custom-call | tf_op jit(solution)/shard_map/y_messages/pallas_call | solution.py:872
  4.6 8.8 %collective-permute-start = (bf16[576,128]{1,0:T(8,128)(2,1)}, bf16[576,128]{1,0:T(8,128)(2,1)S(1)}, u32[]{:S(2)}, u32[]{:S(2)}) collective-permute-start(bf16[576,128]{1,0:T(8,128)(2,1)} %get-tuple-element.30), channel_id=1, source_target_pairs={{0,1},{1,0},{2,3},{3,2},{4,5},{5,4},{6,7},{7,6},{8,9},{9,8},{10,11... | collective-permute-start | bytes 442376 | tf_op jit(solution)/shard_map/ppermute | solution.py:867
  13.3 1.9 %collective-permute-start.1 = (bf16[576,128]{1,0:T(8,128)(2,1)}, bf16[576,128]{1,0:T(8,128)(2,1)S(1)}, u32[]{:S(2)}, u32[]{:S(2)}) collective-permute-start(bf16[576,128]{1,0:T(8,128)(2,1)} %get-tuple-element.31), channel_id=1, source_target_pairs={{0,31},{1,2},{2,1},{3,4},{4,3},{5,6},{6,5},{7,8},{8,7},{9,10},{10,... | collective-permute-start | bytes 442376 | tf_op jit(solution)/shard_map/ppermute | solution.py:867
  15.3 0.0 copy-start.2
  15.3 1.1 %copy-done.2 = bf16[1280,256]{1,0:T(8,128)(2,1)S(1)} copy-done((bf16[1280,256]{1,0:T(8,128)(2,1)S(1)}, bf16[1280,256]{1,0:T(8,128)(2,1)}, u32[]{:S(2)}) %copy-start.2) | copy-done | bytes 655384
  16.4 1.0 %copy-done.7 = bf16[160,1280]{1,0:T(8,128)(2,1)S(1)} copy-done((bf16[160,1280]{1,0:T(8,128)(2,1)S(1)}, bf16[160,1280]{1,0:T(8,128)(2,1)}, u32[]{:S(2)}) %copy-start.7) | copy-done | bytes 409624
  17.4 3.4 %interior.1 = (bf16[4,160,1024]{2,1,0:T(8,128)(2,1)S(1)}, f32[4,160,256]{2,1,0:T(8,128)S(1)}, f32[4,16,1024]{2,1,0:T(8,128)S(1)}, f32[160,128]{1,0:T(8,128)S(1)}, bf16[512,256]{1,0:T(8,128)(2,1)S(1)}) custom-call(s32[4]{0:T(128)S(1)} %copy-done.5, s32[1]{0:T(128)S(6)} %copy.10.cnt_hbm.cnt.refs_1_, s32[4,4]{1,0:T(4,128)S(1)} %copy-done.4, f32[5]{0:T(128)S(1)} %copy-done.6, ...), custom_call_target="tpu_custom_call" | custom-call | flops 2000000000 | bytes 5000000 | tf_op jit(solution)/shard_map/interior/pallas_call | solution.py:898
  20.8 0.0 collective-permute-done.y_near.refs_6_
  20.8 2.5 %collective-permute-done.1.y_far.refs_7_ = bf16[576,128]{1,0:T(8,128)(2,1)S(1)} collective-permute-done((bf16[576,128]{1,0:T(8,128)(2,1)}, bf16[576,128]{1,0:T(8,128)(2,1)S(1)}, u32[]{:S(2)}, u32[]{:S(2)}) %collective-permute-start.1) | collective-permute-done | bytes 147488 | tf_op jit(solution)/shard_map/ppermute | solution.py:867
  23.2 1.1 %z_messages.1 = (bf16[288,128]{1,0:T(8,128)(2,1)S(1)}, bf16[288,128]{1,0:T(8,128)(2,1)S(1)}) custom-call(s32[4]{0:T(128)S(1)} %copy-done.5, s32[1]{0:T(128)S(6)} %copy.10.cnt_hbm.cnt.refs_1_, s32[4,4]{1,0:T(4,128)S(1)} %copy-done.4, f32[5]{0:T(128)S(1)} %copy-done.6, bf16[1280,128]{1,0:T(8,128)(2,1)S(1)} %bitcast.6, ...), custom_call_target="tpu_custom_call" | custom-call | tf_op jit(solution)/shard_map/z_messages/pallas_call | solution.py:920
  24.4 1.9 %collective-permute-start.2 = (bf16[288,128]{1,0:T(8,128)(2,1)S(1)}, bf16[288,128]{1,0:T(8,128)(2,1)S(1)}, u32[]{:S(2)}, u32[]{:S(2)}) collective-permute-start(bf16[288,128]{1,0:T(8,128)(2,1)S(1)} %get-tuple-element.33), channel_id=1, source_target_pairs={{0,32},{32,0},{64,96},{96,64},{128,160},{160,128},{192,224},{224,1... | collective-permute-start | bytes 221192 | tf_op jit(solution)/shard_map/ppermute | solution.py:867
  26.3 0.0 copy-done.3
  26.3 0.0 copy-start.8
  26.3 5.1 %early.1 = (bf16[4,160,1024]{2,1,0:T(8,128)(2,1)S(1)}, f32[4,32,1024]{2,1,0:T(8,128)S(1)}, f32[4,16,1024]{2,1,0:T(8,128)S(1)}, f32[2,160,128]{2,1,0:T(8,128)S(1)}, bf16[2,8,80,512]{3,2,1,0:T(8,128)(2,1)S(1)}) custom-call(s32[4]{0:T(128)S(1)} %copy-done.5, s32[1]{0:T(128)S(6)} %copy.10.cnt_hbm.cnt.refs_1_, s32[4,4]{1,0:T(4,128)S(1)} %copy-done.4, ...), custom_call_target="tpu_custom_call" | custom-call | flops 3000000000 | bytes 8000000 | tf_op jit(solution)/shard_map/early/pallas_call | solution.py:945
  31.5 2.2 %collective-permute-start.3 = (bf16[288,128]{1,0:T(8,128)(2,1)S(1)}, bf16[288,128]{1,0:T(8,128)(2,1)S(1)}, u32[]{:S(2)}, u32[]{:S(2)}) collective-permute-start(bf16[288,128]{1,0:T(8,128)(2,1)S(1)} %get-tuple-element.44), channel_id=1, source_target_pairs={{0,480},{32,64},{64,32},{96,128},{128,96},{160,192},{192,160},{224... | collective-permute-start | bytes 221192 | tf_op jit(solution)/shard_map/ppermute | solution.py:867
  33.6 0.0 copy-done.8
  33.6 2.7 %late.1 = (bf16[1280,128]{1,0:T(8,128)(2,1)S(1)}, f32[160,128]{1,0:T(8,128)S(1)}, bf16[4,160,1024]{2,1,0:T(8,128)(2,1)S(1)}, f32[4,32,1024]{2,1,0:T(8,128)S(1)},...) custom-call(s32[4]{0:T(128)S(1)} %copy-done.5, s32[1]{0:T(128)S(6)} %copy.10.cnt_hbm.cnt.refs_1_, ...), custom_call_target="tpu_custom_call" | custom-call | flops 3000000000 | bytes 8000000 | tf_op jit(solution)/shard_map/late/pallas_call | solution.py:957
  36.4 0.0 collective-permute-done.2.z_near
  36.4 2.3 %collective-permute-done.3.z_far = bf16[288,128]{1,0:T(8,128)(2,1)S(1)} collective-permute-done((bf16[288,128]{1,0:T(8,128)(2,1)S(1)}, bf16[288,128]{1,0:T(8,128)(2,1)S(1)}, u32[]{:S(2)}, u32[]{:S(2)}) %collective-permute-start.3) | collective-permute-done | bytes 73760 | tf_op jit(solution)/shard_map/ppermute | solution.py:867
  38.7 3.9 %last.1 = (bf16[1280,128]{1,0:T(8,128)(2,1)}, bf16[4,160,1024]{2,1,0:T(8,128)(2,1)}) custom-call(s32[4]{0:T(128)S(1)} %copy-done.5, s32[1]{0:T(128)S(6)} %copy.10.cnt_hbm.cnt.refs_1_, s32[4,4]{1,0:T(4,128)S(1)} %copy-done.4, f32[5]{0:T(128)S(1)} %copy-done.6, bf16[1280,128]{1,0:T(8,128)(2,1)S(1)} %bitcast.9, ...), custom_call_target="tpu_custom_call" | custom-call | tf_op jit(solution)/shard_map/last/pallas_call | solution.py:974
  (8 shorter events, 0.0 us)
Async XLA Ops:
  0.6 14.6 %copy-start.4 = (s32[4,4]{1,0:T(4,128)S(1)}, s32[4,4]{1,0:T(4,128)}, u32[]{:S(2)}) copy-start(s32[4,4]{1,0:T(4,128)} %nbr.5) | copy-start | bytes 196
  0.6 14.6 %copy-start.5 = (s32[4]{0:T(128)S(1)}, s32[4]{0:T(128)}, u32[]{:S(2)}) copy-start(s32[4]{0:T(128)} %col.5) | copy-start | bytes 52
  0.7 14.6 %copy-start.6 = (f32[5]{0:T(128)S(1)}, f32[5]{0:T(128)}, u32[]{:S(2)}) copy-start(f32[5]{0:T(128)} %rate.5) | copy-start | bytes 64
  0.7 14.6 %copy-start.1 = (bf16[4,5,32,1024]{3,2,1,0:T(8,128)(2,1)S(1)}, bf16[4,5,32,1024]{3,2,1,0:T(8,128)(2,1)}, u32[]{:S(2)}) copy-start(bf16[4,5,32,1024]{3,2,1,0:T(8,128)(2,1)} %param.9) | copy-start | bytes 3932164
  0.7 14.6 %copy-start = (bf16[5,16,16,128]{3,2,1,0:T(8,128)(2,1)S(1)}, bf16[5,16,16,128]{3,2,1,0:T(8,128)(2,1)}, u32[]{:S(2)}) copy-start(bf16[5,16,16,128]{3,2,1,0:T(8,128)(2,1)} %param.8) | copy-start | bytes 983044
  4.6 16.2 %collective-permute-start = (bf16[576,128]{1,0:T(8,128)(2,1)}, bf16[576,128]{1,0:T(8,128)(2,1)S(1)}, u32[]{:S(2)}, u32[]{:S(2)}) collective-permute-start(bf16[576,128]{1,0:T(8,128)(2,1)} %get-tuple-element.30), channel_id=1, source_target_pairs={{0,1},{1,0},{2,3},{3,2},{4,5},{5,4},{6,7},{7,6},{8,9},{9,8},{10,11... | collective-permute-start | bytes 442376 | tf_op jit(solution)/shard_map/ppermute | solution.py:867
  13.3 9.9 %collective-permute-start.1 = (bf16[576,128]{1,0:T(8,128)(2,1)}, bf16[576,128]{1,0:T(8,128)(2,1)S(1)}, u32[]{:S(2)}, u32[]{:S(2)}) collective-permute-start(bf16[576,128]{1,0:T(8,128)(2,1)} %get-tuple-element.31), channel_id=1, source_target_pairs={{0,31},{1,2},{2,1},{3,4},{4,3},{5,6},{6,5},{7,8},{8,7},{9,10},{10,... | collective-permute-start | bytes 442376 | tf_op jit(solution)/shard_map/ppermute | solution.py:867
  15.3 1.1 %copy-start.2 = (bf16[1280,256]{1,0:T(8,128)(2,1)S(1)}, bf16[1280,256]{1,0:T(8,128)(2,1)}, u32[]{:S(2)}) copy-start(bf16[1280,256]{1,0:T(8,128)(2,1)} %constant.4.clone.weights.refs_11_) | copy-start | bytes 1966084
  16.4 1.0 %copy-start.7 = (bf16[160,1280]{1,0:T(8,128)(2,1)S(1)}, bf16[160,1280]{1,0:T(8,128)(2,1)}, u32[]{:S(2)}) copy-start(bf16[160,1280]{1,0:T(8,128)(2,1)} %constant.5.clone.side_sum.refs_12_) | copy-start | bytes 1228804
  17.4 8.9 %copy-start.3 = (bf16[1280,256]{1,0:T(8,128)(2,1)S(1)}, bf16[1280,256]{1,0:T(8,128)(2,1)}, u32[]{:S(2)}) copy-start(bf16[1280,256]{1,0:T(8,128)(2,1)} %constant.4.clone.weights.refs_11_) | copy-start | bytes 1966084
  24.4 12.0 %collective-permute-start.2 = (bf16[288,128]{1,0:T(8,128)(2,1)S(1)}, bf16[288,128]{1,0:T(8,128)(2,1)S(1)}, u32[]{:S(2)}, u32[]{:S(2)}) collective-permute-start(bf16[288,128]{1,0:T(8,128)(2,1)S(1)} %get-tuple-element.33), channel_id=1, source_target_pairs={{0,32},{32,0},{64,96},{96,64},{128,160},{160,128},{192,224},{224,1... | collective-permute-start | bytes 221192 | tf_op jit(solution)/shard_map/ppermute | solution.py:867
  26.3 7.3 %copy-start.8 = (bf16[160,1280]{1,0:T(8,128)(2,1)S(1)}, bf16[160,1280]{1,0:T(8,128)(2,1)}, u32[]{:S(2)}) copy-start(bf16[160,1280]{1,0:T(8,128)(2,1)} %constant.5.clone.side_sum.refs_12_) | copy-start | bytes 1228804
  31.5 7.2 %collective-permute-start.3 = (bf16[288,128]{1,0:T(8,128)(2,1)S(1)}, bf16[288,128]{1,0:T(8,128)(2,1)S(1)}, u32[]{:S(2)}, u32[]{:S(2)}) collective-permute-start(bf16[288,128]{1,0:T(8,128)(2,1)S(1)} %get-tuple-element.44), channel_id=1, source_target_pairs={{0,480},{32,64},{64,32},{96,128},{128,96},{160,192},{192,160},{224... | collective-permute-start | bytes 221192 | tf_op jit(solution)/shard_map/ppermute | solution.py:867

commit v4 on v3

--- a/solution.py
+++ b/solution.py
@@ -284,6 +284,7 @@
         arrived[1] = far_ref[...]
 
 
+TALL = 8 * EDGE
 PLANES = 16
 
 
@@ -355,8 +356,8 @@
             for h in range(2):
                 part = slice(LANES * h, LANES * (h + 1))
                 at = slice(QUAD * q + LANES * h, QUAD * q + LANES * (h + 1))
-                split[2 * h] = value[:, part]
-                split[2 * h + 1] = both[:, part]
+                split[2 * h, :ROWS, :] = value[:, part]
+                split[2 * h + 1, :ROWS, :] = both[:, part]
                 for p in range(2):
                     first = (EDGE - 1) * p
                     planes_ref[s, 8 * p : 8 * p + COMPS, at] = split[2 * h, pl.ds(first, COMPS, stride=EDGE), :]
@@ -380,7 +381,7 @@
 def z_message_kernel(col, cnt, nbr, rate, coarse_ref, flux_in, y_near, y_far, near_ref, far_ref, arrived, flux):
     tables = Tables(col, cnt, nbr, rate)
     sort_arrivals("fine", y_near, y_far, arrived)
-    flux[...] = flux_in[...]
+    flux[: 2 * CROWS, :] = flux_in[...]
     fine_pick, coarse_pick = plane_rows(EDGE, False), plane_rows(HALF, False)
     place = tables.to_coarse(None)
     rates = chain(iota((PLANES, LANES), 0) % 8, tables.rate + [jnp.zeros((), F32)] * 3)
@@ -575,7 +576,7 @@
             add = edge_lanes(plane_ghost, s, bool(k))[:, part]
             planes_ref[s, :, tile] = planes_ref[s, :, tile] + 2.0 * plane_rates * add
         theirs = mm(y_arr[k, Y_HALF : Y_HALF + ROWS, :], linked) + 2.0 * rates * neighbour_rows(fine_ref, k)
-        theirs_ref[k] = theirs
+        theirs_ref[k, :ROWS, :] = theirs
         theirs = theirs.astype(BF16).astype(F32)
         is_linked = chain(iota((ROWS, LANES), 1) // EDGE, tables.near[2 + k]) >= 0
         second.append(jnp.where(is_linked, theirs, mm(level_row(mean, y), opened)))
@@ -665,7 +666,7 @@
     sort_arrivals("own", z_near, z_far, z_arr)
     fill_old(old, coarse_ref, y_arr, (0, 1, HALF - 2, HALF - 1))
     for k in (0, 1):
-        following[k] = y_arr[k, Y_NEXT : Y_NEXT + CROWS, :].astype(F32)
+        following[k, :CROWS, :] = y_arr[k, Y_NEXT : Y_NEXT + CROWS, :].astype(F32)
     for c in range(COMPS):
         for k, z in ((0, -1), (1, HALF)):
             at = Z_NEAR + c * HALF
@@ -717,7 +718,7 @@
         for s in range(SLOTS):
             part = jnp.where(n // EDGE == s, planes, 0.0)
             part = part + pltpu.roll(part, EDGE, 1)
-            spread[s] = part + pltpu.roll(part, 2 * EDGE, 1)
+            spread[s, : 2 * CROWS, :] = part + pltpu.roll(part, 2 * EDGE, 1)
             for k in range(8):
                 for p in range(2):
                     even = spread[s, pl.ds(CROWS * p + 2 * k, COMPS, stride=HALF), :]
@@ -795,7 +796,7 @@
     for s in range(SLOTS):
         for k in range(8):
             lanes = slice(LANES * k, LANES * (k + 1))
-            fine_out[s, :, lanes] = jnp.where(replaced, put[s, k], fine_in[s, :, lanes].astype(F32)).astype(BF16)
+            fine_out[s, :, lanes] = jnp.where(replaced, put[s, k, :ROWS, :], fine_in[s, :, lanes].astype(F32)).astype(BF16)
         sends.append(pltpu.make_async_copy(fine_out.at[s], fine_hbm.at[s], sems.at[s]))
         sends[s].start()
 
@@ -909,7 +910,7 @@
         scratch_shapes=[
             pltpu.VMEM((PLANES * HALF, LANES), F32),
             pltpu.VMEM((8 * PLANES, SLOTS * LANES), F32),
-            pltpu.VMEM((4, ROWS, LANES), F32),
+            pltpu.VMEM((4, TALL, LANES), F32),
         ],
         compiler_params=PARAMS,
         cost_estimate=pl.CostEstimate(flops=2_000_000_000, bytes_accessed=5_000_000, transcendentals=0),
@@ -922,7 +923,7 @@
         in_specs=SCALARS + [whole()] * 4,
         out_specs=[whole()] * 2,
         out_shape=[z_shape] * 2,
-        scratch_shapes=[pltpu.VMEM((2, Y_ROWS, LANES), BF16), pltpu.VMEM((2 * CROWS, LANES), F32)],
+        scratch_shapes=[pltpu.VMEM((2, Y_ROWS, LANES), BF16), pltpu.VMEM((TALL, LANES), F32)],
         compiler_params=PARAMS,
         name="z_messages",
     )(*tables, coarse, flux, y_near, y_far)
@@ -930,7 +931,7 @@
         field_shape,
         jax.ShapeDtypeStruct((SLOTS, 32, PLANE), F32),
         planes_shape,
-        jax.ShapeDtypeStruct((2, ROWS, LANES), F32),
+        jax.ShapeDtypeStruct((2, TALL, LANES), F32),
     ]
     pairs_shape = (2, 8, CROWS, SLOTS * LANES)
     middle_args = (*tables, fine, coarse, y_near, y_far, half, edges, planes, weights, side_sum, place)
@@ -979,15 +980,15 @@
         scratch_shapes=[
             pltpu.VMEM((2, Y_ROWS, LANES), BF16),
             pltpu.VMEM((2, Z_ROWS, LANES), BF16),
-            level,
+            pltpu.VMEM((8 * DEEP * SPAN, LANES), F32),
             level,
             pltpu.VMEM((SLOTS, 32, PLANE), BF16),
             pltpu.VMEM((PLANES * HALF, LANES), F32),
-            pltpu.VMEM((2, CROWS, LANES), F32),
-            pltpu.VMEM((SLOTS, 2 * CROWS, LANES), F32),
+            pltpu.VMEM((2, 8 * HALF, LANES), F32),
+            pltpu.VMEM((SLOTS, TALL, LANES), F32),
             pltpu.VMEM((2, SLOTS, PLANES, PLANE), F32),
             pltpu.VMEM((3, 32, LANES), F32),
-            pltpu.VMEM((SLOTS, 8, ROWS, LANES), F32),
+            pltpu.VMEM((SLOTS, 8, TALL, LANES), F32),
             pltpu.VMEM((SLOTS, ROWS, PLANE), BF16),
             pltpu.SemaphoreType.DMA((SLOTS,)),
         ],

time: 43.1 us -> 43.1 us (level)
  no operation moved by 1% of the time
where the time goes in v4:
time: 43.1 us; the launch traced here: 42.7 us
  Pallas kernels  19.4 us (45%)
  starting transfers between devices  14.8 us (34%)
  waiting for transfers between devices  4.71 us (11%)
  local copies, waits for them, and re-layouts  2.12 us (5%)
  between operations  1.76 us (4%)
    ppermute x4, starting transfers between devices, swap(): return lax.ppermute(value, axis, pairs)  14.8 us
    pallas_call x1, Pallas kernels, local(): pl.pallas_call(early_kernel, in_specs=SCALARS + [whole()] * 10, out_specs...  5.11 us
    ppermute x4, waiting for transfers between devices, swap(): return lax.ppermute(value, axis, pairs)  4.71 us
    pallas_call x1, Pallas kernels, local(): pl.pallas_call(last_kernel, in_specs=SCALARS + [whole()] * 13, out_specs=...  3.91 us
    pallas_call x1, Pallas kernels, local(): pl.pallas_call(interior_kernel, in_specs=SCALARS + [whole()] * 4, out_spe...  3.37 us
    pallas_call x1, Pallas kernels, local(): pl.pallas_call(y_message_kernel, in_specs=[pl.BlockSpec(memory_space=pl.A...  3.1 us
    pallas_call x1, Pallas kernels, local(): pl.pallas_call(late_kernel, in_specs=SCALARS + [whole()] * 15, out_specs=...  2.74 us
    unnamed x18, local copies, waits for them, and re-layouts  2.12 us
  transfers between devices with their start and end apart: 4, of which 2 were waited for; matrix products, arithmetic and copies ran while one was open for 0% of the time, Pallas kernels for 26%

profile of v4, /device:TPU:1, one launch (start us, length us, event | category | flops | bytes accessed | tf_op | source)
XLA Modules:
  0.0 42.7 jit_solution(9374686939559720749)
XLA Ops:
  0.6 0.0 copy-start.4
  0.6 0.0 copy-start.5
  0.7 0.0 copy-start.6
  0.7 0.0 copy-start.1
  0.7 0.0 copy-start
  1.4 3.1 %y_messages.1 = (bf16[576,128]{1,0:T(8,128)(2,1)}, bf16[576,128]{1,0:T(8,128)(2,1)}) custom-call(s32[4]{0:T(128)} %col.5, s32[1]{0:T(128)S(6)} %copy.10.cnt_hbm.cnt.refs_1_, s32[4,4]{1,0:T(4,128)} %nbr.5, f32[5]{0:T(128)} %rate.5, bf16[4,160,1024]{2,1,0:T(8,128)(2,1)} %bitcast.10, bf16[1280,128]{1,0:T(8,128)(2,1)} %bitcast.4), custom_call_target="tpu_custom_call" | custom-call | tf_op jit(solution)/shard_map/y_messages/pallas_call | solution.py:873
  4.6 8.8 %collective-permute-start = (bf16[576,128]{1,0:T(8,128)(2,1)}, bf16[576,128]{1,0:T(8,128)(2,1)S(1)}, u32[]{:S(2)}, u32[]{:S(2)}) collective-permute-start(bf16[576,128]{1,0:T(8,128)(2,1)} %get-tuple-element.30), channel_id=1, source_target_pairs={{0,1},{1,0},{2,3},{3,2},{4,5},{5,4},{6,7},{7,6},{8,9},{9,8},{10,11... | collective-permute-start | bytes 442376 | tf_op jit(solution)/shard_map/ppermute | solution.py:868
  13.3 1.9 %collective-permute-start.1 = (bf16[576,128]{1,0:T(8,128)(2,1)}, bf16[576,128]{1,0:T(8,128)(2,1)S(1)}, u32[]{:S(2)}, u32[]{:S(2)}) collective-permute-start(bf16[576,128]{1,0:T(8,128)(2,1)} %get-tuple-element.31), channel_id=1, source_target_pairs={{0,31},{1,2},{2,1},{3,4},{4,3},{5,6},{6,5},{7,8},{8,7},{9,10},{10,... | collective-permute-start | bytes 442376 | tf_op jit(solution)/shard_map/ppermute | solution.py:868
  15.3 0.0 copy-done.4
  15.3 0.0 copy-start.2
  15.3 1.1 %copy-done.2 = bf16[1280,256]{1,0:T(8,128)(2,1)S(1)} copy-done((bf16[1280,256]{1,0:T(8,128)(2,1)S(1)}, bf16[1280,256]{1,0:T(8,128)(2,1)}, u32[]{:S(2)}) %copy-start.2) | copy-done | bytes 655384
  16.4 1.0 %copy-done.7 = bf16[160,1280]{1,0:T(8,128)(2,1)S(1)} copy-done((bf16[160,1280]{1,0:T(8,128)(2,1)S(1)}, bf16[160,1280]{1,0:T(8,128)(2,1)}, u32[]{:S(2)}) %copy-start.7) | copy-done | bytes 409624
  17.4 3.4 %interior.1 = (bf16[4,160,1024]{2,1,0:T(8,128)(2,1)S(1)}, f32[4,160,256]{2,1,0:T(8,128)S(1)}, f32[4,16,1024]{2,1,0:T(8,128)S(1)}, f32[160,128]{1,0:T(8,128)S(1)}, bf16[512,256]{1,0:T(8,128)(2,1)S(1)}) custom-call(s32[4]{0:T(128)S(1)} %copy-done.5, s32[1]{0:T(128)S(6)} %copy.10.cnt_hbm.cnt.refs_1_, s32[4,4]{1,0:T(4,128)S(1)} %copy-done.4, f32[5]{0:T(128)S(1)} %copy-done.6, ...), custom_call_target="tpu_custom_call" | custom-call | flops 2000000000 | bytes 5000000 | tf_op jit(solution)/shard_map/interior/pallas_call | solution.py:899
  20.8 0.0 collective-permute-done.y_near.refs_6_
  20.8 2.4 %collective-permute-done.1.y_far.refs_7_ = bf16[576,128]{1,0:T(8,128)(2,1)S(1)} collective-permute-done((bf16[576,128]{1,0:T(8,128)(2,1)}, bf16[576,128]{1,0:T(8,128)(2,1)S(1)}, u32[]{:S(2)}, u32[]{:S(2)}) %collective-permute-start.1) | collective-permute-done | bytes 147488 | tf_op jit(solution)/shard_map/ppermute | solution.py:868
  23.2 1.1 %z_messages.1 = (bf16[288,128]{1,0:T(8,128)(2,1)S(1)}, bf16[288,128]{1,0:T(8,128)(2,1)S(1)}) custom-call(s32[4]{0:T(128)S(1)} %copy-done.5, s32[1]{0:T(128)S(6)} %copy.10.cnt_hbm.cnt.refs_1_, s32[4,4]{1,0:T(4,128)S(1)} %copy-done.4, f32[5]{0:T(128)S(1)} %copy-done.6, bf16[1280,128]{1,0:T(8,128)(2,1)S(1)} %bitcast.6, ...), custom_call_target="tpu_custom_call" | custom-call | tf_op jit(solution)/shard_map/z_messages/pallas_call | solution.py:921
  24.4 1.9 %collective-permute-start.2 = (bf16[288,128]{1,0:T(8,128)(2,1)S(1)}, bf16[288,128]{1,0:T(8,128)(2,1)S(1)}, u32[]{:S(2)}, u32[]{:S(2)}) collective-permute-start(bf16[288,128]{1,0:T(8,128)(2,1)S(1)} %get-tuple-element.33), channel_id=1, source_target_pairs={{0,32},{32,0},{64,96},{96,64},{128,160},{160,128},{192,224},{224,1... | collective-permute-start | bytes 221192 | tf_op jit(solution)/shard_map/ppermute | solution.py:868
  26.3 0.0 copy-start.8
  26.3 5.1 %early.1 = (bf16[4,160,1024]{2,1,0:T(8,128)(2,1)S(1)}, f32[4,32,1024]{2,1,0:T(8,128)S(1)}, f32[4,16,1024]{2,1,0:T(8,128)S(1)}, f32[2,256,128]{2,1,0:T(8,128)S(1)}, bf16[2,8,80,512]{3,2,1,0:T(8,128)(2,1)S(1)}) custom-call(s32[4]{0:T(128)S(1)} %copy-done.5, s32[1]{0:T(128)S(6)} %copy.10.cnt_hbm.cnt.refs_1_, s32[4,4]{1,0:T(4,128)S(1)} %copy-done.4, ...), custom_call_target="tpu_custom_call" | custom-call | flops 3000000000 | bytes 8000000 | tf_op jit(solution)/shard_map/early/pallas_call | solution.py:946
  31.5 2.2 %collective-permute-start.3 = (bf16[288,128]{1,0:T(8,128)(2,1)S(1)}, bf16[288,128]{1,0:T(8,128)(2,1)S(1)}, u32[]{:S(2)}, u32[]{:S(2)}) collective-permute-start(bf16[288,128]{1,0:T(8,128)(2,1)S(1)} %get-tuple-element.44), channel_id=1, source_target_pairs={{0,480},{32,64},{64,32},{96,128},{128,96},{160,192},{192,160},{224... | collective-permute-start | bytes 221192 | tf_op jit(solution)/shard_map/ppermute | solution.py:868
  33.6 2.7 %late.1 = (bf16[1280,128]{1,0:T(8,128)(2,1)S(1)}, f32[160,128]{1,0:T(8,128)S(1)}, bf16[4,160,1024]{2,1,0:T(8,128)(2,1)S(1)}, f32[4,32,1024]{2,1,0:T(8,128)S(1)},...) custom-call(s32[4]{0:T(128)S(1)} %copy-done.5, s32[1]{0:T(128)S(6)} %copy.10.cnt_hbm.cnt.refs_1_, ...), custom_call_target="tpu_custom_call" | custom-call | flops 3000000000 | bytes 8000000 | tf_op jit(solution)/shard_map/late/pallas_call | solution.py:958
  36.4 0.0 collective-permute-done.2.z_near
  36.4 2.3 %collective-permute-done.3.z_far = bf16[288,128]{1,0:T(8,128)(2,1)S(1)} collective-permute-done((bf16[288,128]{1,0:T(8,128)(2,1)S(1)}, bf16[288,128]{1,0:T(8,128)(2,1)S(1)}, u32[]{:S(2)}, u32[]{:S(2)}) %collective-permute-start.3) | collective-permute-done | bytes 73760 | tf_op jit(solution)/shard_map/ppermute | solution.py:868
  38.7 3.9 %last.1 = (bf16[1280,128]{1,0:T(8,128)(2,1)}, bf16[4,160,1024]{2,1,0:T(8,128)(2,1)}) custom-call(s32[4]{0:T(128)S(1)} %copy-done.5, s32[1]{0:T(128)S(6)} %copy.10.cnt_hbm.cnt.refs_1_, s32[4,4]{1,0:T(4,128)S(1)} %copy-done.4, f32[5]{0:T(128)S(1)} %copy-done.6, bf16[1280,128]{1,0:T(8,128)(2,1)S(1)} %bitcast.9, ...), custom_call_target="tpu_custom_call" | custom-call | tf_op jit(solution)/shard_map/last/pallas_call | solution.py:975
  (8 shorter events, 0.0 us)
Async XLA Ops:
  0.6 14.6 %copy-start.4 = (s32[4,4]{1,0:T(4,128)S(1)}, s32[4,4]{1,0:T(4,128)}, u32[]{:S(2)}) copy-start(s32[4,4]{1,0:T(4,128)} %nbr.5) | copy-start | bytes 196
  0.6 14.6 %copy-start.5 = (s32[4]{0:T(128)S(1)}, s32[4]{0:T(128)}, u32[]{:S(2)}) copy-start(s32[4]{0:T(128)} %col.5) | copy-start | bytes 52
  0.7 14.6 %copy-start.6 = (f32[5]{0:T(128)S(1)}, f32[5]{0:T(128)}, u32[]{:S(2)}) copy-start(f32[5]{0:T(128)} %rate.5) | copy-start | bytes 64
  0.7 14.6 %copy-start.1 = (bf16[4,5,32,1024]{3,2,1,0:T(8,128)(2,1)S(1)}, bf16[4,5,32,1024]{3,2,1,0:T(8,128)(2,1)}, u32[]{:S(2)}) copy-start(bf16[4,5,32,1024]{3,2,1,0:T(8,128)(2,1)} %param.9) | copy-start | bytes 3932164
  0.7 14.6 %copy-start = (bf16[5,16,16,128]{3,2,1,0:T(8,128)(2,1)S(1)}, bf16[5,16,16,128]{3,2,1,0:T(8,128)(2,1)}, u32[]{:S(2)}) copy-start(bf16[5,16,16,128]{3,2,1,0:T(8,128)(2,1)} %param.8) | copy-start | bytes 983044
  4.6 16.2 %collective-permute-start = (bf16[576,128]{1,0:T(8,128)(2,1)}, bf16[576,128]{1,0:T(8,128)(2,1)S(1)}, u32[]{:S(2)}, u32[]{:S(2)}) collective-permute-start(bf16[576,128]{1,0:T(8,128)(2,1)} %get-tuple-element.30), channel_id=1, source_target_pairs={{0,1},{1,0},{2,3},{3,2},{4,5},{5,4},{6,7},{7,6},{8,9},{9,8},{10,11... | collective-permute-start | bytes 442376 | tf_op jit(solution)/shard_map/ppermute | solution.py:868
  13.3 9.9 %collective-permute-start.1 = (bf16[576,128]{1,0:T(8,128)(2,1)}, bf16[576,128]{1,0:T(8,128)(2,1)S(1)}, u32[]{:S(2)}, u32[]{:S(2)}) collective-permute-start(bf16[576,128]{1,0:T(8,128)(2,1)} %get-tuple-element.31), channel_id=1, source_target_pairs={{0,31},{1,2},{2,1},{3,4},{4,3},{5,6},{6,5},{7,8},{8,7},{9,10},{10,... | collective-permute-start | bytes 442376 | tf_op jit(solution)/shard_map/ppermute | solution.py:868
  15.3 1.1 %copy-start.2 = (bf16[1280,256]{1,0:T(8,128)(2,1)S(1)}, bf16[1280,256]{1,0:T(8,128)(2,1)}, u32[]{:S(2)}) copy-start(bf16[1280,256]{1,0:T(8,128)(2,1)} %constant.4.clone.weights.refs_11_) | copy-start | bytes 1966084
  16.4 1.0 %copy-start.7 = (bf16[160,1280]{1,0:T(8,128)(2,1)S(1)}, bf16[160,1280]{1,0:T(8,128)(2,1)}, u32[]{:S(2)}) copy-start(bf16[160,1280]{1,0:T(8,128)(2,1)} %constant.5.clone.side_sum.refs_12_) | copy-start | bytes 1228804
  17.4 8.9 %copy-start.3 = (bf16[1280,256]{1,0:T(8,128)(2,1)S(1)}, bf16[1280,256]{1,0:T(8,128)(2,1)}, u32[]{:S(2)}) copy-start(bf16[1280,256]{1,0:T(8,128)(2,1)} %constant.4.clone.weights.refs_11_) | copy-start | bytes 1966084
  24.4 12.0 %collective-permute-start.2 = (bf16[288,128]{1,0:T(8,128)(2,1)S(1)}, bf16[288,128]{1,0:T(8,128)(2,1)S(1)}, u32[]{:S(2)}, u32[]{:S(2)}) collective-permute-start(bf16[288,128]{1,0:T(8,128)(2,1)S(1)} %get-tuple-element.33), channel_id=1, source_target_pairs={{0,32},{32,0},{64,96},{96,64},{128,160},{160,128},{192,224},{224,1... | collective-permute-start | bytes 221192 | tf_op jit(solution)/shard_map/ppermute | solution.py:868
  26.3 7.3 %copy-start.8 = (bf16[160,1280]{1,0:T(8,128)(2,1)S(1)}, bf16[160,1280]{1,0:T(8,128)(2,1)}, u32[]{:S(2)}) copy-start(bf16[160,1280]{1,0:T(8,128)(2,1)} %constant.5.clone.side_sum.refs_12_) | copy-start | bytes 1228804
  31.5 7.2 %collective-permute-start.3 = (bf16[288,128]{1,0:T(8,128)(2,1)S(1)}, bf16[288,128]{1,0:T(8,128)(2,1)S(1)}, u32[]{:S(2)}, u32[]{:S(2)}) collective-permute-start(bf16[288,128]{1,0:T(8,128)(2,1)S(1)} %get-tuple-element.44), channel_id=1, source_target_pairs={{0,480},{32,64},{64,32},{96,128},{128,96},{160,192},{192,160},{224... | collective-permute-start | bytes 221192 | tf_op jit(solution)/shard_map/ppermute | solution.py:868
